TPU v7x, 256 devices: a whole 4x4x8 slice. The times are simulated.
256 devices in a mesh: dp: 32 (over z, x_lo, core), expert: 8 (over x_hi, y).
Axes of the slice: x: 4 (x_hi: 2, x_lo: 2; x = x_hi * 2 + x_lo), y: 4, z: 8, core: 2. Of those that a mesh axis runs over, the one named last changes fastest.
Arguments:
- tokens: bfloat16 [4096, 2048], P('dp'), may hold values from -6 to 6
- expert_ids: int32 [4096, 8], P('dp'), may hold values from 0 to 127, all different within a row; in each aligned block of 128 rows (0 to 127, 128 to 255, ...) at most 16 rows name the same one
- route_weight: float32 [4096, 8], P('dp'), may hold values from 0.05 to 0.6
- expert_slot: int32 [128], replicated, may hold values from 0 to 127, each once
- gate_weight: bfloat16 [256, 2048, 384], P(('dp', 'expert')), may hold values from -0.125 to 0.125
- up_weight: bfloat16 [256, 2048, 384], P(('dp', 'expert')), may hold values from -0.125 to 0.125
- down_weight: bfloat16 [256, 384, 2048], P(('dp', 'expert')), may hold values from -0.21875 to 0.21875
- cotangent: bfloat16 [4096, 2048], P('dp'), may hold values from -6 to 6
Outputs:
- layer_out: bfloat16 [4096, 2048], P(('dp', 'expert'))
- input_grad: bfloat16 [4096, 2048], P(('dp', 'expert'))
- gate_grad: bfloat16 [256, 2048, 384], P(('dp', 'expert'))
- up_grad: bfloat16 [256, 2048, 384], P(('dp', 'expert'))
- down_grad: bfloat16 [256, 384, 2048], P(('dp', 'expert'))
Inputs may be any that keep to these rules, and one draw needn't show every extreme that they name: `expert_ids`: each token names 8 different experts; among the 128 tokens of one dp index (aligned blocks of rows) no expert is named more than 16 times, and in some or all blocks one expert is named exactly 16 times. A permutation: the expert e sits in slot expert_slot[e].
All inputs are finite; a program needn't handle non-finite values.
Results may differ from a plain program's by a relative error of at most 0.0058.
Values may be sent and summed in bfloat16 or wider, within the bound.
No kernel may reach another device: no remote copies, remote signals or barrier semaphores. Data moves between devices by JAX's collectives and lax.ppermute only.
A program may use at most 128 MiB of HBM per device.

v0:
```python
import jax
import jax.numpy as jnp
from jax import lax
from jax.sharding import PartitionSpec as P


def half_expert(x_rows, scaled_rows, w_gate, w_up, w_down):
    gate_val = jnp.dot(x_rows, w_gate, preferred_element_type=jnp.float32)
    up_val = jnp.dot(x_rows, w_up, preferred_element_type=jnp.float32)
    sigma_val = jax.nn.sigmoid(gate_val)
    act_val = gate_val * sigma_val
    hidden = (act_val * up_val).astype(jnp.bfloat16)
    out_part = jnp.dot(hidden, w_down, preferred_element_type=jnp.float32)
    returned = lax.dot_general(
        scaled_rows, w_down, (((1,), (1,)), ((), ())), preferred_element_type=jnp.float32
    )
    d_gate = (returned * up_val * sigma_val * (1.0 + gate_val * (1.0 - sigma_val))).astype(
        jnp.bfloat16
    )
    d_up = (returned * act_val).astype(jnp.bfloat16)
    grad_down = lax.dot_general(
        hidden, scaled_rows, (((0,), (0,)), ((), ())), preferred_element_type=jnp.float32
    ).astype(jnp.bfloat16)
    grad_gate = lax.dot_general(
        x_rows, d_gate, (((0,), (0,)), ((), ())), preferred_element_type=jnp.float32
    ).astype(jnp.bfloat16)
    grad_up = lax.dot_general(
        x_rows, d_up, (((0,), (0,)), ((), ())), preferred_element_type=jnp.float32
    ).astype(jnp.bfloat16)
    first_term = lax.dot_general(
        d_gate, w_gate, (((1,), (1,)), ((), ())), preferred_element_type=jnp.float32
    )
    second_term = lax.dot_general(
        d_up, w_up, (((1,), (1,)), ((), ())), preferred_element_type=jnp.float32
    )
    in_piece = first_term + second_term
    return (out_part, in_piece, grad_gate, grad_up, grad_down)


def deliver(buffer):
    joined = lax.all_to_all(buffer, "dp", split_axis=0, concat_axis=0, tiled=True)
    return joined.reshape(-1, joined.shape[2])


def on_device(
    tokens, expert_ids, route_weight, expert_slot, gate_weight, up_weight, down_weight, cotangent
):
    tok_count, width = tokens.shape
    top_count = expert_ids.shape[1]
    experts = expert_slot.shape[0]
    dp_count = lax.axis_size("dp")
    ex_count = lax.axis_size("expert")
    pair_count = ex_count // 2
    capacity = 2 * tok_count * top_count // experts
    owner_rows = dp_count * capacity
    column = lax.axis_index("expert")
    pair_col = column // 2
    expert_table = jnp.arange(experts, dtype=jnp.int32)
    ids_hot = expert_ids[:, :, None] == expert_table[None, None, :]
    slot_of = jnp.sum(jnp.where(ids_hot, expert_slot[None, None, :], 0), axis=2).reshape(-1)
    slot_hot = (slot_of[:, None] == expert_table[None, :]).astype(jnp.int32)
    before = jnp.cumsum(slot_hot, axis=0) - slot_hot
    slot_place = jnp.sum(before * slot_hot, axis=1)
    is_mine = slot_of % pair_count == pair_col
    target = jnp.where(is_mine, slot_of // pair_count * capacity + slot_place, owner_rows)
    assign_tok = jnp.arange(tok_count * top_count, dtype=jnp.int32) // top_count
    source_tok = jnp.zeros((owner_rows,), jnp.int32).at[target].set(assign_tok, mode="drop")
    is_live = jnp.zeros((owner_rows,), jnp.int32).at[target].set(1, mode="drop") > 0
    row_weight = (
        jnp.zeros((owner_rows,), jnp.float32).at[target].set(route_weight.reshape(-1), mode="drop")
    )
    send_x = jnp.where(is_live[:, None], tokens[source_tok], jnp.zeros((), jnp.bfloat16))
    send_g = jnp.where(
        is_live[:, None], row_weight[:, None] * cotangent[source_tok].astype(jnp.float32), 0.0
    ).astype(jnp.bfloat16)
    x_rows = deliver(send_x.reshape(dp_count, capacity, width))
    g_rows = deliver(send_g.reshape(dp_count, capacity, width))
    out_part, in_piece, grad_gate, grad_up, grad_down = half_expert(
        x_rows, g_rows, gate_weight[0], up_weight[0], down_weight[0]
    )
    out_blocks = out_part.reshape(dp_count, capacity, width)
    in_blocks = in_piece.reshape(dp_count, capacity, width)
    back_out, back_in = (
        lax.all_to_all(out_blocks, "dp", split_axis=0, concat_axis=0, tiled=True),
        lax.all_to_all(in_blocks, "dp", split_axis=0, concat_axis=0, tiled=True),
    )
    back_out = back_out.reshape(-1, width)
    back_in = back_in.reshape(-1, width)
    y_part = jax.ops.segment_sum(row_weight[:, None] * back_out, source_tok, num_segments=tok_count)
    dx_part = jax.ops.segment_sum(
        jnp.where(is_live[:, None], back_in, 0.0), source_tok, num_segments=tok_count
    )
    out_sum, grad_sum = (
        lax.psum_scatter(y_part, "expert", scatter_dimension=0, tiled=True),
        lax.psum_scatter(dx_part, "expert", scatter_dimension=0, tiled=True),
    )
    return (
        out_sum.astype(jnp.bfloat16),
        grad_sum.astype(jnp.bfloat16),
        grad_gate[None],
        grad_up[None],
        grad_down[None],
    )


def solution(mesh):
    in_specs = (
        P("dp", None),
        P("dp", None),
        P("dp", None),
        P(),
        P(("dp", "expert"), None, None),
        P(("dp", "expert"), None, None),
        P(("dp", "expert"), None, None),
        P("dp", None),
    )
    out_specs = (
        P(("dp", "expert"), None),
        P(("dp", "expert"), None),
        P(("dp", "expert"), None, None),
        P(("dp", "expert"), None, None),
        P(("dp", "expert"), None, None),
    )
    return jax.shard_map(
        on_device, mesh=mesh, in_specs=in_specs, out_specs=out_specs, check_vma=False
    )
```

profile of v0, /device:TPU:28, one launch (start us, length us, event | category | flops | bytes accessed | tf_op | source)
XLA Modules:
  0.0 446.7 jit_solution(10531161640842518673)
XLA Ops:
  8.1 3.0 select_reduce_fusion
  12.4 4.3 scatter_custom_fusion
  16.7 4.3 scatter_custom_fusion.2
  21.2 3.3 gather_fusion
  24.5 3.2 broadcast_select_fusion
  27.6 9.7 %all-to-all-start = ((bf16[32,16,2048]{2,1,0:T(8,128)(2,1)}), bf16[32,16,2048]{2,1,0:T(8,128)(2,1)}, u32[]{:S(2)}, u32[]{:S(2)}) async-start(bf16[32,16,2048]{2,1,0:T(8,128)(2,1)} %broadcast_select_fusion), calls=%async_computation | async-start | bytes 4194304 | tf_op jit(solution)/shard_map/all_to_all | solution.py:41
  37.6 4.3 scatter_custom_fusion.1
  42.0 3.3 gather_fusion.1
  45.3 3.4 fusion.1
  48.7 38.9 %all-to-all-done = bf16[32,16,2048]{2,1,0:T(8,128)(2,1)} async-done(((bf16[32,16,2048]{2,1,0:T(8,128)(2,1)}), bf16[32,16,2048]{2,1,0:T(8,128)(2,1)}, u32[]{:S(2)}, u32[]{:S(2)}) %all-to-all-start) | async-done | bytes 2097184 | tf_op jit(solution)/shard_map/all_to_all | solution.py:41
  87.7 4.9 %all-to-all-start.2 = ((bf16[32,16,2048]{2,1,0:T(8,128)(2,1)}), bf16[32,16,2048]{2,1,0:T(8,128)(2,1)}, u32[]{:S(2)}, u32[]{:S(2)}) async-start(bf16[32,16,2048]{2,1,0:T(8,128)(2,1)} %fusion.1), calls=%async_computation.3 | async-start | bytes 4194304 | tf_op jit(solution)/shard_map/all_to_all | solution.py:41
  92.6 4.3 fusion.10
  96.9 3.7 fusion.14
  100.6 42.0 %all-to-all-done.2 = bf16[32,16,2048]{2,1,0:T(8,128)(2,1)} async-done(((bf16[32,16,2048]{2,1,0:T(8,128)(2,1)}), bf16[32,16,2048]{2,1,0:T(8,128)(2,1)}, u32[]{:S(2)}, u32[]{:S(2)}) %all-to-all-start.2) | async-done | bytes 2097184 | tf_op jit(solution)/shard_map/all_to_all | solution.py:41
  142.6 3.5 multiply_convert_fusion
  146.1 1.3 fusion.12
  147.8 3.2 convolution_add_fusion
  151.0 4.9 %all-to-all-start.3 = ((f32[32,16,2048]{2,1,0:T(8,128)}), f32[32,16,2048]{2,1,0:T(8,128)}, u32[]{:S(2)}, u32[]{:S(2)}) async-start(f32[32,16,2048]{2,1,0:T(8,128)} %bitcast.62), calls=%async_computation.4 | async-start | bytes 8388608 | tf_op jit(solution)/shard_map/all_to_all | solution.py:85
  155.9 3.2 fusion.5
  159.1 93.4 %all-to-all-done.3 = f32[32,16,2048]{2,1,0:T(8,128)} async-done(((f32[32,16,2048]{2,1,0:T(8,128)}), f32[32,16,2048]{2,1,0:T(8,128)}, u32[]{:S(2)}, u32[]{:S(2)}) %all-to-all-start.3) | async-done | bytes 4194336 | tf_op jit(solution)/shard_map/all_to_all | solution.py:85
  252.5 4.9 %all-to-all-start.1 = ((f32[32,16,2048]{2,1,0:T(8,128)}), f32[32,16,2048]{2,1,0:T(8,128)}, u32[]{:S(2)}, u32[]{:S(2)}) async-start(f32[32,16,2048]{2,1,0:T(8,128)} %fusion.5), calls=%async_computation.1 | async-start | bytes 8388608 | tf_op jit(solution)/shard_map/all_to_all | solution.py:84
  257.4 4.5 %bitcast_select_fusion = f32[512,2048]{1,0:T(8,128)} fusion(f32[32,16,2048]{2,1,0:T(8,128)} %all-to-all-done.3, pred[512]{0:T(512)(128)(4,1)S(1)} %broadcast_compare_fusion), kind=kLoop, calls=%fused_computation.10 | loop fusion | flops 1048576 | bytes 8389120 | tf_op jit(solution)/shard_map/jit(_where)/select_n | solution.py:91
  261.9 9.5 %scatter_custom_fusion.4 = f32[128,2048]{1,0:T(8,128)} fusion(s32[512]{0:T(512)S(1)} %scatter_custom_fusion, f32[512,2048]{1,0:T(8,128)} %bitcast_select_fusion, f32[]{:T(128)} %constant.64.clone.1), kind=kCustom, calls=%fused_computation.45 | custom fusion | flops 1048576 | bytes 1049088 | tf_op jit(solution)/shard_map/scatter-add | solution.py:90
  271.8 82.3 %all-to-all-done.1 = f32[32,16,2048]{2,1,0:T(8,128)} async-done(((f32[32,16,2048]{2,1,0:T(8,128)}), f32[32,16,2048]{2,1,0:T(8,128)}, u32[]{:S(2)}, u32[]{:S(2)}) %all-to-all-start.1) | async-done | bytes 4194336 | tf_op jit(solution)/shard_map/all_to_all | solution.py:84
  354.1 4.5 %bitcast_multiply_fusion = f32[512,2048]{1,0:T(8,128)} fusion(f32[32,16,2048]{2,1,0:T(8,128)} %all-to-all-done.1, f32[512]{0:T(512)S(1)} %scatter_custom_fusion.1), kind=kLoop, calls=%fused_computation.11 | loop fusion | flops 1048576 | bytes 8390656 | tf_op jit(solution)/shard_map/mul | solution.py:89
  358.6 9.4 %scatter_custom_fusion.3 = f32[128,2048]{1,0:T(8,128)} fusion(s32[512]{0:T(512)S(1)} %scatter_custom_fusion, f32[512,2048]{1,0:T(8,128)} %bitcast_multiply_fusion, f32[]{:T(128)} %constant.64.clone.1), kind=kCustom, calls=%fused_computation.47 | custom fusion | flops 1048576 | bytes 1049088 | tf_op jit(solution)/shard_map/scatter-add | solution.py:89
  368.0 3.8 fusion.4
  371.8 4.1 fusion.3
  375.9 4.1 fusion.2
  380.0 1.5 convert_element_type.51
  381.5 56.8 %reduce-scatter.3.cloned.1.call-done = f32[16,2048]{1,0:T(8,128)} async-done(((f32[128,2048]{1,0:T(8,128)}), f32[16,2048]{1,0:T(8,128)}) %reduce-scatter.3.cloned.1.call-update) | async-done | bytes 131088 | tf_op jit(solution)/shard_map/reduce_scatter | solution.py:94
  438.4 1.5 convert_element_type.45
  (47 shorter events, 3.2 us)
Async XLA Ops:
  7.2 135.5 %copy-start = (bf16[1,384,2048]{2,1,0:T(8,128)(2,1)S(1)}, bf16[1,384,2048]{2,1,0:T(8,128)(2,1)}, u32[]{:S(2)}) copy-start(bf16[1,384,2048]{2,1,0:T(8,128)(2,1)} %param.14) | copy-start | bytes 4718596
  7.2 14.0 %copy-start.1 = (bf16[128,2048]{1,0:T(8,128)(2,1)S(1)}, bf16[128,2048]{1,0:T(8,128)(2,1)}, u32[]{:S(2)}) copy-start(bf16[128,2048]{1,0:T(8,128)(2,1)} %param.8) | copy-start | bytes 1572868
  27.6 9.8 %copy-start.9 = (f32[128,8]{0,1:T(8,128)S(1)}, f32[128,8]{0,1:T(8,128)}, u32[]{:S(2)}) copy-start(f32[128,8]{0,1:T(8,128)} %param.10) | copy-start | bytes 12292
  27.6 14.4 %copy-start.2 = (bf16[128,2048]{1,0:T(8,128)(2,1)S(1)}, bf16[128,2048]{1,0:T(8,128)(2,1)}, u32[]{:S(2)}) copy-start(bf16[128,2048]{1,0:T(8,128)(2,1)} %param.15) | copy-start | bytes 1572868
  27.6 60.1 %all-to-all-start = ((bf16[32,16,2048]{2,1,0:T(8,128)(2,1)}), bf16[32,16,2048]{2,1,0:T(8,128)(2,1)}, u32[]{:S(2)}, u32[]{:S(2)}) async-start(bf16[32,16,2048]{2,1,0:T(8,128)(2,1)} %broadcast_select_fusion), calls=%async_computation | async-start | bytes 4194304 | tf_op jit(solution)/shard_map/all_to_all | solution.py:41
  87.7 55.0 %all-to-all-start.2 = ((bf16[32,16,2048]{2,1,0:T(8,128)(2,1)}), bf16[32,16,2048]{2,1,0:T(8,128)(2,1)}, u32[]{:S(2)}, u32[]{:S(2)}) async-start(bf16[32,16,2048]{2,1,0:T(8,128)(2,1)} %fusion.1), calls=%async_computation.3 | async-start | bytes 4194304 | tf_op jit(solution)/shard_map/all_to_all | solution.py:41
  92.6 4.3 copy-start.3
  146.1 1.3 copy-start.5
  146.1 1.3 copy-start.7
  146.1 1.7 copy-start.4
  151.0 101.5 %all-to-all-start.3 = ((f32[32,16,2048]{2,1,0:T(8,128)}), f32[32,16,2048]{2,1,0:T(8,128)}, u32[]{:S(2)}, u32[]{:S(2)}) async-start(f32[32,16,2048]{2,1,0:T(8,128)} %bitcast.62), calls=%async_computation.4 | async-start | bytes 8388608 | tf_op jit(solution)/shard_map/all_to_all | solution.py:85
  252.5 101.5 %all-to-all-start.1 = ((f32[32,16,2048]{2,1,0:T(8,128)}), f32[32,16,2048]{2,1,0:T(8,128)}, u32[]{:S(2)}, u32[]{:S(2)}) async-start(f32[32,16,2048]{2,1,0:T(8,128)} %fusion.5), calls=%async_computation.1 | async-start | bytes 8388608 | tf_op jit(solution)/shard_map/all_to_all | solution.py:84
  257.4 122.6 %reduce-scatter.5.cloned.1.call-start = ((), (), s32[]{:S(2)}) async-start(), calls=%async_computation.7 | async-start | bytes 1179648 | tf_op jit(solution)/shard_map/reduce_scatter | solution.py:95
  271.5 166.9 %reduce-scatter.3.cloned.1.call-start = ((), (), s32[]{:S(2)}) async-start(), calls=%async_computation.6 | async-start | bytes 1179648 | tf_op jit(solution)/shard_map/reduce_scatter | solution.py:94
  368.0 3.8 copy-start.8
  371.8 4.1 copy-start.6
Sparse Core Ops, SparseCore 0:
  271.6 81.7 reduce-scatter.4
  368.1 70.1 reduce-scatter.2
where the time goes:
time: 450 us; the launch traced here: 447 us
  waiting for transfers between devices  313 us (70%)
  other arithmetic  41.4 us (9%)
  matrix products  31.1 us (7%)
  starting transfers between devices  24.7 us (5%)
  local copies, waits for them, and re-layouts  21.7 us (5%)
  between operations  14.3 us (3%)
    all_to_all x1, waiting for transfers between devices, on_device(): lax.all_to_all(in_blocks, 'dp', split_axis=0, concat_axis=0, tiled=True)  93.4 us
    all_to_all x1, waiting for transfers between devices, on_device(): lax.all_to_all(out_blocks, 'dp', split_axis=0, concat_axis=0, tiled=True)  82.3 us
    all_to_all x2, waiting for transfers between devices, deliver(): lax.all_to_all(buffer, 'dp', split_axis=0, concat_axis=0, tiled=True)  80.9 us
    reduce_scatter x1, waiting for transfers between devices, on_device(): lax.psum_scatter(y_part, 'expert', scatter_dimension=0, tiled=True)  56.8 us
    all_to_all x2, starting transfers between devices, deliver(): lax.all_to_all(buffer, 'dp', split_axis=0, concat_axis=0, tiled=True)  14.7 us
    scatter-add x1, other arithmetic, on_device(): jax.ops.segment_sum(jnp.where(is_live[:, None], back_in, 0.0), source_tok...  9.53 us
    scatter-add x1, other arithmetic, on_device(): jax.ops.segment_sum(row_weight[:, None] * back_out, source_tok, num_segme...  9.45 us
  transfers between devices with their start and end apart: 6, of which 5 were waited for; matrix products, arithmetic and copies ran while one was open for 14% of the time, Pallas kernels for 0%

commit v1 on v0

v1 whole, which is shorter than its diff:
```python
import jax
import jax.numpy as jnp
from jax import lax
from jax.experimental import pallas as pl
from jax.experimental.pallas import tpu as pltpu
from jax.sharding import Mesh, PartitionSpec as P

DP = ("z", "xl", "core")
EX = ("xh", "y")
PLANE = ("xl", "core", "xh", "y")
BF16 = jnp.bfloat16
F32 = jnp.float32
CAP = 16
META = 16


def nn(a, b):
    return lax.dot_general(a, b, (((1,), (0,)), ((), ())), preferred_element_type=F32)


def nt(a, b):
    return lax.dot_general(a, b, (((1,), (1,)), ((), ())), preferred_element_type=F32)


def tn(a, b):
    return lax.dot_general(a, b, (((0,), (0,)), ((), ())), preferred_element_type=F32)


def params(mib=48):
    return pltpu.CompilerParams(vmem_limit_bytes=mib * 2**20)


def whole(shape):
    return pl.BlockSpec(shape, lambda *_: (0,) * len(shape))


def route_kernel(col_ref, tok_ref, cot_ref, ids_ref, rw_ref, slot_ref, x_ref, g_ref):
    ntok = tok_ref.shape[0]
    x_ref[0:ntok, :] = tok_ref[...]
    g_ref[...] = cot_ref[...]
    table = jnp.broadcast_to(slot_ref[...], (8, slot_ref.shape[1]))
    slots = jnp.take_along_axis(table, ids_ref[...], axis=1, mode="promise_in_bounds").astype(F32)
    w = rw_ref[...]
    hi = w.astype(BF16).astype(F32)
    rest = w - hi
    mid = rest.astype(BF16).astype(F32)
    low = rest - mid
    left = jnp.concatenate([slots, mid], axis=0)
    right = jnp.concatenate([hi, low], axis=0)
    x_ref[ntok : ntok + META, 0:128] = left.astype(BF16)
    x_ref[ntok : ntok + META, 128:256] = right.astype(BF16)


def route(col, tokens, cotangent, ids_t, rw_t, slot_row):
    ntok, width = tokens.shape
    cut = width // 8
    return pl.pallas_call(
        route_kernel,
        grid_spec=pltpu.PrefetchScalarGridSpec(
            num_scalar_prefetch=1,
            grid=(1,),
            in_specs=[
                pl.BlockSpec((ntok, cut), lambda i, c: (0, c[0])),
                pl.BlockSpec((ntok, cut), lambda i, c: (0, c[0])),
                whole(ids_t.shape),
                whole(rw_t.shape),
                whole(slot_row.shape),
            ],
            out_specs=[whole((ntok + META, cut)), whole((ntok, cut))],
        ),
        out_shape=[
            jax.ShapeDtypeStruct((ntok + META, cut), BF16),
            jax.ShapeDtypeStruct((ntok, cut), BF16),
        ],
        compiler_params=params(),
        name="route",
    )(col, tokens, cotangent, ids_t, rw_t, slot_row)


def one_hot(place):
    slots, ntok = place.shape
    spread = jnp.broadcast_to(place[:, None, :], (slots, CAP, ntok)).reshape(slots * CAP, ntok)
    at = lax.broadcasted_iota(jnp.int32, (slots * CAP, ntok), 0) % CAP
    return spread == at.astype(F32)


def row_weights(hot, weight):
    slots, ntok = weight.shape
    spread = jnp.broadcast_to(weight[:, None, :], (slots, CAP, ntok)).reshape(slots * CAP, ntok)
    return jnp.sum(jnp.where(hot, spread, 0.0), axis=1, keepdims=True)


def as_bf16(hot):
    return jnp.where(hot, 1.0, 0.0).astype(BF16)


def put_rows(rows, send_ref):
    for l in range(rows.shape[0] // CAP):
        part = rows[l * CAP : (l + 1) * CAP]
        send_ref[2 * l] = part
        send_ref[2 * l + 1] = part


def pick_x_kernel(z_ref, x_ref, send_ref, place_ref, weight_ref):
    ntok = x_ref.shape[1] - META
    left = x_ref[0, ntok : ntok + META, 0:128].astype(F32)
    right = x_ref[0, ntok : ntok + META, 128:256].astype(F32)
    slots = left[0:8]
    w = right[0:8] + left[8:16] + right[8:16]
    first = (z_ref[0] * 16).astype(F32)
    local = lax.broadcasted_iota(jnp.int32, (16, ntok), 0).astype(F32) + first
    chosen = jnp.zeros((16, ntok), F32)
    weight = jnp.zeros((16, ntok), F32)
    for k in range(8):
        same = local == slots[k : k + 1, :]
        chosen = jnp.where(same, 1.0, chosen)
        weight = jnp.where(same, w[k : k + 1, :], weight)
    row = lax.broadcasted_iota(jnp.int32, (ntok, ntok), 0)
    column = lax.broadcasted_iota(jnp.int32, (ntok, ntok), 1)
    earlier = jnp.where(row < column, 1.0, 0.0).astype(BF16)
    before = nn(chosen.astype(BF16), earlier)
    place = jnp.where(chosen > 0.0, before, -1.0)
    place_ref[0] = place
    weight_ref[0] = weight
    rows = nn(as_bf16(one_hot(place)), x_ref[0, 0:ntok, :])
    put_rows(rows.astype(BF16), send_ref)


def pick_x(zs, x_all):
    blocks, rows, cut = x_all.shape
    ntok = rows - META
    return pl.pallas_call(
        pick_x_kernel,
        grid_spec=pltpu.PrefetchScalarGridSpec(
            num_scalar_prefetch=1,
            grid=(blocks,),
            in_specs=[pl.BlockSpec((1, rows, cut), lambda b, z: (b, 0, 0))],
            out_specs=[
                pl.BlockSpec((32, CAP, cut), lambda b, z: (0, b, 0)),
                pl.BlockSpec((1, 16, ntok), lambda b, z: (b, 0, 0)),
                pl.BlockSpec((1, 16, ntok), lambda b, z: (b, 0, 0)),
            ],
        ),
        out_shape=[
            jax.ShapeDtypeStruct((32, blocks * CAP, cut), BF16),
            jax.ShapeDtypeStruct((blocks, 16, ntok), F32),
            jax.ShapeDtypeStruct((blocks, 16, ntok), F32),
        ],
        compiler_params=params(),
        name="pick_x",
    )(zs, x_all)


def pick_g_kernel(g_ref, place_ref, weight_ref, send_ref):
    hot = one_hot(place_ref[0])
    rows = nn(as_bf16(hot), g_ref[0]) * row_weights(hot, weight_ref[0])
    put_rows(rows.astype(BF16), send_ref)


def pick_g(g_all, place, weight):
    blocks, ntok, cut = g_all.shape
    return pl.pallas_call(
        pick_g_kernel,
        grid=(blocks,),
        in_specs=[
            pl.BlockSpec((1, ntok, cut), lambda b: (b, 0, 0)),
            pl.BlockSpec((1, 16, ntok), lambda b: (b, 0, 0)),
            pl.BlockSpec((1, 16, ntok), lambda b: (b, 0, 0)),
        ],
        out_specs=pl.BlockSpec((32, CAP, cut), lambda b: (0, b, 0)),
        out_shape=jax.ShapeDtypeStruct((32, blocks * CAP, cut), BF16),
        compiler_params=params(),
        name="pick_g",
    )(g_all, place, weight)


def chunk(ref, e):
    return jnp.concatenate([ref[q * 8 + e] for q in range(4)], axis=0)


def put_chunk(ref, e, rows):
    for q in range(4):
        ref[q * 8 + e] = rows[q * 128 : (q + 1) * 128]


def forward_kernel(x_ref, wg_ref, wu_ref, wd_ref, out_ref, gate_ref, up_ref, hidden_ref):
    cut = x_ref.shape[2]

    def first(e, _):
        at = pl.ds(pl.multiple_of(e * cut, cut), cut)
        x = chunk(x_ref, e)
        gate_ref[...] += nn(x, wg_ref[0, at, :])
        up_ref[...] += nn(x, wu_ref[0, at, :])
        return 0

    gate_ref[...] = jnp.zeros_like(gate_ref)
    up_ref[...] = jnp.zeros_like(up_ref)
    lax.fori_loop(0, 8, first, 0)
    gate = gate_ref[...]
    hidden_ref[...] = (gate * jax.nn.sigmoid(gate) * up_ref[...]).astype(BF16)

    def second(e, _):
        at = pl.ds(pl.multiple_of(e * cut, cut), cut)
        put_chunk(out_ref, e, nn(hidden_ref[...], wd_ref[0, :, at]).astype(BF16))
        return 0

    lax.fori_loop(0, 8, second, 0)


def forward(x_rows, wg, wu, wd):
    rows, ff = 512, wg.shape[2]
    return pl.pallas_call(
        forward_kernel,
        out_shape=[
            jax.ShapeDtypeStruct(x_rows.shape, BF16),
            jax.ShapeDtypeStruct((rows, ff), F32),
            jax.ShapeDtypeStruct((rows, ff), F32),
            jax.ShapeDtypeStruct((rows, ff), BF16),
        ],
        compiler_params=params(),
        cost_estimate=pl.CostEstimate(
            flops=6 * rows * 2048 * ff, bytes_accessed=11 * 2**20, transcendentals=rows * ff
        ),
        name="forward",
    )(x_rows, wg, wu, wd)


def backward_kernel(
    g_ref, gate_ref, up_ref, wg_ref, wu_ref, wd_ref, in_ref, dgate_ref, dup_ref, back_ref
):
    cut = g_ref.shape[2]

    def first(e, _):
        at = pl.ds(pl.multiple_of(e * cut, cut), cut)
        back_ref[...] += nt(chunk(g_ref, e), wd_ref[0, :, at])
        return 0

    back_ref[...] = jnp.zeros_like(back_ref)
    lax.fori_loop(0, 8, first, 0)
    back, gate = back_ref[...], gate_ref[...]
    sigma = jax.nn.sigmoid(gate)
    dgate_ref[...] = (back * up_ref[...] * sigma * (1.0 + gate * (1.0 - sigma))).astype(BF16)
    dup_ref[...] = (back * (gate * sigma)).astype(BF16)

    def second(e, _):
        at = pl.ds(pl.multiple_of(e * cut, cut), cut)
        piece = nt(dgate_ref[...], wg_ref[0, at, :]) + nt(dup_ref[...], wu_ref[0, at, :])
        put_chunk(in_ref, e, piece.astype(BF16))
        return 0

    lax.fori_loop(0, 8, second, 0)


def backward(g_rows, gate, up, wg, wu, wd):
    rows, ff = gate.shape
    return pl.pallas_call(
        backward_kernel,
        out_shape=[
            jax.ShapeDtypeStruct(g_rows.shape, BF16),
            jax.ShapeDtypeStruct((rows, ff), BF16),
            jax.ShapeDtypeStruct((rows, ff), BF16),
        ],
        scratch_shapes=[pltpu.VMEM((rows, ff), F32)],
        compiler_params=params(),
        cost_estimate=pl.CostEstimate(
            flops=6 * rows * 2048 * ff, bytes_accessed=11 * 2**20, transcendentals=rows * ff
        ),
        name="backward",
    )(g_rows, gate, up, wg, wu, wd)


def grads_kernel(x_ref, g_ref, hidden_ref, dgate_ref, dup_ref, gg_ref, gu_ref, gd_ref):
    cut = x_ref.shape[2]

    def step(e, _):
        at = pl.ds(pl.multiple_of(e * cut, cut), cut)
        x = chunk(x_ref, e)
        gg_ref[0, at, :] = tn(x, dgate_ref[...]).astype(BF16)
        gu_ref[0, at, :] = tn(x, dup_ref[...]).astype(BF16)
        gd_ref[0, :, at] = tn(hidden_ref[...], chunk(g_ref, e)).astype(BF16)
        return 0

    lax.fori_loop(0, 8, step, 0)


def grads(x_rows, g_rows, hidden, dgate, dup):
    rows, ff = hidden.shape
    width = 8 * x_rows.shape[2]
    return pl.pallas_call(
        grads_kernel,
        out_shape=[
            jax.ShapeDtypeStruct((1, width, ff), BF16),
            jax.ShapeDtypeStruct((1, width, ff), BF16),
            jax.ShapeDtypeStruct((1, ff, width), BF16),
        ],
        compiler_params=params(),
        cost_estimate=pl.CostEstimate(
            flops=6 * rows * 2048 * ff, bytes_accessed=10 * 2**20, transcendentals=0
        ),
        name="grads",
    )(x_rows, g_rows, hidden, dgate, dup)


def add_rows(place, scale, back_ref, sum_ref):
    hot = one_hot(place)
    rows = jnp.concatenate(
        [back_ref[2 * l].astype(F32) + back_ref[2 * l + 1].astype(F32) for l in range(16)], axis=0
    )
    if scale is not None:
        rows = rows * row_weights(hot, scale)
    hi = rows.astype(BF16)
    low = (rows - hi.astype(F32)).astype(BF16)
    pick = as_bf16(hot)
    sum_ref[0] = (tn(pick, hi) + tn(pick, low)).astype(BF16)


def join_out_kernel(place_ref, weight_ref, back_ref, sum_ref):
    add_rows(place_ref[0], weight_ref[0], back_ref, sum_ref)


def join_in_kernel(place_ref, back_ref, sum_ref):
    add_rows(place_ref[0], None, back_ref, sum_ref)


def join(kernel, per_block, back, name):
    blocks, _, ntok = per_block[0].shape
    cut = back.shape[2]
    return pl.pallas_call(
        kernel,
        grid=(blocks,),
        in_specs=[pl.BlockSpec((1, 16, ntok), lambda b: (b, 0, 0)) for _ in per_block]
        + [pl.BlockSpec((32, CAP, cut), lambda b: (0, b, 0))],
        out_specs=pl.BlockSpec((1, ntok, cut), lambda b: (b, 0, 0)),
        out_shape=jax.ShapeDtypeStruct((blocks, ntok, cut), BF16),
        compiler_params=params(),
        name=name,
    )(*per_block, back)


def last_kernel(part_ref, out_ref, in_ref):
    cut = part_ref.shape[2]
    for e in range(8):
        total = part_ref[e].astype(F32)
        for z in range(1, 8):
            total = total + part_ref[z * 8 + e].astype(F32)
        half = total.shape[0] // 2
        out_ref[:, e * cut : (e + 1) * cut] = total[:half].astype(BF16)
        in_ref[:, e * cut : (e + 1) * cut] = total[half:].astype(BF16)


def last(parts):
    _, two, cut = parts.shape
    shape = jax.ShapeDtypeStruct((two // 2, 8 * cut), BF16)
    return pl.pallas_call(
        last_kernel, out_shape=[shape, shape], compiler_params=params(), name="last"
    )(parts)


def swap(buffer, axes):
    return lax.all_to_all(buffer, axes, split_axis=0, concat_axis=0, tiled=True)


def on_device(
    tokens, expert_ids, route_weight, expert_slot, gate_weight, up_weight, down_weight, cotangent
):
    col = lax.axis_index(EX).astype(jnp.int32).reshape(1)
    zs = lax.axis_index("z").astype(jnp.int32).reshape(1)
    x_cut, g_cut = route(
        col, tokens, cotangent, expert_ids.T, route_weight.T, expert_slot.reshape(1, -1)
    )
    x_all = lax.all_gather(x_cut, "z", axis=0, tiled=False)
    g_all = lax.all_gather(g_cut, "z", axis=0, tiled=False)
    x_send, place, weight = pick_x(zs, x_all)
    x_rows = swap(x_send, PLANE)
    g_send = pick_g(g_all, place, weight)
    g_rows = swap(g_send, PLANE)
    out_send, gate, up, hidden = forward(x_rows, gate_weight, up_weight, down_weight)
    out_back = swap(out_send, PLANE)
    in_send, dgate, dup = backward(g_rows, gate, up, gate_weight, up_weight, down_weight)
    in_back = swap(in_send, PLANE)
    grad_gate, grad_up, grad_down = grads(x_rows, g_rows, hidden, dgate, dup)
    y_part = join(join_out_kernel, (place, weight), out_back, "join_out")
    dx_part = join(join_in_kernel, (place,), in_back, "join_in")
    cut = y_part.shape[2]
    both = jnp.concatenate(
        [y_part.reshape(64, 16, cut), dx_part.reshape(64, 16, cut)], axis=1
    )
    layer_out, input_grad = last(swap(both, ("z", "xh", "y")))
    return layer_out, input_grad, grad_gate, grad_up, grad_down


def solution(mesh):
    fine = Mesh(mesh.devices.reshape(8, 2, 2, 2, 4), ("z", "xl", "core", "xh", "y"))
    rows, every = P(DP, None), P(DP + EX, None)
    half = P(DP + EX, None, None)
    return jax.shard_map(
        on_device,
        mesh=fine,
        in_specs=(rows, rows, rows, P(), half, half, half, rows),
        out_specs=(every, every, half, half, half),
        check_vma=False,
    )
```

time: 450 us -> 223 us (0.50)
  waiting for transfers between devices: 313 us -> 64.3 us
  blocking collectives: 0 us -> 54.8 us
  Pallas kernels: 0 us -> 42.7 us
  other arithmetic: 41.4 us -> 1.19 us
  matrix products: 31.1 us -> 0 us
  starting transfers between devices: 24.7 us -> 39.2 us
  between operations: 14.3 us -> 0.8 us
    all_to_all x4 -> x5, waiting for transfers between devices: 257 us -> 64.3 us  [swap(): return lax.all_to_all(buffer, axes, split_axis=0, concat_axis=0, tiled=True)]
    reduce_scatter x2 -> x0, waiting for transfers between devices: 56.8 us -> none  [the longest x1 56.8 us: on_device(): lax.psum_scatter(y_part, 'expert', scatter_dimension=0, tiled=True)]
    all_gather x0 -> x2, blocking collectives: none -> 54.8 us  [the longest x1 29.2 us: on_device(): x_all = lax.all_gather(x_cut, 'z', axis=0, tiled=False)]
    pallas_call x0 -> x9, Pallas kernels: none -> 42.7 us  [the longest x1 10 us: backward(): pl.pallas_call(backward_kernel, out_shape=[jax.ShapeDtypeStruct(g_rows.sh...]
    dot_general x9 -> x0, matrix products: 31.1 us -> none  [the longest x1 4.28 us: half_expert(): up_val = jnp.dot(x_rows, w_up, preferred_element_type=jnp.float32)]
    scatter-add x2 -> x0, other arithmetic: 19 us -> none  [the longest x1 9.53 us: on_device(): jax.ops.segment_sum(jnp.where(is_live[:, None], back_in, 0.0), source_tok...]
    unnamed x22 -> x40, local copies, waits for them, and re-layouts: 1.45 us -> 17.9 us
    all_to_all x4 -> x5, starting transfers between devices: 24.4 us -> 39.2 us  [swap(): return lax.all_to_all(buffer, axes, split_axis=0, concat_axis=0, tiled=True)]
  transfers between devices with their start and end apart: 6 -> 5, of which waited for: 5 -> 4; matrix products, arithmetic and copies ran while one was open for 14% -> 0% of each run, Pallas kernels for 0% -> 15%
where the time goes in v1:
time: 223 us; the launch traced here: 221 us
  waiting for transfers between devices  64.3 us (29%)
  blocking collectives  54.8 us (25%)
  Pallas kernels  42.7 us (19%)
  starting transfers between devices  39.2 us (18%)
  local copies, waits for them, and re-layouts  17.9 us (8%)
    all_to_all x5, waiting for transfers between devices, swap(): return lax.all_to_all(buffer, axes, split_axis=0, concat_axis=0, tiled=True)  64.3 us
    all_to_all x5, starting transfers between devices, swap(): return lax.all_to_all(buffer, axes, split_axis=0, concat_axis=0, tiled=True)  39.2 us
    all_gather x1, blocking collectives, on_device(): x_all = lax.all_gather(x_cut, 'z', axis=0, tiled=False)  29.2 us
    all_gather x1, blocking collectives, on_device(): g_all = lax.all_gather(g_cut, 'z', axis=0, tiled=False)  25.5 us
    unnamed x40, local copies, waits for them, and re-layouts  17.9 us
    pallas_call x1, Pallas kernels, backward(): pl.pallas_call(backward_kernel, out_shape=[jax.ShapeDtypeStruct(g_rows.sh...  10 us
    pallas_call x1, Pallas kernels, forward(): pl.pallas_call(forward_kernel, out_shape=[jax.ShapeDtypeStruct(x_rows.sha...  9.59 us
    pallas_call x1, Pallas kernels, grads(): pl.pallas_call(grads_kernel, out_shape=[jax.ShapeDtypeStruct((1, width, f...  8.1 us
  transfers between devices with their start and end apart: 5, of which 4 were waited for; matrix products, arithmetic and copies ran while one was open for 0% of the time, Pallas kernels for 15%

profile of v1, /device:TPU:28, one launch (start us, length us, event | category | flops | bytes accessed | tf_op | source)
XLA Modules:
  0.0 220.9 jit_solution(17507154500209045799)
XLA Ops:
  0.6 1.0 copy-done.3
  1.7 1.0 copy-done.4
  4.8 29.2 %all-gather = bf16[1152,256]{1,0:T(8,128)(2,1)S(1)} all-gather(bf16[144,256]{1,0:T(8,128)(2,1)S(1)} %get-tuple-element.22), channel_id=2, replica_groups=mesh['z'=8,'xl'=2,'core'=2,'xh'=2,'y'=4] {'z'}, dimensions={0}, use_global_device_ids=true | all-gather | bytes 663552 | tf_op jit(solution)/shard_map/all_gather | solution.py:371
  34.1 2.6 %pick_x.1 = (bf16[32,128,256]{2,1,0:T(8,128)(2,1)S(1)}, f32[8,16,128]{2,1,0:T(8,128)S(1)}, f32[8,16,128]{2,1,0:T(8,128)S(1)}) custom-call(s32[1]{0:T(128)} %bitcast.z_ref, bf16[8,144,256]{2,1,0:T(8,128)(2,1)S(1)} %bitcast.9), custom_call_target="tpu_custom_call" | custom-call | tf_op jit(solution)/shard_map/pick_x/pallas_call | solution.py:132
  36.7 1.3 copy-done.2
  38.0 7.3 %all-to-all-start = ((bf16[32,128,256]{2,1,0:T(8,128)(2,1)}), bf16[32,128,256]{2,1,0:T(8,128)(2,1)S(1)}, u32[]{:S(2)}, u32[]{:S(2)}) async-start(bf16[32,128,256]{2,1,0:T(8,128)(2,1)} %copy-done.2), calls=%async_computation | async-start | bytes 4194304 | tf_op jit(solution)/shard_map/all_to_all | solution.py:360
  45.3 25.5 %all-gather.1 = bf16[1024,256]{1,0:T(8,128)(2,1)S(1)} all-gather(bf16[128,256]{1,0:T(8,128)(2,1)S(1)} %get-tuple-element.27), channel_id=3, replica_groups=mesh['z'=8,'xl'=2,'core'=2,'xh'=2,'y'=4] {'z'}, dimensions={0}, use_global_device_ids=true | all-gather | bytes 589824 | tf_op jit(solution)/shard_map/all_gather | solution.py:372
  70.8 3.9 %pick_g.1 = bf16[32,128,256]{2,1,0:T(8,128)(2,1)} custom-call(bf16[8,128,256]{2,1,0:T(8,128)(2,1)S(1)} %bitcast.10, f32[8,16,128]{2,1,0:T(8,128)S(1)} %get-tuple-element.23.place_ref, f32[8,16,128]{2,1,0:T(8,128)S(1)} %get-tuple-element.24.weight_ref), custom_call_target="tpu_custom_call" | custom-call | tf_op jit(solution)/shard_map/pick_g/pallas_call | solution.py:162
  74.7 1.3 copy-done
  76.1 7.3 %all-to-all-start.2 = ((bf16[32,128,256]{2,1,0:T(8,128)(2,1)}), bf16[32,128,256]{2,1,0:T(8,128)(2,1)}, u32[]{:S(2)}, u32[]{:S(2)}) async-start(bf16[32,128,256]{2,1,0:T(8,128)(2,1)} %pick_g.1), calls=%async_computation.2 | async-start | bytes 4194304 | tf_op jit(solution)/shard_map/all_to_all | solution.py:360
  83.4 1.4 copy-done.8
  84.8 1.4 copy-done.10
  86.2 9.6 %forward.1 = (bf16[32,128,256]{2,1,0:T(8,128)(2,1)}, f32[512,384]{1,0:T(8,128)S(1)}, f32[512,384]{1,0:T(8,128)S(1)}, bf16[512,384]{1,0:T(8,128)(2,1)S(1)}) custom-call(bf16[32,128,256]{2,1,0:T(8,128)(2,1)} %copy-done, bf16[1,2048,384]{2,1,0:T(8,128)(2,1)S(1)} %copy-done.8, bf16[1,2048,384]{2,1,0:T(8,128)(2,1)S(1)} %copy-done.10, bf16[1,384,2048]{2,1,0:T(8,128)(2,1)} %wd_ref.3), custom_call_target="tpu_custom_call" | custom-call | flops 2415919104 | bytes 11534336 | tf_op jit(solution)/shard_map/forward/pallas_call | solution.py:212
  95.8 0.9 copy-done.12
  97.4 12.1 %all-to-all-done.2.g_ref = bf16[32,128,256]{2,1,0:T(8,128)(2,1)} async-done(((bf16[32,128,256]{2,1,0:T(8,128)(2,1)}), bf16[32,128,256]{2,1,0:T(8,128)(2,1)}, u32[]{:S(2)}, u32[]{:S(2)}) %all-to-all-start.2) | async-done | bytes 2097184 | tf_op jit(solution)/shard_map/all_to_all | solution.py:360
  109.5 7.1 %all-to-all-start.1 = ((bf16[32,128,256]{2,1,0:T(8,128)(2,1)}), bf16[32,128,256]{2,1,0:T(8,128)(2,1)S(1)}, u32[]{:S(2)}, u32[]{:S(2)}) async-start(bf16[32,128,256]{2,1,0:T(8,128)(2,1)} %get-tuple-element.26), calls=%async_computation.1 | async-start | bytes 4194304 | tf_op jit(solution)/shard_map/all_to_all | solution.py:360
  116.6 1.4 copy-done.9
  118.0 1.4 copy-done.11
  119.4 1.1 copy-done.13
  120.5 10.0 %backward.1 = (bf16[32,128,256]{2,1,0:T(8,128)(2,1)}, bf16[512,384]{1,0:T(8,128)(2,1)S(1)}, bf16[512,384]{1,0:T(8,128)(2,1)S(1)}) custom-call(bf16[32,128,256]{2,1,0:T(8,128)(2,1)} %all-to-all-done.2.g_ref, f32[512,384]{1,0:T(8,128)S(1)} %get-tuple-element.28.gate_ref, f32[512,384]{1,0:T(8,128)S(1)} %copy-done.13, bf16[1,2048,384]{2,1,0:T(8,128)(2,1)S(1)} %copy-done.9, ...), custom_call_target="tpu_custom_call" | custom-call | flops 2415919104 | bytes 11534336 | tf_op jit(solution)/shard_map/backward/pallas_call | solution.py:256
  131.3 11.4 %all-to-all-done.1.back_ref = bf16[32,128,256]{2,1,0:T(8,128)(2,1)S(1)} async-done(((bf16[32,128,256]{2,1,0:T(8,128)(2,1)}), bf16[32,128,256]{2,1,0:T(8,128)(2,1)S(1)}, u32[]{:S(2)}, u32[]{:S(2)}) %all-to-all-start.1) | async-done | bytes 2097184 | tf_op jit(solution)/shard_map/all_to_all | solution.py:360
  142.6 7.1 %all-to-all-start.3 = ((bf16[32,128,256]{2,1,0:T(8,128)(2,1)}), bf16[32,128,256]{2,1,0:T(8,128)(2,1)}, u32[]{:S(2)}, u32[]{:S(2)}) async-start(bf16[32,128,256]{2,1,0:T(8,128)(2,1)} %get-tuple-element.30), calls=%async_computation.3 | async-start | bytes 4194304 | tf_op jit(solution)/shard_map/all_to_all | solution.py:360
  149.8 2.5 %join_out.1 = bf16[8,128,256]{2,1,0:T(8,128)(2,1)S(1)} custom-call(f32[8,16,128]{2,1,0:T(8,128)S(1)} %get-tuple-element.23.place_ref, f32[8,16,128]{2,1,0:T(8,128)S(1)} %get-tuple-element.24.weight_ref, bf16[32,128,256]{2,1,0:T(8,128)(2,1)S(1)} %all-to-all-done.1.back_ref), custom_call_target="tpu_custom_call" | custom-call | tf_op jit(solution)/shard_map/join_out/pallas_call | solution.py:328
  152.2 23.7 %all-to-all-done.3.back_ref = bf16[32,128,256]{2,1,0:T(8,128)(2,1)} async-done(((bf16[32,128,256]{2,1,0:T(8,128)(2,1)}), bf16[32,128,256]{2,1,0:T(8,128)(2,1)}, u32[]{:S(2)}, u32[]{:S(2)}) %all-to-all-start.3) | async-done | bytes 2097184 | tf_op jit(solution)/shard_map/all_to_all | solution.py:360
  175.9 5.2 %join_in.1 = bf16[8,128,256]{2,1,0:T(8,128)(2,1)S(1)} custom-call(f32[8,16,128]{2,1,0:T(8,128)S(1)} %get-tuple-element.23.place_ref, bf16[32,128,256]{2,1,0:T(8,128)(2,1)} %all-to-all-done.3.back_ref), custom_call_target="tpu_custom_call" | custom-call | tf_op jit(solution)/shard_map/join_in/pallas_call | solution.py:328
  181.1 1.2 pad_maximum_fusion
  182.3 10.5 %all-to-all-start.4 = ((bf16[64,32,256]{2,1,0:T(8,128)(2,1)}), bf16[64,32,256]{2,1,0:T(8,128)(2,1)S(1)}, u32[]{:S(2)}, u32[]{:S(2)}) async-start(bf16[64,32,256]{2,1,0:T(8,128)(2,1)} %pad_maximum_fusion), calls=%async_computation.4 | async-start | bytes 2097152 | tf_op jit(solution)/shard_map/all_to_all | solution.py:360
  192.8 1.0 copy-done.17
  193.8 1.0 copy-done.19
  194.8 8.1 %grads.1 = (bf16[1,2048,384]{2,1,0:T(8,128)(2,1)}, bf16[1,2048,384]{2,1,0:T(8,128)(2,1)}, bf16[1,384,2048]{2,1,0:T(8,128)(2,1)}) custom-call(bf16[32,128,256]{2,1,0:T(8,128)(2,1)S(1)} %copy-done.1, bf16[32,128,256]{2,1,0:T(8,128)(2,1)} %all-to-all-done.2.g_ref, bf16[512,384]{1,0:T(8,128)(2,1)S(1)} %copy-done.19, bf16[512,384]{1,0:T(8,128)(2,1)S(1)} %copy-done.15, ...), custom_call_target="tpu_custom_call" | custom-call | flops 2415919104 | bytes 10485760 | tf_op jit(solution)/shard_map/grads/pallas_call | solution.py:289
  202.9 17.2 %all-to-all-done.4.part_ref = bf16[64,32,256]{2,1,0:T(8,128)(2,1)S(1)} async-done(((bf16[64,32,256]{2,1,0:T(8,128)(2,1)}), bf16[64,32,256]{2,1,0:T(8,128)(2,1)S(1)}, u32[]{:S(2)}, u32[]{:S(2)}) %all-to-all-start.4) | async-done | bytes 1048608 | tf_op jit(solution)/shard_map/all_to_all | solution.py:360
  220.1 0.8 last.1
  (30 shorter events, 3.6 us)
Async XLA Ops:
  0.6 1.0 copy-start.3
  1.7 1.0 copy-start.4
  2.7 0.7 copy-start.5
  3.4 0.7 copy-start.6
  4.1 0.7 copy-start.7
  36.7 1.3 copy-start.2
  38.0 36.7 %all-to-all-start = ((bf16[32,128,256]{2,1,0:T(8,128)(2,1)}), bf16[32,128,256]{2,1,0:T(8,128)(2,1)S(1)}, u32[]{:S(2)}, u32[]{:S(2)}) async-start(bf16[32,128,256]{2,1,0:T(8,128)(2,1)} %copy-done.2), calls=%async_computation | async-start | bytes 4194304 | tf_op jit(solution)/shard_map/all_to_all | solution.py:360
  74.7 1.3 copy-start
  76.1 33.4 %all-to-all-start.2 = ((bf16[32,128,256]{2,1,0:T(8,128)(2,1)}), bf16[32,128,256]{2,1,0:T(8,128)(2,1)}, u32[]{:S(2)}, u32[]{:S(2)}) async-start(bf16[32,128,256]{2,1,0:T(8,128)(2,1)} %pick_g.1), calls=%async_computation.2 | async-start | bytes 4194304 | tf_op jit(solution)/shard_map/all_to_all | solution.py:360
  83.4 1.4 copy-start.8
  84.8 1.4 copy-start.10
  95.8 0.9 copy-start.12
  96.7 0.7 copy-start.18
  109.5 33.2 %all-to-all-start.1 = ((bf16[32,128,256]{2,1,0:T(8,128)(2,1)}), bf16[32,128,256]{2,1,0:T(8,128)(2,1)S(1)}, u32[]{:S(2)}, u32[]{:S(2)}) async-start(bf16[32,128,256]{2,1,0:T(8,128)(2,1)} %get-tuple-element.26), calls=%async_computation.1 | async-start | bytes 4194304 | tf_op jit(solution)/shard_map/all_to_all | solution.py:360
  116.6 1.4 copy-start.9
  118.0 1.4 copy-start.11
  119.4 1.1 copy-start.13
  130.5 0.7 copy-start.16
  131.3 11.4 %copy-start.14 = (bf16[512,384]{1,0:T(8,128)(2,1)}, bf16[512,384]{1,0:T(8,128)(2,1)S(1)}, u32[]{:S(2)}) copy-start(bf16[512,384]{1,0:T(8,128)(2,1)S(1)} %get-tuple-element.34.dgate_ref) | copy-start | bytes 1179652
  142.6 33.3 %all-to-all-start.3 = ((bf16[32,128,256]{2,1,0:T(8,128)(2,1)}), bf16[32,128,256]{2,1,0:T(8,128)(2,1)}, u32[]{:S(2)}, u32[]{:S(2)}) async-start(bf16[32,128,256]{2,1,0:T(8,128)(2,1)} %get-tuple-element.30), calls=%async_computation.3 | async-start | bytes 4194304 | tf_op jit(solution)/shard_map/all_to_all | solution.py:360
  181.1 11.7 %copy-start.1 = (bf16[32,128,256]{2,1,0:T(8,128)(2,1)S(1)}, bf16[32,128,256]{2,1,0:T(8,128)(2,1)}, u32[]{:S(2)}) copy-start(bf16[32,128,256]{2,1,0:T(8,128)(2,1)} %copy-done) | copy-start | bytes 6291460
  181.1 11.7 %copy-start.15 = (bf16[512,384]{1,0:T(8,128)(2,1)S(1)}, bf16[512,384]{1,0:T(8,128)(2,1)}, u32[]{:S(2)}) copy-start(bf16[512,384]{1,0:T(8,128)(2,1)} %copy-done.14) | copy-start | bytes 1179652
  182.3 37.8 %all-to-all-start.4 = ((bf16[64,32,256]{2,1,0:T(8,128)(2,1)}), bf16[64,32,256]{2,1,0:T(8,128)(2,1)S(1)}, u32[]{:S(2)}, u32[]{:S(2)}) async-start(bf16[64,32,256]{2,1,0:T(8,128)(2,1)} %pad_maximum_fusion), calls=%async_computation.4 | async-start | bytes 2097152 | tf_op jit(solution)/shard_map/all_to_all | solution.py:360
  192.8 1.0 copy-start.17
  193.8 1.0 copy-start.19

commit v2 on v1

--- a/solution.py
+++ b/solution.py
@@ -1,3 +1,5 @@
+import functools
+
 import jax
 import jax.numpy as jnp
 from jax import lax
@@ -26,7 +28,7 @@
     return lax.dot_general(a, b, (((0,), (0,)), ((), ())), preferred_element_type=F32)
 
 
-def params(mib=48):
+def params(mib=16):
     return pltpu.CompilerParams(vmem_limit_bytes=mib * 2**20)
 
 
@@ -36,7 +38,6 @@
 
 def route_kernel(col_ref, tok_ref, cot_ref, ids_ref, rw_ref, slot_ref, x_ref, g_ref):
     ntok = tok_ref.shape[0]
-    x_ref[0:ntok, :] = tok_ref[...]
     g_ref[...] = cot_ref[...]
     table = jnp.broadcast_to(slot_ref[...], (8, slot_ref.shape[1]))
     slots = jnp.take_along_axis(table, ids_ref[...], axis=1, mode="promise_in_bounds").astype(F32)
@@ -47,8 +48,11 @@
     low = rest - mid
     left = jnp.concatenate([slots, mid], axis=0)
     right = jnp.concatenate([hi, low], axis=0)
-    x_ref[ntok : ntok + META, 0:128] = left.astype(BF16)
-    x_ref[ntok : ntok + META, 128:256] = right.astype(BF16)
+    tok, left, right = tok_ref[...], left.astype(BF16), right.astype(BF16)
+    for z in range(x_ref.shape[0]):
+        x_ref[z, 0:ntok, :] = tok
+        x_ref[z, ntok : ntok + META, 0:128] = left
+        x_ref[z, ntok : ntok + META, 128:256] = right
 
 
 def route(col, tokens, cotangent, ids_t, rw_t, slot_row):
@@ -66,13 +70,13 @@
                 whole(rw_t.shape),
                 whole(slot_row.shape),
             ],
-            out_specs=[whole((ntok + META, cut)), whole((ntok, cut))],
+            out_specs=[whole((8, ntok + META, cut)), whole((ntok, cut))],
         ),
         out_shape=[
-            jax.ShapeDtypeStruct((ntok + META, cut), BF16),
+            jax.ShapeDtypeStruct((8, ntok + META, cut), BF16),
             jax.ShapeDtypeStruct((ntok, cut), BF16),
         ],
-        compiler_params=params(),
+        compiler_params=params(60),
         name="route",
     )(col, tokens, cotangent, ids_t, rw_t, slot_row)
 
@@ -151,27 +155,30 @@
     )(zs, x_all)
 
 
-def pick_g_kernel(g_ref, place_ref, weight_ref, send_ref):
-    hot = one_hot(place_ref[0])
-    rows = nn(as_bf16(hot), g_ref[0]) * row_weights(hot, weight_ref[0])
-    put_rows(rows.astype(BF16), send_ref)
-
-
-def pick_g(g_all, place, weight):
-    blocks, ntok, cut = g_all.shape
+def pick_g_kernel(z_ref, *refs):
+    g_refs, (place_ref, weight_ref, send_ref) = refs[:8], refs[8:]
+    for shift, g_ref in enumerate(g_refs):
+        block = lax.rem(z_ref[0] + 8 - shift, 8)
+        hot = one_hot(place_ref[block])
+        rows = nn(as_bf16(hot), g_ref[...]) * row_weights(hot, weight_ref[block])
+        put_rows(rows.astype(BF16), send_ref.at[:, pl.ds(pl.multiple_of(block * CAP, CAP), CAP), :])
+
+
+def pick_g(zs, g_blocks, place, weight):
+    blocks = place.shape[0]
+    ntok, cut = g_blocks[0].shape
     return pl.pallas_call(
         pick_g_kernel,
-        grid=(blocks,),
-        in_specs=[
-            pl.BlockSpec((1, ntok, cut), lambda b: (b, 0, 0)),
-            pl.BlockSpec((1, 16, ntok), lambda b: (b, 0, 0)),
-            pl.BlockSpec((1, 16, ntok), lambda b: (b, 0, 0)),
-        ],
-        out_specs=pl.BlockSpec((32, CAP, cut), lambda b: (0, b, 0)),
+        grid_spec=pltpu.PrefetchScalarGridSpec(
+            num_scalar_prefetch=1,
+            grid=(1,),
+            in_specs=[whole((ntok, cut))] * 8 + [whole(place.shape), whole(weight.shape)],
+            out_specs=whole((32, blocks * CAP, cut)),
+        ),
         out_shape=jax.ShapeDtypeStruct((32, blocks * CAP, cut), BF16),
         compiler_params=params(),
         name="pick_g",
-    )(g_all, place, weight)
+    )(zs, *g_blocks, place, weight)
 
 
 def chunk(ref, e):
@@ -301,40 +308,52 @@
     )(x_rows, g_rows, hidden, dgate, dup)
 
 
-def add_rows(place, scale, back_ref, sum_ref):
+def add_rows(place, scale, back, like):
     hot = one_hot(place)
     rows = jnp.concatenate(
-        [back_ref[2 * l].astype(F32) + back_ref[2 * l + 1].astype(F32) for l in range(16)], axis=0
+        [back[2 * l].astype(F32) + back[2 * l + 1].astype(F32) for l in range(16)], axis=0
     )
     if scale is not None:
         rows = rows * row_weights(hot, scale)
     hi = rows.astype(BF16)
     low = (rows - hi.astype(F32)).astype(BF16)
     pick = as_bf16(hot)
-    sum_ref[0] = (tn(pick, hi) + tn(pick, low)).astype(BF16)
-
-
-def join_out_kernel(place_ref, weight_ref, back_ref, sum_ref):
-    add_rows(place_ref[0], weight_ref[0], back_ref, sum_ref)
-
-
-def join_in_kernel(place_ref, back_ref, sum_ref):
-    add_rows(place_ref[0], None, back_ref, sum_ref)
-
-
-def join(kernel, per_block, back, name):
+    return (tn(pick, hi) + tn(pick, low)).astype(BF16).reshape(like)
+
+
+def join_kernel(weighted, *refs):
+    place_ref, back_ref, sum_ref = refs[0], refs[2 if weighted else 1], refs[-1]
+    blocks = place_ref.shape[0]
+    eighth, part, cut = sum_ref.shape[0] // blocks, sum_ref.shape[1], sum_ref.shape[2]
+
+    def step(b, _):
+        rows = pl.ds(pl.multiple_of(b * CAP, CAP), CAP)
+        scale = refs[1][b] if weighted else None
+        total = add_rows(place_ref[b], scale, back_ref.at[:, rows, :], (eighth, part, cut))
+        sum_ref[pl.ds(b * eighth, eighth)] = total
+        return 0
+
+    lax.fori_loop(0, blocks, step, 0)
+
+
+def join(per_block, back, half, buffer, name):
     blocks, _, ntok = per_block[0].shape
     cut = back.shape[2]
-    return pl.pallas_call(
-        kernel,
-        grid=(blocks,),
-        in_specs=[pl.BlockSpec((1, 16, ntok), lambda b: (b, 0, 0)) for _ in per_block]
-        + [pl.BlockSpec((32, CAP, cut), lambda b: (0, b, 0))],
-        out_specs=pl.BlockSpec((1, ntok, cut), lambda b: (b, 0, 0)),
-        out_shape=jax.ShapeDtypeStruct((blocks, ntok, cut), BF16),
+    part = ntok // 8
+    given = [] if buffer is None else [buffer]
+    count = len(per_block) + 1
+    return pl.pallas_call(
+        functools.partial(join_kernel, len(per_block) == 2),
+        grid=(1,),
+        in_specs=[whole(a.shape) for a in per_block]
+        + [whole(back.shape)]
+        + [pl.BlockSpec(memory_space=pl.ANY) for _ in given],
+        out_specs=pl.BlockSpec((8 * blocks, part, cut), lambda i: (0, half, 0)),
+        out_shape=jax.ShapeDtypeStruct((8 * blocks, 2 * part, cut), BF16),
+        input_output_aliases={count: 0} if given else {},
         compiler_params=params(),
         name=name,
-    )(*per_block, back)
+    )(*per_block, back, *given)
 
 
 def last_kernel(part_ref, out_ref, in_ref):
@@ -368,25 +387,24 @@
     x_cut, g_cut = route(
         col, tokens, cotangent, expert_ids.T, route_weight.T, expert_slot.reshape(1, -1)
     )
-    x_all = lax.all_gather(x_cut, "z", axis=0, tiled=False)
-    g_all = lax.all_gather(g_cut, "z", axis=0, tiled=False)
+    x_all = swap(x_cut, ("z",))
     x_send, place, weight = pick_x(zs, x_all)
+    g_blocks = [g_cut] + [
+        lax.ppermute(g_cut, "z", [(z, (z + shift) % 8) for z in range(8)]) for shift in range(1, 8)
+    ]
     x_rows = swap(x_send, PLANE)
-    g_send = pick_g(g_all, place, weight)
+    g_send = pick_g(zs, g_blocks, place, weight)
     g_rows = swap(g_send, PLANE)
     out_send, gate, up, hidden = forward(x_rows, gate_weight, up_weight, down_weight)
     out_back = swap(out_send, PLANE)
     in_send, dgate, dup = backward(g_rows, gate, up, gate_weight, up_weight, down_weight)
     in_back = swap(in_send, PLANE)
-    grad_gate, grad_up, grad_down = grads(x_rows, g_rows, hidden, dgate, dup)
-    y_part = join(join_out_kernel, (place, weight), out_back, "join_out")
-    dx_part = join(join_in_kernel, (place,), in_back, "join_in")
-    cut = y_part.shape[2]
-    both = jnp.concatenate(
-        [y_part.reshape(64, 16, cut), dx_part.reshape(64, 16, cut)], axis=1
-    )
+    weight_grads = grads(x_rows, g_rows, hidden, dgate, dup)
+    both = join((place, weight), out_back, 0, None, "join_out")
+    in_back, both, weight_grads = lax.optimization_barrier((in_back, both, weight_grads))
+    both = join((place,), in_back, 1, both, "join_in")
     layer_out, input_grad = last(swap(both, ("z", "xh", "y")))
-    return layer_out, input_grad, grad_gate, grad_up, grad_down
+    return layer_out, input_grad, *weight_grads
 
 
 def solution(mesh):

time: 223 us -> 208 us (0.933)
  blocking collectives: 54.8 us -> 34.6 us
  starting transfers between devices: 39.2 us -> 50.2 us
  Pallas kernels: 42.7 us -> 35.3 us
    all_gather x2 -> x0, blocking collectives: 54.8 us -> none  [the longest x1 29.2 us: on_device(): x_all = lax.all_gather(x_cut, 'z', axis=0, tiled=False)]
    all_to_all x0 -> x1, blocking collectives: none -> 34.6 us  [swap(): return lax.all_to_all(buffer, axes, split_axis=0, concat_axis=0, tiled=True)]
    ppermute x0 -> x7, starting transfers between devices: none -> 12.9 us  [on_device(): lax.ppermute(g_cut, 'z', [(z, (z + shift) % 8) for z in range(8)])]
    ppermute x0 -> x7, waiting for transfers between devices: none -> 7.42 us  [on_device(): lax.ppermute(g_cut, 'z', [(z, (z + shift) % 8) for z in range(8)])]
    all_to_all x5, waiting for transfers between devices: 64.3 us -> 58.2 us  [swap(): return lax.all_to_all(buffer, axes, split_axis=0, concat_axis=0, tiled=True)]
    pallas_call x3, Pallas kernels: 11.5 us -> 7.75 us  [the longest x2 5.87 us: join(): pl.pallas_call(functools.partial(join_kernel, len(per_block) == 2), grid=...]
    pallas_call x1, Pallas kernels: 9.59 us -> 6.16 us  [forward(): pl.pallas_call(forward_kernel, out_shape=[jax.ShapeDtypeStruct(x_rows.sha...]
  transfers between devices with their start and end apart: 5 -> 12, of which waited for: 4 -> 9; matrix products, arithmetic and copies ran while one was open for 0% -> 0% of each run, Pallas kernels for 15% -> 13%
where the time goes in v2:
time: 208 us; the launch traced here: 206 us
  waiting for transfers between devices  65.6 us (32%)
  starting transfers between devices  50.2 us (24%)
  Pallas kernels  35.3 us (17%)
  blocking collectives  34.6 us (17%)
  local copies, waits for them, and re-layouts  19.4 us (9%)
    all_to_all x5, waiting for transfers between devices, swap(): return lax.all_to_all(buffer, axes, split_axis=0, concat_axis=0, tiled=True)  58.2 us
    all_to_all x5, starting transfers between devices, swap(): return lax.all_to_all(buffer, axes, split_axis=0, concat_axis=0, tiled=True)  37.3 us
    all_to_all x1, blocking collectives, swap(): return lax.all_to_all(buffer, axes, split_axis=0, concat_axis=0, tiled=True)  34.6 us
    unnamed x40, local copies, waits for them, and re-layouts  19.4 us
    ppermute x7, starting transfers between devices, on_device(): lax.ppermute(g_cut, 'z', [(z, (z + shift) % 8) for z in range(8)])  12.9 us
    pallas_call x1, Pallas kernels, backward(): pl.pallas_call(backward_kernel, out_shape=[jax.ShapeDtypeStruct(g_rows.sh...  8.19 us
    pallas_call x1, Pallas kernels, grads(): pl.pallas_call(grads_kernel, out_shape=[jax.ShapeDtypeStruct((1, width, f...  8.1 us
    ppermute x7, waiting for transfers between devices, on_device(): lax.ppermute(g_cut, 'z', [(z, (z + shift) % 8) for z in range(8)])  7.42 us
  transfers between devices with their start and end apart: 12, of which 9 were waited for; matrix products, arithmetic and copies ran while one was open for 0% of the time, Pallas kernels for 13%

profile of v2, /device:TPU:28, one launch (start us, length us, event | category | flops | bytes accessed | tf_op | source)
XLA Modules:
  0.0 206.0 jit_solution(1614840015000255117)
XLA Ops:
  0.6 1.8 route.1
  2.4 8.5 %all-to-all-start = ((bf16[8,144,256]{2,1,0:T(8,128)(2,1)}), bf16[8,144,256]{2,1,0:T(8,128)(2,1)S(1)}, u32[]{:S(2)}, u32[]{:S(2)}) async-start(bf16[8,144,256]{2,1,0:T(8,128)(2,1)} %get-tuple-element.27), calls=%async_computation | async-start | bytes 1179648 | tf_op jit(solution)/shard_map/all_to_all | solution.py:379
  10.9 18.9 %all-to-all-done.x_ref = bf16[8,144,256]{2,1,0:T(8,128)(2,1)S(1)} async-done(((bf16[8,144,256]{2,1,0:T(8,128)(2,1)}), bf16[8,144,256]{2,1,0:T(8,128)(2,1)S(1)}, u32[]{:S(2)}, u32[]{:S(2)}) %all-to-all-start) | async-done | bytes 589856 | tf_op jit(solution)/shard_map/all_to_all | solution.py:379
  29.8 2.6 %pick_x.1 = (bf16[32,128,256]{2,1,0:T(8,128)(2,1)S(1)}, f32[8,16,128]{2,1,0:T(8,128)S(1)}, f32[8,16,128]{2,1,0:T(8,128)S(1)}) custom-call(s32[1]{0:T(128)} %bitcast.z_ref, bf16[8,144,256]{2,1,0:T(8,128)(2,1)S(1)} %all-to-all-done.x_ref), custom_call_target="tpu_custom_call" | custom-call | tf_op jit(solution)/shard_map/pick_x/pallas_call | solution.py:136
  33.7 7.4 %all-to-all-start.2 = ((bf16[32,128,256]{2,1,0:T(8,128)(2,1)}), bf16[32,128,256]{2,1,0:T(8,128)(2,1)S(1)}, u32[]{:S(2)}, u32[]{:S(2)}) async-start(bf16[32,128,256]{2,1,0:T(8,128)(2,1)} %copy-done.2), calls=%async_computation.2 | async-start | bytes 4194304 | tf_op jit(solution)/shard_map/all_to_all | solution.py:379
  42.3 2.1 %collective-permute-start.4 = (bf16[128,256]{1,0:T(8,128)(2,1)S(1)}, bf16[128,256]{1,0:T(8,128)(2,1)S(1)}, u32[]{:S(2)}, u32[]{:S(2)}) collective-permute-start(bf16[128,256]{1,0:T(8,128)(2,1)S(1)} %copy-done.5), channel_id=1, source_target_pairs={{0,160},{32,192},{64,224},{96,0},{128,32},{160,64},{192,96},{224,1... | collective-permute-start | bytes 196616 | tf_op jit(solution)/shard_map/ppermute | solution.py:393
  44.4 3.7 %collective-permute-start.3 = (bf16[128,256]{1,0:T(8,128)(2,1)S(1)}, bf16[128,256]{1,0:T(8,128)(2,1)S(1)}, u32[]{:S(2)}, u32[]{:S(2)}) collective-permute-start(bf16[128,256]{1,0:T(8,128)(2,1)S(1)} %copy-done.5), channel_id=1, source_target_pairs={{0,128},{32,160},{64,192},{96,224},{128,0},{160,32},{192,64},{224,... | collective-permute-start | bytes 196616 | tf_op jit(solution)/shard_map/ppermute | solution.py:393
  48.1 2.6 %collective-permute-start.2 = (bf16[128,256]{1,0:T(8,128)(2,1)S(1)}, bf16[128,256]{1,0:T(8,128)(2,1)S(1)}, u32[]{:S(2)}, u32[]{:S(2)}) collective-permute-start(bf16[128,256]{1,0:T(8,128)(2,1)S(1)} %copy-done.5), channel_id=1, source_target_pairs={{0,96},{32,128},{64,160},{96,192},{128,224},{160,0},{192,32},{224,... | collective-permute-start | bytes 196616 | tf_op jit(solution)/shard_map/ppermute | solution.py:393
  51.6 2.4 %collective-permute-start = (bf16[128,256]{1,0:T(8,128)(2,1)S(1)}, bf16[128,256]{1,0:T(8,128)(2,1)S(1)}, u32[]{:S(2)}, u32[]{:S(2)}) collective-permute-start(bf16[128,256]{1,0:T(8,128)(2,1)S(1)} %copy-done.5), channel_id=1, source_target_pairs={{0,32},{32,64},{64,96},{96,128},{128,160},{160,192},{192,224},{224... | collective-permute-start | bytes 196616 | tf_op jit(solution)/shard_map/ppermute | solution.py:393
  54.6 4.1 %collective-permute-done.2.refs_3_ = bf16[128,256]{1,0:T(8,128)(2,1)S(1)} collective-permute-done((bf16[128,256]{1,0:T(8,128)(2,1)S(1)}, bf16[128,256]{1,0:T(8,128)(2,1)S(1)}, u32[]{:S(2)}, u32[]{:S(2)}) %collective-permute-start.2) | collective-permute-done | bytes 65568 | tf_op jit(solution)/shard_map/ppermute | solution.py:393
  59.0 2.5 %collective-permute-done.refs_1_ = bf16[128,256]{1,0:T(8,128)(2,1)S(1)} collective-permute-done((bf16[128,256]{1,0:T(8,128)(2,1)S(1)}, bf16[128,256]{1,0:T(8,128)(2,1)S(1)}, u32[]{:S(2)}, u32[]{:S(2)}) %collective-permute-start) | collective-permute-done | bytes 65568 | tf_op jit(solution)/shard_map/ppermute | solution.py:393
  61.4 1.9 pick_g.1
  63.3 3.9 %all-to-all-done.2.x_ref = bf16[32,128,256]{2,1,0:T(8,128)(2,1)S(1)} async-done(((bf16[32,128,256]{2,1,0:T(8,128)(2,1)}), bf16[32,128,256]{2,1,0:T(8,128)(2,1)S(1)}, u32[]{:S(2)}, u32[]{:S(2)}) %all-to-all-start.2) | async-done | bytes 2097184 | tf_op jit(solution)/shard_map/all_to_all | solution.py:379
  67.2 7.1 %all-to-all-start.1 = ((bf16[32,128,256]{2,1,0:T(8,128)(2,1)}), bf16[32,128,256]{2,1,0:T(8,128)(2,1)}, u32[]{:S(2)}, u32[]{:S(2)}) async-start(bf16[32,128,256]{2,1,0:T(8,128)(2,1)} %pick_g.1), calls=%async_computation.1 | async-start | bytes 4194304 | tf_op jit(solution)/shard_map/all_to_all | solution.py:379
  75.8 1.4 copy-done.8
  77.2 1.4 copy-done.10
  78.6 6.2 %forward.1 = (bf16[32,128,256]{2,1,0:T(8,128)(2,1)S(1)}, f32[512,384]{1,0:T(8,128)S(1)}, f32[512,384]{1,0:T(8,128)S(1)}, bf16[512,384]{1,0:T(8,128)(2,1)S(1)}) custom-call(bf16[32,128,256]{2,1,0:T(8,128)(2,1)S(1)} %all-to-all-done.2.x_ref, bf16[1,2048,384]{2,1,0:T(8,128)(2,1)S(1)} %copy-done.6, bf16[1,2048,384]{2,1,0:T(8,128)(2,1)S(1)} %copy-done.8, ...), custom_call_target="tpu_custom_call" | custom-call | flops 2415919104 | bytes 11534336 | tf_op jit(solution)/shard_map/forward/pallas_call | solution.py:219
  84.8 1.4 copy-done.4
  87.8 12.7 %all-to-all-done.1.g_ref = bf16[32,128,256]{2,1,0:T(8,128)(2,1)} async-done(((bf16[32,128,256]{2,1,0:T(8,128)(2,1)}), bf16[32,128,256]{2,1,0:T(8,128)(2,1)}, u32[]{:S(2)}, u32[]{:S(2)}) %all-to-all-start.1) | async-done | bytes 2097184 | tf_op jit(solution)/shard_map/all_to_all | solution.py:379
  100.5 7.1 %all-to-all-start.4 = ((bf16[32,128,256]{2,1,0:T(8,128)(2,1)}), bf16[32,128,256]{2,1,0:T(8,128)(2,1)S(1)}, u32[]{:S(2)}, u32[]{:S(2)}) async-start(bf16[32,128,256]{2,1,0:T(8,128)(2,1)} %copy-done.4), calls=%async_computation.4 | async-start | bytes 4194304 | tf_op jit(solution)/shard_map/all_to_all | solution.py:379
  107.6 1.4 copy-done.7
  109.0 1.4 copy-done.9
  110.4 1.4 copy-done.11
  112.9 8.2 %backward.1 = (bf16[32,128,256]{2,1,0:T(8,128)(2,1)S(1)}, bf16[512,384]{1,0:T(8,128)(2,1)S(1)}, bf16[512,384]{1,0:T(8,128)(2,1)S(1)}) custom-call(bf16[32,128,256]{2,1,0:T(8,128)(2,1)} %all-to-all-done.1.g_ref, f32[512,384]{1,0:T(8,128)S(1)} %get-tuple-element.32.gate_ref, f32[512,384]{1,0:T(8,128)S(1)} %copy-done.13, bf16[1,2048,384]{2,1,0:T(8,128)(2,1)S(1)} %copy-done.7, ...), custom_call_target="tpu_custom_call" | custom-call | flops 2415919104 | bytes 11534336 | tf_op jit(solution)/shard_map/backward/pallas_call | solution.py:263
  124.0 9.7 %all-to-all-done.4.refs_2_ = bf16[32,128,256]{2,1,0:T(8,128)(2,1)S(1)} async-done(((bf16[32,128,256]{2,1,0:T(8,128)(2,1)}), bf16[32,128,256]{2,1,0:T(8,128)(2,1)S(1)}, u32[]{:S(2)}, u32[]{:S(2)}) %all-to-all-start.4) | async-done | bytes 2097184 | tf_op jit(solution)/shard_map/all_to_all | solution.py:379
  133.6 7.3 %all-to-all-start.3 = ((bf16[32,128,256]{2,1,0:T(8,128)(2,1)}), bf16[32,128,256]{2,1,0:T(8,128)(2,1)}, u32[]{:S(2)}, u32[]{:S(2)}) async-start(bf16[32,128,256]{2,1,0:T(8,128)(2,1)} %copy-done.3), calls=%async_computation.3 | async-start | bytes 4194304 | tf_op jit(solution)/shard_map/all_to_all | solution.py:379
  140.9 1.6 copy-done.1
  143.5 8.1 %grads.1 = (bf16[1,2048,384]{2,1,0:T(8,128)(2,1)}, bf16[1,2048,384]{2,1,0:T(8,128)(2,1)}, bf16[1,384,2048]{2,1,0:T(8,128)(2,1)}) custom-call(bf16[32,128,256]{2,1,0:T(8,128)(2,1)S(1)} %copy-done.1, bf16[32,128,256]{2,1,0:T(8,128)(2,1)} %all-to-all-done.1.g_ref, bf16[512,384]{1,0:T(8,128)(2,1)S(1)} %copy-done.19, bf16[512,384]{1,0:T(8,128)(2,1)S(1)} %copy-done.15, ...), custom_call_target="tpu_custom_call" | custom-call | flops 2415919104 | bytes 10485760 | tf_op jit(solution)/shard_map/grads/pallas_call | solution.py:296
  151.6 2.3 %join_out.1.refs_2_ = bf16[64,32,256]{2,1,0:T(8,128)(2,1)S(1)} custom-call(f32[8,16,128]{2,1,0:T(8,128)S(1)} %get-tuple-element.28.refs_8_.refs_0_, f32[8,16,128]{2,1,0:T(8,128)S(1)} %get-tuple-element.30.refs_9_.refs_1_, bf16[32,128,256]{2,1,0:T(8,128)(2,1)S(1)} %all-to-all-done.4.refs_2_), custom_call_target="tpu_custom_call" | custom-call | tf_op jit(solution)/shard_map/join_out/pallas_call | solution.py:345
  153.9 13.1 %all-to-all-done.3.refs_1_ = bf16[32,128,256]{2,1,0:T(8,128)(2,1)} async-done(((bf16[32,128,256]{2,1,0:T(8,128)(2,1)}), bf16[32,128,256]{2,1,0:T(8,128)(2,1)}, u32[]{:S(2)}, u32[]{:S(2)}) %all-to-all-start.3) | async-done | bytes 2097184 | tf_op jit(solution)/shard_map/all_to_all | solution.py:379
  167.0 3.6 %join_in.1 = bf16[64,32,256]{2,1,0:T(8,128)(2,1)S(1)} custom-call(f32[8,16,128]{2,1,0:T(8,128)S(1)} %get-tuple-element.28.refs_8_.refs_0_, bf16[32,128,256]{2,1,0:T(8,128)(2,1)} %all-to-all-done.3.refs_1_, bf16[64,32,256]{2,1,0:T(8,128)(2,1)S(1)} %join_out.1.refs_2_), custom_call_target="tpu_custom_call", output_to_operand_aliasing={{}: (2, {})} | custom-call | tf_op jit(solution)/shard_map/join_in/pallas_call | solution.py:345
  170.6 34.6 %all_to_all.30.part_ref = bf16[64,32,256]{2,1,0:T(8,128)(2,1)S(1)} all-to-all(bf16[64,32,256]{2,1,0:T(8,128)(2,1)S(1)} %join_in.1), channel_id=1, replica_groups=mesh['z'=8,'xl'=2,'core'=2,'xh'=2,'y'=4] {'z','xh','y'}, dimensions={0} | all-to-all | bytes 2097152 | tf_op jit(solution)/shard_map/all_to_all | solution.py:379
  (42 shorter events, 13.1 us)
Async XLA Ops:
  2.4 27.4 %all-to-all-start = ((bf16[8,144,256]{2,1,0:T(8,128)(2,1)}), bf16[8,144,256]{2,1,0:T(8,128)(2,1)S(1)}, u32[]{:S(2)}, u32[]{:S(2)}) async-start(bf16[8,144,256]{2,1,0:T(8,128)(2,1)} %get-tuple-element.27), calls=%async_computation | async-start | bytes 1179648 | tf_op jit(solution)/shard_map/all_to_all | solution.py:379
  32.4 1.4 copy-start.2
  33.7 7.4 %copy-start.5 = (bf16[128,256]{1,0:T(8,128)(2,1)S(1)}, bf16[128,256]{1,0:T(8,128)(2,1)}, u32[]{:S(2)}) copy-start(bf16[128,256]{1,0:T(8,128)(2,1)} %get-tuple-element.29.refs_0_) | copy-start | bytes 196612
  33.7 33.5 %all-to-all-start.2 = ((bf16[32,128,256]{2,1,0:T(8,128)(2,1)}), bf16[32,128,256]{2,1,0:T(8,128)(2,1)S(1)}, u32[]{:S(2)}, u32[]{:S(2)}) async-start(bf16[32,128,256]{2,1,0:T(8,128)(2,1)} %copy-done.2), calls=%async_computation.2 | async-start | bytes 4194304 | tf_op jit(solution)/shard_map/all_to_all | solution.py:379
  41.1 9.5 %collective-permute-start.6 = (bf16[128,256]{1,0:T(8,128)(2,1)S(1)}, bf16[128,256]{1,0:T(8,128)(2,1)S(1)}, u32[]{:S(2)}, u32[]{:S(2)}) collective-permute-start(bf16[128,256]{1,0:T(8,128)(2,1)S(1)} %copy-done.5), channel_id=1, source_target_pairs={{0,224},{32,0},{64,32},{96,64},{128,96},{160,128},{192,160},{224,1... | collective-permute-start | bytes 196616 | tf_op jit(solution)/shard_map/ppermute | solution.py:393
  41.2 10.4 %collective-permute-start.5 = (bf16[128,256]{1,0:T(8,128)(2,1)S(1)}, bf16[128,256]{1,0:T(8,128)(2,1)S(1)}, u32[]{:S(2)}, u32[]{:S(2)}) collective-permute-start(bf16[128,256]{1,0:T(8,128)(2,1)S(1)} %copy-done.5), channel_id=1, source_target_pairs={{0,192},{32,224},{64,0},{96,32},{128,64},{160,96},{192,128},{224,1... | collective-permute-start | bytes 196616 | tf_op jit(solution)/shard_map/ppermute | solution.py:393
  42.3 12.4 %collective-permute-start.4 = (bf16[128,256]{1,0:T(8,128)(2,1)S(1)}, bf16[128,256]{1,0:T(8,128)(2,1)S(1)}, u32[]{:S(2)}, u32[]{:S(2)}) collective-permute-start(bf16[128,256]{1,0:T(8,128)(2,1)S(1)} %copy-done.5), channel_id=1, source_target_pairs={{0,160},{32,192},{64,224},{96,0},{128,32},{160,64},{192,96},{224,1... | collective-permute-start | bytes 196616 | tf_op jit(solution)/shard_map/ppermute | solution.py:393
  44.4 10.2 %collective-permute-start.3 = (bf16[128,256]{1,0:T(8,128)(2,1)S(1)}, bf16[128,256]{1,0:T(8,128)(2,1)S(1)}, u32[]{:S(2)}, u32[]{:S(2)}) collective-permute-start(bf16[128,256]{1,0:T(8,128)(2,1)S(1)} %copy-done.5), channel_id=1, source_target_pairs={{0,128},{32,160},{64,192},{96,224},{128,0},{160,32},{192,64},{224,... | collective-permute-start | bytes 196616 | tf_op jit(solution)/shard_map/ppermute | solution.py:393
  48.1 10.7 %collective-permute-start.2 = (bf16[128,256]{1,0:T(8,128)(2,1)S(1)}, bf16[128,256]{1,0:T(8,128)(2,1)S(1)}, u32[]{:S(2)}, u32[]{:S(2)}) collective-permute-start(bf16[128,256]{1,0:T(8,128)(2,1)S(1)} %copy-done.5), channel_id=1, source_target_pairs={{0,96},{32,128},{64,160},{96,192},{128,224},{160,0},{192,32},{224,... | collective-permute-start | bytes 196616 | tf_op jit(solution)/shard_map/ppermute | solution.py:393
  50.6 8.3 %collective-permute-start.1 = (bf16[128,256]{1,0:T(8,128)(2,1)S(1)}, bf16[128,256]{1,0:T(8,128)(2,1)S(1)}, u32[]{:S(2)}, u32[]{:S(2)}) collective-permute-start(bf16[128,256]{1,0:T(8,128)(2,1)S(1)} %copy-done.5), channel_id=1, source_target_pairs={{0,64},{32,96},{64,128},{96,160},{128,192},{160,224},{192,0},{224,... | collective-permute-start | bytes 196616 | tf_op jit(solution)/shard_map/ppermute | solution.py:393
  51.6 9.8 %collective-permute-start = (bf16[128,256]{1,0:T(8,128)(2,1)S(1)}, bf16[128,256]{1,0:T(8,128)(2,1)S(1)}, u32[]{:S(2)}, u32[]{:S(2)}) collective-permute-start(bf16[128,256]{1,0:T(8,128)(2,1)S(1)} %copy-done.5), channel_id=1, source_target_pairs={{0,32},{32,64},{64,96},{96,128},{128,160},{160,192},{192,224},{224... | collective-permute-start | bytes 196616 | tf_op jit(solution)/shard_map/ppermute | solution.py:393
  67.2 17.5 %copy-start = (bf16[32,128,256]{2,1,0:T(8,128)(2,1)}, bf16[32,128,256]{2,1,0:T(8,128)(2,1)S(1)}, u32[]{:S(2)}) copy-start(bf16[32,128,256]{2,1,0:T(8,128)(2,1)S(1)} %all-to-all-done.2.x_ref) | copy-start | bytes 6291460
  67.2 33.3 %all-to-all-start.1 = ((bf16[32,128,256]{2,1,0:T(8,128)(2,1)}), bf16[32,128,256]{2,1,0:T(8,128)(2,1)}, u32[]{:S(2)}, u32[]{:S(2)}) async-start(bf16[32,128,256]{2,1,0:T(8,128)(2,1)} %pick_g.1), calls=%async_computation.1 | async-start | bytes 4194304 | tf_op jit(solution)/shard_map/all_to_all | solution.py:379
  74.4 1.4 copy-start.6
  75.8 1.4 copy-start.8
  77.2 1.4 copy-start.10
  84.8 1.4 copy-start.4
  86.2 0.9 copy-start.12
  87.0 0.7 copy-start.18
  100.5 33.2 %all-to-all-start.4 = ((bf16[32,128,256]{2,1,0:T(8,128)(2,1)}), bf16[32,128,256]{2,1,0:T(8,128)(2,1)S(1)}, u32[]{:S(2)}, u32[]{:S(2)}) async-start(bf16[32,128,256]{2,1,0:T(8,128)(2,1)} %copy-done.4), calls=%async_computation.4 | async-start | bytes 4194304 | tf_op jit(solution)/shard_map/all_to_all | solution.py:379
  107.6 1.4 copy-start.7
  109.0 1.4 copy-start.9
  110.4 1.4 copy-start.11
  111.8 1.1 copy-start.13
  121.1 1.4 copy-start.3
  122.5 0.7 copy-start.14
  123.2 0.7 copy-start.16
  133.6 7.3 %copy-start.15 = (bf16[512,384]{1,0:T(8,128)(2,1)S(1)}, bf16[512,384]{1,0:T(8,128)(2,1)}, u32[]{:S(2)}) copy-start(bf16[512,384]{1,0:T(8,128)(2,1)} %copy-done.14) | copy-start | bytes 1179652
  133.6 7.3 %copy-start.17 = (bf16[512,384]{1,0:T(8,128)(2,1)S(1)}, bf16[512,384]{1,0:T(8,128)(2,1)}, u32[]{:S(2)}) copy-start(bf16[512,384]{1,0:T(8,128)(2,1)} %copy-done.16) | copy-start | bytes 1179652
  133.6 33.4 %all-to-all-start.3 = ((bf16[32,128,256]{2,1,0:T(8,128)(2,1)}), bf16[32,128,256]{2,1,0:T(8,128)(2,1)}, u32[]{:S(2)}, u32[]{:S(2)}) async-start(bf16[32,128,256]{2,1,0:T(8,128)(2,1)} %copy-done.3), calls=%async_computation.3 | async-start | bytes 4194304 | tf_op jit(solution)/shard_map/all_to_all | solution.py:379
  140.9 1.6 copy-start.1
  142.5 1.0 copy-start.19

commit v3 on v2

--- a/solution.py
+++ b/solution.py
@@ -1,5 +1,3 @@
-import functools
-
 import jax
 import jax.numpy as jnp
 from jax import lax
@@ -107,27 +105,28 @@
 
 def pick_x_kernel(z_ref, x_ref, send_ref, place_ref, weight_ref):
     ntok = x_ref.shape[1] - META
-    left = x_ref[0, ntok : ntok + META, 0:128].astype(F32)
-    right = x_ref[0, ntok : ntok + META, 128:256].astype(F32)
-    slots = left[0:8]
-    w = right[0:8] + left[8:16] + right[8:16]
     first = (z_ref[0] * 16).astype(F32)
     local = lax.broadcasted_iota(jnp.int32, (16, ntok), 0).astype(F32) + first
-    chosen = jnp.zeros((16, ntok), F32)
-    weight = jnp.zeros((16, ntok), F32)
-    for k in range(8):
-        same = local == slots[k : k + 1, :]
-        chosen = jnp.where(same, 1.0, chosen)
-        weight = jnp.where(same, w[k : k + 1, :], weight)
     row = lax.broadcasted_iota(jnp.int32, (ntok, ntok), 0)
     column = lax.broadcasted_iota(jnp.int32, (ntok, ntok), 1)
     earlier = jnp.where(row < column, 1.0, 0.0).astype(BF16)
-    before = nn(chosen.astype(BF16), earlier)
-    place = jnp.where(chosen > 0.0, before, -1.0)
-    place_ref[0] = place
-    weight_ref[0] = weight
-    rows = nn(as_bf16(one_hot(place)), x_ref[0, 0:ntok, :])
-    put_rows(rows.astype(BF16), send_ref)
+    for b in range(x_ref.shape[0]):
+        left = x_ref[b, ntok : ntok + META, 0:128].astype(F32)
+        right = x_ref[b, ntok : ntok + META, 128:256].astype(F32)
+        slots = left[0:8]
+        w = right[0:8] + left[8:16] + right[8:16]
+        chosen = jnp.zeros((16, ntok), F32)
+        weight = jnp.zeros((16, ntok), F32)
+        for k in range(8):
+            same = local == slots[k : k + 1, :]
+            chosen = jnp.where(same, 1.0, chosen)
+            weight = jnp.where(same, w[k : k + 1, :], weight)
+        before = nn(chosen.astype(BF16), earlier)
+        place = jnp.where(chosen > 0.0, before, -1.0)
+        place_ref[b] = place
+        weight_ref[b] = weight
+        rows = nn(as_bf16(one_hot(place)), x_ref[b, 0:ntok, :])
+        put_rows(rows.astype(BF16), send_ref.at[:, b * CAP : (b + 1) * CAP, :])
 
 
 def pick_x(zs, x_all):
@@ -137,16 +136,16 @@
         pick_x_kernel,
         grid_spec=pltpu.PrefetchScalarGridSpec(
             num_scalar_prefetch=1,
-            grid=(blocks,),
-            in_specs=[pl.BlockSpec((1, rows, cut), lambda b, z: (b, 0, 0))],
+            grid=(1,),
+            in_specs=[whole(x_all.shape)],
             out_specs=[
-                pl.BlockSpec((32, CAP, cut), lambda b, z: (0, b, 0)),
-                pl.BlockSpec((1, 16, ntok), lambda b, z: (b, 0, 0)),
-                pl.BlockSpec((1, 16, ntok), lambda b, z: (b, 0, 0)),
+                whole((32, blocks * CAP, cut)),
+                whole((blocks, 16, ntok)),
+                whole((blocks, 16, ntok)),
             ],
         ),
         out_shape=[
-            jax.ShapeDtypeStruct((32, blocks * CAP, cut), BF16),
+            pltpu.HBM((32, blocks * CAP, cut), BF16),
             jax.ShapeDtypeStruct((blocks, 16, ntok), F32),
             jax.ShapeDtypeStruct((blocks, 16, ntok), F32),
         ],
@@ -308,7 +307,7 @@
     )(x_rows, g_rows, hidden, dgate, dup)
 
 
-def add_rows(place, scale, back, like):
+def add_rows(place, scale, back):
     hot = one_hot(place)
     rows = jnp.concatenate(
         [back[2 * l].astype(F32) + back[2 * l + 1].astype(F32) for l in range(16)], axis=0
@@ -318,65 +317,118 @@
     hi = rows.astype(BF16)
     low = (rows - hi.astype(F32)).astype(BF16)
     pick = as_bf16(hot)
-    return (tn(pick, hi) + tn(pick, low)).astype(BF16).reshape(like)
-
-
-def join_kernel(weighted, *refs):
-    place_ref, back_ref, sum_ref = refs[0], refs[2 if weighted else 1], refs[-1]
-    blocks = place_ref.shape[0]
-    eighth, part, cut = sum_ref.shape[0] // blocks, sum_ref.shape[1], sum_ref.shape[2]
-
-    def step(b, _):
-        rows = pl.ds(pl.multiple_of(b * CAP, CAP), CAP)
-        scale = refs[1][b] if weighted else None
-        total = add_rows(place_ref[b], scale, back_ref.at[:, rows, :], (eighth, part, cut))
-        sum_ref[pl.ds(b * eighth, eighth)] = total
-        return 0
-
-    lax.fori_loop(0, blocks, step, 0)
-
-
-def join(per_block, back, half, buffer, name):
-    blocks, _, ntok = per_block[0].shape
-    cut = back.shape[2]
-    part = ntok // 8
-    given = [] if buffer is None else [buffer]
-    count = len(per_block) + 1
-    return pl.pallas_call(
-        functools.partial(join_kernel, len(per_block) == 2),
-        grid=(1,),
-        in_specs=[whole(a.shape) for a in per_block]
-        + [whole(back.shape)]
-        + [pl.BlockSpec(memory_space=pl.ANY) for _ in given],
-        out_specs=pl.BlockSpec((8 * blocks, part, cut), lambda i: (0, half, 0)),
-        out_shape=jax.ShapeDtypeStruct((8 * blocks, 2 * part, cut), BF16),
-        input_output_aliases={count: 0} if given else {},
-        compiler_params=params(),
-        name=name,
-    )(*per_block, back, *given)
-
-
-def last_kernel(part_ref, out_ref, in_ref):
+    return tn(pick, hi) + tn(pick, low)
+
+
+def join_out_kernel(z_ref, place_ref, weight_ref, back_ref, own_ref, *sum_refs):
+    for shift, sum_ref in enumerate((own_ref, *sum_refs)):
+        block = lax.rem(z_ref[0] + shift, 8)
+        rows = back_ref.at[:, pl.ds(pl.multiple_of(block * CAP, CAP), CAP), :]
+        sum_ref[...] = add_rows(place_ref[block], weight_ref[block], rows).astype(sum_ref.dtype)
+
+
+def join_out(zs, place, weight, back):
+    ntok, cut = place.shape[2], back.shape[2]
+    shapes = [jax.ShapeDtypeStruct((ntok, cut), F32 if s == 0 else BF16) for s in range(8)]
+    return pl.pallas_call(
+        join_out_kernel,
+        grid_spec=pltpu.PrefetchScalarGridSpec(
+            num_scalar_prefetch=1,
+            grid=(1,),
+            in_specs=[whole(place.shape), whole(weight.shape), whole(back.shape)],
+            out_specs=[whole((ntok, cut))] * 8,
+        ),
+        out_shape=shapes,
+        compiler_params=params(),
+        name="join_out",
+    )(zs, place, weight, back)
+
+
+def join_in_kernel(place_ref, back_ref, sum_ref):
+    eighth = sum_ref.shape[0] // place_ref.shape[0]
+    for b in range(place_ref.shape[0]):
+        total = add_rows(place_ref[b], None, back_ref.at[:, b * CAP : (b + 1) * CAP, :])
+        sum_ref[b * eighth : (b + 1) * eighth] = total.astype(BF16).reshape(eighth, *sum_ref.shape[1:])
+
+
+def join_in(place, back):
+    blocks, _, ntok = place.shape
+    return pl.pallas_call(
+        join_in_kernel,
+        out_shape=jax.ShapeDtypeStruct((blocks * 8, ntok // 8, back.shape[2]), BF16),
+        compiler_params=params(),
+        name="join_in",
+    )(place, back)
+
+
+def total_kernel(col_ref, *refs):
+    parts, pieces, total_ref = refs[:8], refs[8:16], refs[16]
+    total = parts[0][...]
+    for part in parts[1:]:
+        total = total + part[...].astype(F32)
+    total_ref[...] = total
+    count = pieces[0].shape[0]
+    for shift, piece in enumerate(pieces):
+        to = lax.rem(col_ref[0] + shift, 8)
+        piece[...] = total_ref[pl.ds(pl.multiple_of(to * count, count), count), :].astype(BF16)
+
+
+def total(col, parts):
+    ntok, cut = parts[0].shape
+    return pl.pallas_call(
+        total_kernel,
+        grid_spec=pltpu.PrefetchScalarGridSpec(
+            num_scalar_prefetch=1,
+            grid=(1,),
+            in_specs=[whole((ntok, cut))] * 8,
+            out_specs=[whole((ntok // 8, cut))] * 8,
+            scratch_shapes=[pltpu.VMEM((ntok, cut), F32)],
+        ),
+        out_shape=[jax.ShapeDtypeStruct((ntok // 8, cut), BF16)] * 8,
+        compiler_params=params(),
+        name="total",
+    )(col, *parts)
+
+
+def last_kernel(col_ref, *refs):
+    pieces, part_ref, out_ref, in_ref = refs[:8], refs[8], refs[9], refs[10]
     cut = part_ref.shape[2]
+    for shift, piece in enumerate(pieces):
+        at = lax.rem(col_ref[0] + 8 - shift, 8) * cut
+        out_ref[:, pl.ds(pl.multiple_of(at, cut), cut)] = piece[...]
     for e in range(8):
-        total = part_ref[e].astype(F32)
+        whole_sum = part_ref[e].astype(F32)
         for z in range(1, 8):
-            total = total + part_ref[z * 8 + e].astype(F32)
-        half = total.shape[0] // 2
-        out_ref[:, e * cut : (e + 1) * cut] = total[:half].astype(BF16)
-        in_ref[:, e * cut : (e + 1) * cut] = total[half:].astype(BF16)
-
-
-def last(parts):
-    _, two, cut = parts.shape
-    shape = jax.ShapeDtypeStruct((two // 2, 8 * cut), BF16)
-    return pl.pallas_call(
-        last_kernel, out_shape=[shape, shape], compiler_params=params(), name="last"
-    )(parts)
+            whole_sum = whole_sum + part_ref[z * 8 + e].astype(F32)
+        in_ref[:, e * cut : (e + 1) * cut] = whole_sum.astype(BF16)
+
+
+def last(col, pieces, parts):
+    _, count, cut = parts.shape
+    shape = jax.ShapeDtypeStruct((count, 8 * cut), BF16)
+    return pl.pallas_call(
+        last_kernel,
+        grid_spec=pltpu.PrefetchScalarGridSpec(
+            num_scalar_prefetch=1,
+            grid=(1,),
+            in_specs=[whole((count, cut))] * 8 + [whole(parts.shape)],
+            out_specs=[whole(shape.shape)] * 2,
+        ),
+        out_shape=[shape, shape],
+        compiler_params=params(),
+        name="last",
+    )(col, *pieces, parts)
 
 
 def swap(buffer, axes):
     return lax.all_to_all(buffer, axes, split_axis=0, concat_axis=0, tiled=True)
+
+
+def spread(arrays, axes):
+    return [arrays[0]] + [
+        lax.ppermute(arrays[shift], axes, [(i, (i + shift) % 8) for i in range(8)])
+        for shift in range(1, 8)
+    ]
 
 
 def on_device(
@@ -389,21 +441,22 @@
     )
     x_all = swap(x_cut, ("z",))
     x_send, place, weight = pick_x(zs, x_all)
-    g_blocks = [g_cut] + [
-        lax.ppermute(g_cut, "z", [(z, (z + shift) % 8) for z in range(8)]) for shift in range(1, 8)
-    ]
+    g_blocks = spread([g_cut] * 8, ("z",))
     x_rows = swap(x_send, PLANE)
     g_send = pick_g(zs, g_blocks, place, weight)
     g_rows = swap(g_send, PLANE)
     out_send, gate, up, hidden = forward(x_rows, gate_weight, up_weight, down_weight)
-    out_back = swap(out_send, PLANE)
+    out_back = pltpu.with_memory_space_constraint(swap(out_send, PLANE), pltpu.HBM)
     in_send, dgate, dup = backward(g_rows, gate, up, gate_weight, up_weight, down_weight)
+    weight_grads = grads(x_rows, g_rows, hidden, dgate, dup)
+    in_send, weight_grads = lax.optimization_barrier((in_send, weight_grads))
     in_back = swap(in_send, PLANE)
-    weight_grads = grads(x_rows, g_rows, hidden, dgate, dup)
-    both = join((place, weight), out_back, 0, None, "join_out")
-    in_back, both, weight_grads = lax.optimization_barrier((in_back, both, weight_grads))
-    both = join((place,), in_back, 1, both, "join_in")
-    layer_out, input_grad = last(swap(both, ("z", "xh", "y")))
+    y_parts = spread(join_out(zs, place, weight, out_back), ("z",))
+    pieces = total(col, y_parts)
+    in_back, pieces = lax.optimization_barrier((in_back, pieces))
+    dx_part = join_in(place, in_back)
+    pieces = spread(pieces, EX)
+    layer_out, input_grad = last(col, pieces, swap(dx_part, ("z", "xh", "y")))
     return layer_out, input_grad, *weight_grads
 
 

time: 208 us -> 195 us (0.938)
  blocking collectives: 34.6 us -> 0 us
  starting transfers between devices: 50.2 us -> 79.9 us
  local copies, waits for them, and re-layouts: 19.4 us -> 13.1 us
    all_to_all x1 -> x0, blocking collectives: 34.6 us -> none  [swap(): return lax.all_to_all(buffer, axes, split_axis=0, concat_axis=0, tiled=True)]
    ppermute x7 -> x21, starting transfers between devices: 12.9 us -> 35.1 us  [spread(): lax.ppermute(arrays[shift], axes, [(i, (i + shift) % 8) for i in range(8)])]
    all_to_all x5 -> x6, waiting for transfers between devices: 58.2 us -> 40.2 us  [swap(): return lax.all_to_all(buffer, axes, split_axis=0, concat_axis=0, tiled=True)]
    ppermute x7 -> x21, waiting for transfers between devices: 7.42 us -> 24.3 us  [spread(): lax.ppermute(arrays[shift], axes, [(i, (i + shift) % 8) for i in range(8)])]
    all_to_all x5 -> x6, starting transfers between devices: 37.3 us -> 44.7 us  [swap(): return lax.all_to_all(buffer, axes, split_axis=0, concat_axis=0, tiled=True)]
    unnamed x40 -> x22, local copies, waits for them, and re-layouts: 19.4 us -> 13.1 us
    pallas_call x3 -> x4, Pallas kernels: 6.65 us -> 5.07 us  [the longest x1 2.63 us: join_out(): pl.pallas_call(join_out_kernel, grid_spec=pltpu.PrefetchScalarGridSpec(nu...]
  transfers between devices with their start and end apart: 12 -> 27, of which waited for: 9 -> 16; matrix products, arithmetic and copies ran while one was open for 0% -> 0% of each run, Pallas kernels for 13% -> 15%
where the time goes in v3:
time: 195 us; the launch traced here: 194 us
  starting transfers between devices  79.9 us (41%)
  waiting for transfers between devices  64.5 us (33%)
  Pallas kernels  35.7 us (18%)
  local copies, waits for them, and re-layouts  13.1 us (7%)
    all_to_all x6, starting transfers between devices, swap(): return lax.all_to_all(buffer, axes, split_axis=0, concat_axis=0, tiled=True)  44.7 us
    all_to_all x6, waiting for transfers between devices, swap(): return lax.all_to_all(buffer, axes, split_axis=0, concat_axis=0, tiled=True)  40.2 us
    ppermute x21, starting transfers between devices, spread(): lax.ppermute(arrays[shift], axes, [(i, (i + shift) % 8) for i in range(8)])  35.1 us
    ppermute x21, waiting for transfers between devices, spread(): lax.ppermute(arrays[shift], axes, [(i, (i + shift) % 8) for i in range(8)])  24.3 us
    unnamed x22, local copies, waits for them, and re-layouts  13.1 us
    pallas_call x1, Pallas kernels, grads(): pl.pallas_call(grads_kernel, out_shape=[jax.ShapeDtypeStruct((1, width, f...  8.74 us
    pallas_call x1, Pallas kernels, backward(): pl.pallas_call(backward_kernel, out_shape=[jax.ShapeDtypeStruct(g_rows.sh...  8.18 us
    pallas_call x1, Pallas kernels, forward(): pl.pallas_call(forward_kernel, out_shape=[jax.ShapeDtypeStruct(x_rows.sha...  7.75 us
  transfers between devices with their start and end apart: 27, of which 16 were waited for; matrix products, arithmetic and copies ran while one was open for 0% of the time, Pallas kernels for 15%

profile of v3, /device:TPU:28, one launch (start us, length us, event | category | flops | bytes accessed | tf_op | source)
XLA Modules:
  0.0 194.0 jit_solution(16335196767324397367)
XLA Ops:
  2.4 8.5 %all-to-all-start = ((bf16[8,144,256]{2,1,0:T(8,128)(2,1)}), bf16[8,144,256]{2,1,0:T(8,128)(2,1)S(1)}, u32[]{:S(2)}, u32[]{:S(2)}) async-start(bf16[8,144,256]{2,1,0:T(8,128)(2,1)} %get-tuple-element.52), calls=%async_computation | async-start | bytes 1179648 | tf_op jit(solution)/shard_map/all_to_all | solution.py:424
  10.9 18.9 %all-to-all-done.x_ref = bf16[8,144,256]{2,1,0:T(8,128)(2,1)S(1)} async-done(((bf16[8,144,256]{2,1,0:T(8,128)(2,1)}), bf16[8,144,256]{2,1,0:T(8,128)(2,1)S(1)}, u32[]{:S(2)}, u32[]{:S(2)}) %all-to-all-start) | async-done | bytes 589856 | tf_op jit(solution)/shard_map/all_to_all | solution.py:424
  29.8 2.3 %pick_x.1 = (bf16[32,128,256]{2,1,0:T(8,128)(2,1)}, f32[8,16,128]{2,1,0:T(8,128)S(1)}, f32[8,16,128]{2,1,0:T(8,128)S(1)}) custom-call(s32[1]{0:T(128)} %bitcast.1.z_ref, bf16[8,144,256]{2,1,0:T(8,128)(2,1)S(1)} %all-to-all-done.x_ref), custom_call_target="tpu_custom_call" | custom-call | tf_op jit(solution)/shard_map/pick_x/pallas_call | solution.py:135
  32.1 7.4 %all-to-all-start.2 = ((bf16[32,128,256]{2,1,0:T(8,128)(2,1)}), bf16[32,128,256]{2,1,0:T(8,128)(2,1)}, u32[]{:S(2)}, u32[]{:S(2)}) async-start(bf16[32,128,256]{2,1,0:T(8,128)(2,1)} %get-tuple-element.55), calls=%async_computation.2 | async-start | bytes 4194304 | tf_op jit(solution)/shard_map/all_to_all | solution.py:424
  40.7 2.1 %collective-permute-start.4 = (bf16[128,256]{1,0:T(8,128)(2,1)S(1)}, bf16[128,256]{1,0:T(8,128)(2,1)S(1)}, u32[]{:S(2)}, u32[]{:S(2)}) collective-permute-start(bf16[128,256]{1,0:T(8,128)(2,1)S(1)} %copy-done.2), channel_id=1, source_target_pairs={{0,160},{32,192},{64,224},{96,0},{128,32},{160,64},{192,96},{224,1... | collective-permute-start | bytes 196616 | tf_op jit(solution)/shard_map/ppermute | solution.py:429
  42.8 3.7 %collective-permute-start.3 = (bf16[128,256]{1,0:T(8,128)(2,1)S(1)}, bf16[128,256]{1,0:T(8,128)(2,1)S(1)}, u32[]{:S(2)}, u32[]{:S(2)}) collective-permute-start(bf16[128,256]{1,0:T(8,128)(2,1)S(1)} %copy-done.2), channel_id=1, source_target_pairs={{0,128},{32,160},{64,192},{96,224},{128,0},{160,32},{192,64},{224,... | collective-permute-start | bytes 196616 | tf_op jit(solution)/shard_map/ppermute | solution.py:429
  46.5 2.6 %collective-permute-start.2 = (bf16[128,256]{1,0:T(8,128)(2,1)S(1)}, bf16[128,256]{1,0:T(8,128)(2,1)S(1)}, u32[]{:S(2)}, u32[]{:S(2)}) collective-permute-start(bf16[128,256]{1,0:T(8,128)(2,1)S(1)} %copy-done.2), channel_id=1, source_target_pairs={{0,96},{32,128},{64,160},{96,192},{128,224},{160,0},{192,32},{224,... | collective-permute-start | bytes 196616 | tf_op jit(solution)/shard_map/ppermute | solution.py:429
  53.0 4.1 %collective-permute-done.2.refs_3_ = bf16[128,256]{1,0:T(8,128)(2,1)S(1)} collective-permute-done((bf16[128,256]{1,0:T(8,128)(2,1)S(1)}, bf16[128,256]{1,0:T(8,128)(2,1)S(1)}, u32[]{:S(2)}, u32[]{:S(2)}) %collective-permute-start.2) | collective-permute-done | bytes 65568 | tf_op jit(solution)/shard_map/ppermute | solution.py:429
  57.4 2.4 %collective-permute-done.refs_1_ = bf16[128,256]{1,0:T(8,128)(2,1)S(1)} collective-permute-done((bf16[128,256]{1,0:T(8,128)(2,1)S(1)}, bf16[128,256]{1,0:T(8,128)(2,1)S(1)}, u32[]{:S(2)}, u32[]{:S(2)}) %collective-permute-start) | collective-permute-done | bytes 65568 | tf_op jit(solution)/shard_map/ppermute | solution.py:429
  61.7 3.9 %all-to-all-done.2.x_ref = bf16[32,128,256]{2,1,0:T(8,128)(2,1)} async-done(((bf16[32,128,256]{2,1,0:T(8,128)(2,1)}), bf16[32,128,256]{2,1,0:T(8,128)(2,1)}, u32[]{:S(2)}, u32[]{:S(2)}) %all-to-all-start.2) | async-done | bytes 2097184 | tf_op jit(solution)/shard_map/all_to_all | solution.py:424
  65.7 7.1 %all-to-all-start.1 = ((bf16[32,128,256]{2,1,0:T(8,128)(2,1)}), bf16[32,128,256]{2,1,0:T(8,128)(2,1)}, u32[]{:S(2)}, u32[]{:S(2)}) async-start(bf16[32,128,256]{2,1,0:T(8,128)(2,1)} %pick_g.1), calls=%async_computation.1 | async-start | bytes 4194304 | tf_op jit(solution)/shard_map/all_to_all | solution.py:424
  77.0 7.8 %forward.1 = (bf16[32,128,256]{2,1,0:T(8,128)(2,1)S(1)}, f32[512,384]{1,0:T(8,128)S(1)}, f32[512,384]{1,0:T(8,128)S(1)}, bf16[512,384]{1,0:T(8,128)(2,1)S(1)}) custom-call(bf16[32,128,256]{2,1,0:T(8,128)(2,1)} %all-to-all-done.2.x_ref, bf16[1,2048,384]{2,1,0:T(8,128)(2,1)S(1)} %copy-done.3, bf16[1,2048,384]{2,1,0:T(8,128)(2,1)S(1)} %copy-done.5, ...), custom_call_target="tpu_custom_call" | custom-call | flops 2415919104 | bytes 11534336 | tf_op jit(solution)/shard_map/forward/pallas_call | solution.py:218
  87.0 11.9 %all-to-all-done.1.g_ref = bf16[32,128,256]{2,1,0:T(8,128)(2,1)} async-done(((bf16[32,128,256]{2,1,0:T(8,128)(2,1)}), bf16[32,128,256]{2,1,0:T(8,128)(2,1)}, u32[]{:S(2)}, u32[]{:S(2)}) %all-to-all-start.1) | async-done | bytes 2097184 | tf_op jit(solution)/shard_map/all_to_all | solution.py:424
  98.9 7.1 %all-to-all-start.4 = ((bf16[32,128,256]{2,1,0:T(8,128)(2,1)}), bf16[32,128,256]{2,1,0:T(8,128)(2,1)}, u32[]{:S(2)}, u32[]{:S(2)}) async-start(bf16[32,128,256]{2,1,0:T(8,128)(2,1)} %copy-done.1), calls=%async_computation.4 | async-start | bytes 4194304 | tf_op jit(solution)/shard_map/all_to_all | solution.py:424
  111.4 8.2 %backward.1 = (bf16[32,128,256]{2,1,0:T(8,128)(2,1)S(1)}, bf16[512,384]{1,0:T(8,128)(2,1)S(1)}, bf16[512,384]{1,0:T(8,128)(2,1)S(1)}) custom-call(bf16[32,128,256]{2,1,0:T(8,128)(2,1)} %all-to-all-done.1.g_ref, f32[512,384]{1,0:T(8,128)S(1)} %get-tuple-element.56.gate_ref, f32[512,384]{1,0:T(8,128)S(1)} %copy-done.10, bf16[1,2048,384]{2,1,0:T(8,128)(2,1)S(1)} %copy-done.4, ...), custom_call_target="tpu_custom_call" | custom-call | flops 2415919104 | bytes 11534336 | tf_op jit(solution)/shard_map/backward/pallas_call | solution.py:262
  120.9 8.7 %grads.1 = (bf16[1,2048,384]{2,1,0:T(8,128)(2,1)}, bf16[1,2048,384]{2,1,0:T(8,128)(2,1)}, bf16[1,384,2048]{2,1,0:T(8,128)(2,1)}) custom-call(bf16[32,128,256]{2,1,0:T(8,128)(2,1)} %all-to-all-done.2.x_ref, bf16[32,128,256]{2,1,0:T(8,128)(2,1)} %all-to-all-done.1.g_ref, bf16[512,384]{1,0:T(8,128)(2,1)S(1)} %get-tuple-element.59.hidden_ref, ...), custom_call_target="tpu_custom_call" | custom-call | flops 2415919104 | bytes 10485760 | tf_op jit(solution)/shard_map/grads/pallas_call | solution.py:295
  129.7 2.5 %all-to-all-done.4.back_ref = bf16[32,128,256]{2,1,0:T(8,128)(2,1)} async-done(((bf16[32,128,256]{2,1,0:T(8,128)(2,1)}), bf16[32,128,256]{2,1,0:T(8,128)(2,1)}, u32[]{:S(2)}, u32[]{:S(2)}) %all-to-all-start.4) | async-done | bytes 2097184 | tf_op jit(solution)/shard_map/all_to_all | solution.py:424
  132.2 7.1 %all-to-all-start.3 = ((bf16[32,128,256]{2,1,0:T(8,128)(2,1)}), bf16[32,128,256]{2,1,0:T(8,128)(2,1)S(1)}, u32[]{:S(2)}, u32[]{:S(2)}) async-start(bf16[32,128,256]{2,1,0:T(8,128)(2,1)} %copy-done), calls=%async_computation.3 | async-start | bytes 4194304 | tf_op jit(solution)/shard_map/all_to_all | solution.py:424
  139.3 2.6 %join_out.1 = (f32[128,256]{1,0:T(8,128)S(1)}, bf16[128,256]{1,0:T(8,128)(2,1)S(1)}, bf16[128,256]{1,0:T(8,128)(2,1)S(1)}, bf16[128,256]{1,0:T(8,128)(2,1)S(1)},...) custom-call(s32[1]{0:T(128)} %bitcast.1.z_ref, ...), custom_call_target="tpu_custom_call" | custom-call | tf_op jit(solution)/shard_map/join_out/pallas_call | solution.py:333
  142.8 2.7 %collective-permute-start.9 = (bf16[128,256]{1,0:T(8,128)(2,1)S(1)}, bf16[128,256]{1,0:T(8,128)(2,1)S(1)}, u32[]{:S(2)}, u32[]{:S(2)}) collective-permute-start(bf16[128,256]{1,0:T(8,128)(2,1)S(1)} %get-tuple-element.70), channel_id=1, source_target_pairs={{0,96},{32,128},{64,160},{96,192},{128,224},{160,0},{192,32},{224,... | collective-permute-start | bytes 196616 | tf_op jit(solution)/shard_map/ppermute | solution.py:429
  145.4 3.3 %collective-permute-start.10 = (bf16[128,256]{1,0:T(8,128)(2,1)S(1)}, bf16[128,256]{1,0:T(8,128)(2,1)S(1)}, u32[]{:S(2)}, u32[]{:S(2)}) collective-permute-start(bf16[128,256]{1,0:T(8,128)(2,1)S(1)} %get-tuple-element.71), channel_id=1, source_target_pairs={{0,128},{32,160},{64,192},{96,224},{128,0},{160,32},{192,64},{224,... | collective-permute-start | bytes 196616 | tf_op jit(solution)/shard_map/ppermute | solution.py:429
  150.0 3.3 %collective-permute-start.12 = (bf16[128,256]{1,0:T(8,128)(2,1)S(1)}, bf16[128,256]{1,0:T(8,128)(2,1)S(1)}, u32[]{:S(2)}, u32[]{:S(2)}) collective-permute-start(bf16[128,256]{1,0:T(8,128)(2,1)S(1)} %get-tuple-element.73), channel_id=1, source_target_pairs={{0,192},{32,224},{64,0},{96,32},{128,64},{160,96},{192,128},{224,1... | collective-permute-start | bytes 196616 | tf_op jit(solution)/shard_map/ppermute | solution.py:429
  155.4 2.7 %collective-permute-done.11.refs_5_ = bf16[128,256]{1,0:T(8,128)(2,1)S(1)} collective-permute-done((bf16[128,256]{1,0:T(8,128)(2,1)S(1)}, bf16[128,256]{1,0:T(8,128)(2,1)S(1)}, u32[]{:S(2)}, u32[]{:S(2)}) %collective-permute-start.11) | collective-permute-done | bytes 65568 | tf_op jit(solution)/shard_map/ppermute | solution.py:429
  158.1 3.2 %collective-permute-done.12.refs_6_ = bf16[128,256]{1,0:T(8,128)(2,1)S(1)} collective-permute-done((bf16[128,256]{1,0:T(8,128)(2,1)S(1)}, bf16[128,256]{1,0:T(8,128)(2,1)S(1)}, u32[]{:S(2)}, u32[]{:S(2)}) %collective-permute-start.12) | collective-permute-done | bytes 65568 | tf_op jit(solution)/shard_map/ppermute | solution.py:429
  162.3 3.0 %all-to-all-done.3.back_ref = bf16[32,128,256]{2,1,0:T(8,128)(2,1)S(1)} async-done(((bf16[32,128,256]{2,1,0:T(8,128)(2,1)}), bf16[32,128,256]{2,1,0:T(8,128)(2,1)S(1)}, u32[]{:S(2)}, u32[]{:S(2)}) %all-to-all-start.3) | async-done | bytes 2097184 | tf_op jit(solution)/shard_map/all_to_all | solution.py:424
  167.0 7.5 %all-to-all-start.5 = ((bf16[64,16,256]{2,1,0:T(8,128)(2,1)}), bf16[64,16,256]{2,1,0:T(8,128)(2,1)S(1)}, u32[]{:S(2)}, u32[]{:S(2)}) async-start(bf16[64,16,256]{2,1,0:T(8,128)(2,1)} %join_in.1), calls=%async_computation.5 | async-start | bytes 1048576 | tf_op jit(solution)/shard_map/all_to_all | solution.py:424
  175.0 2.5 %collective-permute-start.15 = (bf16[16,256]{1,0:T(8,128)(2,1)S(1)}, bf16[16,256]{1,0:T(8,128)(2,1)S(1)}, u32[]{:S(2)}, u32[]{:S(2)}) collective-permute-start(bf16[16,256]{1,0:T(8,128)(2,1)S(1)} %get-tuple-element.85), channel_id=1, source_target_pairs={{0,2},{1,3},{2,4},{3,5},{4,6},{5,7},{6,0},{7,1},{8,10},{9,11},{10,... | collective-permute-start | bytes 24584 | tf_op jit(solution)/shard_map/ppermute | solution.py:429
  177.5 2.4 %collective-permute-start.16 = (bf16[16,256]{1,0:T(8,128)(2,1)S(1)}, bf16[16,256]{1,0:T(8,128)(2,1)S(1)}, u32[]{:S(2)}, u32[]{:S(2)}) collective-permute-start(bf16[16,256]{1,0:T(8,128)(2,1)S(1)} %get-tuple-element.86), channel_id=1, source_target_pairs={{0,3},{1,4},{2,5},{3,6},{4,7},{5,0},{6,1},{7,2},{8,11},{9,12},{10,... | collective-permute-start | bytes 24584 | tf_op jit(solution)/shard_map/ppermute | solution.py:429
  180.5 3.2 %collective-permute-start.18 = (bf16[16,256]{1,0:T(8,128)(2,1)S(1)}, bf16[16,256]{1,0:T(8,128)(2,1)S(1)}, u32[]{:S(2)}, u32[]{:S(2)}) collective-permute-start(bf16[16,256]{1,0:T(8,128)(2,1)S(1)} %get-tuple-element.88), channel_id=1, source_target_pairs={{0,5},{1,6},{2,7},{3,0},{4,1},{5,2},{6,3},{7,4},{8,13},{9,14},{10,... | collective-permute-start | bytes 24584 | tf_op jit(solution)/shard_map/ppermute | solution.py:429
  183.7 2.4 %collective-permute-start.19 = (bf16[16,256]{1,0:T(8,128)(2,1)S(1)}, bf16[16,256]{1,0:T(8,128)(2,1)S(1)}, u32[]{:S(2)}, u32[]{:S(2)}) collective-permute-start(bf16[16,256]{1,0:T(8,128)(2,1)S(1)} %get-tuple-element.89), channel_id=1, source_target_pairs={{0,6},{1,7},{2,0},{3,1},{4,2},{5,3},{6,4},{7,5},{8,14},{9,15},{10,... | collective-permute-start | bytes 24584 | tf_op jit(solution)/shard_map/ppermute | solution.py:429
  186.5 4.7 %collective-permute-done.19.refs_6_ = bf16[16,256]{1,0:T(8,128)(2,1)S(1)} collective-permute-done((bf16[16,256]{1,0:T(8,128)(2,1)S(1)}, bf16[16,256]{1,0:T(8,128)(2,1)S(1)}, u32[]{:S(2)}, u32[]{:S(2)}) %collective-permute-start.19) | collective-permute-done | bytes 8224 | tf_op jit(solution)/shard_map/ppermute | solution.py:429
  191.3 2.1 %collective-permute-done.20.refs_7_ = bf16[16,256]{1,0:T(8,128)(2,1)S(1)} collective-permute-done((bf16[16,256]{1,0:T(8,128)(2,1)S(1)}, bf16[16,256]{1,0:T(8,128)(2,1)S(1)}, u32[]{:S(2)}, u32[]{:S(2)}) %collective-permute-start.20) | collective-permute-done | bytes 8224 | tf_op jit(solution)/shard_map/ppermute | solution.py:429
  (54 shorter events, 31.2 us)
Async XLA Ops:
  2.4 27.4 %all-to-all-start = ((bf16[8,144,256]{2,1,0:T(8,128)(2,1)}), bf16[8,144,256]{2,1,0:T(8,128)(2,1)S(1)}, u32[]{:S(2)}, u32[]{:S(2)}) async-start(bf16[8,144,256]{2,1,0:T(8,128)(2,1)} %get-tuple-element.52), calls=%async_computation | async-start | bytes 1179648 | tf_op jit(solution)/shard_map/all_to_all | solution.py:424
  32.1 7.5 %copy-start.2 = (bf16[128,256]{1,0:T(8,128)(2,1)S(1)}, bf16[128,256]{1,0:T(8,128)(2,1)}, u32[]{:S(2)}) copy-start(bf16[128,256]{1,0:T(8,128)(2,1)} %get-tuple-element.51.refs_0_) | copy-start | bytes 196612
  32.1 33.6 %all-to-all-start.2 = ((bf16[32,128,256]{2,1,0:T(8,128)(2,1)}), bf16[32,128,256]{2,1,0:T(8,128)(2,1)}, u32[]{:S(2)}, u32[]{:S(2)}) async-start(bf16[32,128,256]{2,1,0:T(8,128)(2,1)} %get-tuple-element.55), calls=%async_computation.2 | async-start | bytes 4194304 | tf_op jit(solution)/shard_map/all_to_all | solution.py:424
  39.6 9.5 %collective-permute-start.6 = (bf16[128,256]{1,0:T(8,128)(2,1)S(1)}, bf16[128,256]{1,0:T(8,128)(2,1)S(1)}, u32[]{:S(2)}, u32[]{:S(2)}) collective-permute-start(bf16[128,256]{1,0:T(8,128)(2,1)S(1)} %copy-done.2), channel_id=1, source_target_pairs={{0,224},{32,0},{64,32},{96,64},{128,96},{160,128},{192,160},{224,1... | collective-permute-start | bytes 196616 | tf_op jit(solution)/shard_map/ppermute | solution.py:429
  39.7 10.4 %collective-permute-start.5 = (bf16[128,256]{1,0:T(8,128)(2,1)S(1)}, bf16[128,256]{1,0:T(8,128)(2,1)S(1)}, u32[]{:S(2)}, u32[]{:S(2)}) collective-permute-start(bf16[128,256]{1,0:T(8,128)(2,1)S(1)} %copy-done.2), channel_id=1, source_target_pairs={{0,192},{32,224},{64,0},{96,32},{128,64},{160,96},{192,128},{224,1... | collective-permute-start | bytes 196616 | tf_op jit(solution)/shard_map/ppermute | solution.py:429
  40.7 12.4 %collective-permute-start.4 = (bf16[128,256]{1,0:T(8,128)(2,1)S(1)}, bf16[128,256]{1,0:T(8,128)(2,1)S(1)}, u32[]{:S(2)}, u32[]{:S(2)}) collective-permute-start(bf16[128,256]{1,0:T(8,128)(2,1)S(1)} %copy-done.2), channel_id=1, source_target_pairs={{0,160},{32,192},{64,224},{96,0},{128,32},{160,64},{192,96},{224,1... | collective-permute-start | bytes 196616 | tf_op jit(solution)/shard_map/ppermute | solution.py:429
  42.8 10.2 %collective-permute-start.3 = (bf16[128,256]{1,0:T(8,128)(2,1)S(1)}, bf16[128,256]{1,0:T(8,128)(2,1)S(1)}, u32[]{:S(2)}, u32[]{:S(2)}) collective-permute-start(bf16[128,256]{1,0:T(8,128)(2,1)S(1)} %copy-done.2), channel_id=1, source_target_pairs={{0,128},{32,160},{64,192},{96,224},{128,0},{160,32},{192,64},{224,... | collective-permute-start | bytes 196616 | tf_op jit(solution)/shard_map/ppermute | solution.py:429
  46.5 10.7 %collective-permute-start.2 = (bf16[128,256]{1,0:T(8,128)(2,1)S(1)}, bf16[128,256]{1,0:T(8,128)(2,1)S(1)}, u32[]{:S(2)}, u32[]{:S(2)}) collective-permute-start(bf16[128,256]{1,0:T(8,128)(2,1)S(1)} %copy-done.2), channel_id=1, source_target_pairs={{0,96},{32,128},{64,160},{96,192},{128,224},{160,0},{192,32},{224,... | collective-permute-start | bytes 196616 | tf_op jit(solution)/shard_map/ppermute | solution.py:429
  49.1 8.4 %collective-permute-start.1 = (bf16[128,256]{1,0:T(8,128)(2,1)S(1)}, bf16[128,256]{1,0:T(8,128)(2,1)S(1)}, u32[]{:S(2)}, u32[]{:S(2)}) collective-permute-start(bf16[128,256]{1,0:T(8,128)(2,1)S(1)} %copy-done.2), channel_id=1, source_target_pairs={{0,64},{32,96},{64,128},{96,160},{128,192},{160,224},{192,0},{224,... | collective-permute-start | bytes 196616 | tf_op jit(solution)/shard_map/ppermute | solution.py:429
  50.1 9.8 %collective-permute-start = (bf16[128,256]{1,0:T(8,128)(2,1)S(1)}, bf16[128,256]{1,0:T(8,128)(2,1)S(1)}, u32[]{:S(2)}, u32[]{:S(2)}) collective-permute-start(bf16[128,256]{1,0:T(8,128)(2,1)S(1)} %copy-done.2), channel_id=1, source_target_pairs={{0,32},{32,64},{64,96},{96,128},{128,160},{160,192},{192,224},{224... | collective-permute-start | bytes 196616 | tf_op jit(solution)/shard_map/ppermute | solution.py:429
  65.7 33.3 %all-to-all-start.1 = ((bf16[32,128,256]{2,1,0:T(8,128)(2,1)}), bf16[32,128,256]{2,1,0:T(8,128)(2,1)}, u32[]{:S(2)}, u32[]{:S(2)}) async-start(bf16[32,128,256]{2,1,0:T(8,128)(2,1)} %pick_g.1), calls=%async_computation.1 | async-start | bytes 4194304 | tf_op jit(solution)/shard_map/all_to_all | solution.py:424
  72.8 1.4 copy-start.3
  74.2 1.4 copy-start.5
  75.6 1.4 copy-start.7
  98.9 33.3 %all-to-all-start.4 = ((bf16[32,128,256]{2,1,0:T(8,128)(2,1)}), bf16[32,128,256]{2,1,0:T(8,128)(2,1)}, u32[]{:S(2)}, u32[]{:S(2)}) async-start(bf16[32,128,256]{2,1,0:T(8,128)(2,1)} %copy-done.1), calls=%async_computation.4 | async-start | bytes 4194304 | tf_op jit(solution)/shard_map/all_to_all | solution.py:424
  106.1 1.4 copy-start.4
  132.2 33.2 %all-to-all-start.3 = ((bf16[32,128,256]{2,1,0:T(8,128)(2,1)}), bf16[32,128,256]{2,1,0:T(8,128)(2,1)S(1)}, u32[]{:S(2)}, u32[]{:S(2)}) async-start(bf16[32,128,256]{2,1,0:T(8,128)(2,1)} %copy-done), calls=%async_computation.3 | async-start | bytes 4194304 | tf_op jit(solution)/shard_map/all_to_all | solution.py:424
  141.9 8.1 %collective-permute-start.7 = (bf16[128,256]{1,0:T(8,128)(2,1)S(1)}, bf16[128,256]{1,0:T(8,128)(2,1)S(1)}, u32[]{:S(2)}, u32[]{:S(2)}) collective-permute-start(bf16[128,256]{1,0:T(8,128)(2,1)S(1)} %get-tuple-element.68), channel_id=1, source_target_pairs={{0,32},{32,64},{64,96},{96,128},{128,160},{160,192},{192,224},{224... | collective-permute-start | bytes 196616 | tf_op jit(solution)/shard_map/ppermute | solution.py:429
  142.7 12.6 %collective-permute-start.8 = (bf16[128,256]{1,0:T(8,128)(2,1)S(1)}, bf16[128,256]{1,0:T(8,128)(2,1)S(1)}, u32[]{:S(2)}, u32[]{:S(2)}) collective-permute-start(bf16[128,256]{1,0:T(8,128)(2,1)S(1)} %get-tuple-element.69), channel_id=1, source_target_pairs={{0,64},{32,96},{64,128},{96,160},{128,192},{160,224},{192,0},{224,... | collective-permute-start | bytes 196616 | tf_op jit(solution)/shard_map/ppermute | solution.py:429
  142.8 12.6 %collective-permute-start.9 = (bf16[128,256]{1,0:T(8,128)(2,1)S(1)}, bf16[128,256]{1,0:T(8,128)(2,1)S(1)}, u32[]{:S(2)}, u32[]{:S(2)}) collective-permute-start(bf16[128,256]{1,0:T(8,128)(2,1)S(1)} %get-tuple-element.70), channel_id=1, source_target_pairs={{0,96},{32,128},{64,160},{96,192},{128,224},{160,0},{192,32},{224,... | collective-permute-start | bytes 196616 | tf_op jit(solution)/shard_map/ppermute | solution.py:429
  145.4 9.9 %collective-permute-start.10 = (bf16[128,256]{1,0:T(8,128)(2,1)S(1)}, bf16[128,256]{1,0:T(8,128)(2,1)S(1)}, u32[]{:S(2)}, u32[]{:S(2)}) collective-permute-start(bf16[128,256]{1,0:T(8,128)(2,1)S(1)} %get-tuple-element.71), channel_id=1, source_target_pairs={{0,128},{32,160},{64,192},{96,224},{128,0},{160,32},{192,64},{224,... | collective-permute-start | bytes 196616 | tf_op jit(solution)/shard_map/ppermute | solution.py:429
  148.8 9.3 %collective-permute-start.11 = (bf16[128,256]{1,0:T(8,128)(2,1)S(1)}, bf16[128,256]{1,0:T(8,128)(2,1)S(1)}, u32[]{:S(2)}, u32[]{:S(2)}) collective-permute-start(bf16[128,256]{1,0:T(8,128)(2,1)S(1)} %get-tuple-element.72), channel_id=1, source_target_pairs={{0,160},{32,192},{64,224},{96,0},{128,32},{160,64},{192,96},{224,1... | collective-permute-start | bytes 196616 | tf_op jit(solution)/shard_map/ppermute | solution.py:429
  150.0 11.3 %collective-permute-start.12 = (bf16[128,256]{1,0:T(8,128)(2,1)S(1)}, bf16[128,256]{1,0:T(8,128)(2,1)S(1)}, u32[]{:S(2)}, u32[]{:S(2)}) collective-permute-start(bf16[128,256]{1,0:T(8,128)(2,1)S(1)} %get-tuple-element.73), channel_id=1, source_target_pairs={{0,192},{32,224},{64,0},{96,32},{128,64},{160,96},{192,128},{224,1... | collective-permute-start | bytes 196616 | tf_op jit(solution)/shard_map/ppermute | solution.py:429
  155.3 6.9 %collective-permute-start.13 = (bf16[128,256]{1,0:T(8,128)(2,1)S(1)}, bf16[128,256]{1,0:T(8,128)(2,1)S(1)}, u32[]{:S(2)}, u32[]{:S(2)}) collective-permute-start(bf16[128,256]{1,0:T(8,128)(2,1)S(1)} %get-tuple-element.74), channel_id=1, source_target_pairs={{0,224},{32,0},{64,32},{96,64},{128,96},{160,128},{192,160},{224,1... | collective-permute-start | bytes 196616 | tf_op jit(solution)/shard_map/ppermute | solution.py:429
  167.0 26.3 %all-to-all-start.5 = ((bf16[64,16,256]{2,1,0:T(8,128)(2,1)}), bf16[64,16,256]{2,1,0:T(8,128)(2,1)S(1)}, u32[]{:S(2)}, u32[]{:S(2)}) async-start(bf16[64,16,256]{2,1,0:T(8,128)(2,1)} %join_in.1), calls=%async_computation.5 | async-start | bytes 1048576 | tf_op jit(solution)/shard_map/all_to_all | solution.py:424
  174.5 9.2 %collective-permute-start.14 = (bf16[16,256]{1,0:T(8,128)(2,1)S(1)}, bf16[16,256]{1,0:T(8,128)(2,1)S(1)}, u32[]{:S(2)}, u32[]{:S(2)}) collective-permute-start(bf16[16,256]{1,0:T(8,128)(2,1)S(1)} %get-tuple-element.84), channel_id=1, source_target_pairs={{0,1},{1,2},{2,3},{3,4},{4,5},{5,6},{6,7},{7,0},{8,9},{9,10},{10,1... | collective-permute-start | bytes 24584 | tf_op jit(solution)/shard_map/ppermute | solution.py:429
  175.0 11.0 %collective-permute-start.15 = (bf16[16,256]{1,0:T(8,128)(2,1)S(1)}, bf16[16,256]{1,0:T(8,128)(2,1)S(1)}, u32[]{:S(2)}, u32[]{:S(2)}) collective-permute-start(bf16[16,256]{1,0:T(8,128)(2,1)S(1)} %get-tuple-element.85), channel_id=1, source_target_pairs={{0,2},{1,3},{2,4},{3,5},{4,6},{5,7},{6,0},{7,1},{8,10},{9,11},{10,... | collective-permute-start | bytes 24584 | tf_op jit(solution)/shard_map/ppermute | solution.py:429
  177.5 8.6 %collective-permute-start.16 = (bf16[16,256]{1,0:T(8,128)(2,1)S(1)}, bf16[16,256]{1,0:T(8,128)(2,1)S(1)}, u32[]{:S(2)}, u32[]{:S(2)}) collective-permute-start(bf16[16,256]{1,0:T(8,128)(2,1)S(1)} %get-tuple-element.86), channel_id=1, source_target_pairs={{0,3},{1,4},{2,5},{3,6},{4,7},{5,0},{6,1},{7,2},{8,11},{9,12},{10,... | collective-permute-start | bytes 24584 | tf_op jit(solution)/shard_map/ppermute | solution.py:429
  179.8 6.2 %collective-permute-start.17 = (bf16[16,256]{1,0:T(8,128)(2,1)S(1)}, bf16[16,256]{1,0:T(8,128)(2,1)S(1)}, u32[]{:S(2)}, u32[]{:S(2)}) collective-permute-start(bf16[16,256]{1,0:T(8,128)(2,1)S(1)} %get-tuple-element.87), channel_id=1, source_target_pairs={{0,4},{1,5},{2,6},{3,7},{4,0},{5,1},{6,2},{7,3},{8,12},{9,13},{10,... | collective-permute-start | bytes 24584 | tf_op jit(solution)/shard_map/ppermute | solution.py:429
  180.5 6.1 %collective-permute-start.18 = (bf16[16,256]{1,0:T(8,128)(2,1)S(1)}, bf16[16,256]{1,0:T(8,128)(2,1)S(1)}, u32[]{:S(2)}, u32[]{:S(2)}) collective-permute-start(bf16[16,256]{1,0:T(8,128)(2,1)S(1)} %get-tuple-element.88), channel_id=1, source_target_pairs={{0,5},{1,6},{2,7},{3,0},{4,1},{5,2},{6,3},{7,4},{8,13},{9,14},{10,... | collective-permute-start | bytes 24584 | tf_op jit(solution)/shard_map/ppermute | solution.py:429
  183.7 7.6 %collective-permute-start.19 = (bf16[16,256]{1,0:T(8,128)(2,1)S(1)}, bf16[16,256]{1,0:T(8,128)(2,1)S(1)}, u32[]{:S(2)}, u32[]{:S(2)}) collective-permute-start(bf16[16,256]{1,0:T(8,128)(2,1)S(1)} %get-tuple-element.89), channel_id=1, source_target_pairs={{0,6},{1,7},{2,0},{3,1},{4,2},{5,3},{6,4},{7,5},{8,14},{9,15},{10,... | collective-permute-start | bytes 24584 | tf_op jit(solution)/shard_map/ppermute | solution.py:429
  186.1 7.3 %collective-permute-start.20 = (bf16[16,256]{1,0:T(8,128)(2,1)S(1)}, bf16[16,256]{1,0:T(8,128)(2,1)S(1)}, u32[]{:S(2)}, u32[]{:S(2)}) collective-permute-start(bf16[16,256]{1,0:T(8,128)(2,1)S(1)} %get-tuple-element.90), channel_id=1, source_target_pairs={{0,7},{1,0},{2,1},{3,2},{4,3},{5,4},{6,5},{7,6},{8,15},{9,8},{10,9... | collective-permute-start | bytes 24584 | tf_op jit(solution)/shard_map/ppermute | solution.py:429
  (6 other events, 7.5 us)

commit v4 on v3

--- a/solution.py
+++ b/solution.py
@@ -424,10 +424,12 @@
     return lax.all_to_all(buffer, axes, split_axis=0, concat_axis=0, tiled=True)
 
 
-def spread(arrays, axes):
-    return [arrays[0]] + [
+def spread(arrays, axes, shifts=range(8)):
+    return [
         lax.ppermute(arrays[shift], axes, [(i, (i + shift) % 8) for i in range(8)])
-        for shift in range(1, 8)
+        if shift
+        else arrays[0]
+        for shift in shifts
     ]
 
 
@@ -453,9 +455,10 @@
     in_back = swap(in_send, PLANE)
     y_parts = spread(join_out(zs, place, weight, out_back), ("z",))
     pieces = total(col, y_parts)
-    in_back, pieces = lax.optimization_barrier((in_back, pieces))
-    dx_part = join_in(place, in_back)
-    pieces = spread(pieces, EX)
+    early = spread(pieces, EX, range(4))
+    in_back, early = lax.optimization_barrier((in_back, early))
+    dx_part, pieces = lax.optimization_barrier((join_in(place, in_back), pieces))
+    pieces = early + spread(pieces, EX, range(4, 8))
     layer_out, input_grad = last(col, pieces, swap(dx_part, ("z", "xh", "y")))
     return layer_out, input_grad, *weight_grads
 

time: 195 us -> 202 us (1.036); the launches traced: 194 us -> 199 us
  starting transfers between devices: 79.9 us -> 82.6 us
    all_to_all x6, starting transfers between devices: 44.7 us -> 47.7 us  [swap(): return lax.all_to_all(buffer, axes, split_axis=0, concat_axis=0, tiled=True)]
    ppermute x21, waiting for transfers between devices: 24.3 us -> 26.8 us  [spread(): lax.ppermute(arrays[shift], axes, [(i, (i + shift) % 8) for i in range(8)])]
  transfers between devices with their start and end apart: 27 -> 27, of which waited for: 16 -> 17; matrix products, arithmetic and copies ran while one was open for 0% -> 0% of each run, Pallas kernels for 15% -> 15%
where the time goes in v4:
time: 202 us; the launch traced here: 199 us
  starting transfers between devices  82.6 us (41%)
  waiting for transfers between devices  66.3 us (33%)
  Pallas kernels  35.7 us (18%)
  local copies, waits for them, and re-layouts  13.1 us (6%)
    all_to_all x6, starting transfers between devices, swap(): return lax.all_to_all(buffer, axes, split_axis=0, concat_axis=0, tiled=True)  47.7 us
    all_to_all x6, waiting for transfers between devices, swap(): return lax.all_to_all(buffer, axes, split_axis=0, concat_axis=0, tiled=True)  39.4 us
    ppermute x21, starting transfers between devices, spread(): lax.ppermute(arrays[shift], axes, [(i, (i + shift) % 8) for i in range(8)])  34.9 us
    ppermute x21, waiting for transfers between devices, spread(): lax.ppermute(arrays[shift], axes, [(i, (i + shift) % 8) for i in range(8)])  26.8 us
    unnamed x22, local copies, waits for them, and re-layouts  13.1 us
    pallas_call x1, Pallas kernels, grads(): pl.pallas_call(grads_kernel, out_shape=[jax.ShapeDtypeStruct((1, width, f...  8.74 us
    pallas_call x1, Pallas kernels, backward(): pl.pallas_call(backward_kernel, out_shape=[jax.ShapeDtypeStruct(g_rows.sh...  8.18 us
    pallas_call x1, Pallas kernels, forward(): pl.pallas_call(forward_kernel, out_shape=[jax.ShapeDtypeStruct(x_rows.sha...  7.75 us
  transfers between devices with their start and end apart: 27, of which 17 were waited for; matrix products, arithmetic and copies ran while one was open for 0% of the time, Pallas kernels for 15%

profile of v4, /device:TPU:28, one launch (start us, length us, event | category | flops | bytes accessed | tf_op | source)
XLA Modules:
  0.0 198.5 jit_solution(3113346027838083143)
XLA Ops:
  2.4 8.5 %all-to-all-start = ((bf16[8,144,256]{2,1,0:T(8,128)(2,1)}), bf16[8,144,256]{2,1,0:T(8,128)(2,1)S(1)}, u32[]{:S(2)}, u32[]{:S(2)}) async-start(bf16[8,144,256]{2,1,0:T(8,128)(2,1)} %get-tuple-element.53), calls=%async_computation | async-start | bytes 1179648 | tf_op jit(solution)/shard_map/all_to_all | solution.py:424
  10.9 18.9 %all-to-all-done.x_ref = bf16[8,144,256]{2,1,0:T(8,128)(2,1)S(1)} async-done(((bf16[8,144,256]{2,1,0:T(8,128)(2,1)}), bf16[8,144,256]{2,1,0:T(8,128)(2,1)S(1)}, u32[]{:S(2)}, u32[]{:S(2)}) %all-to-all-start) | async-done | bytes 589856 | tf_op jit(solution)/shard_map/all_to_all | solution.py:424
  29.8 2.3 %pick_x.1 = (bf16[32,128,256]{2,1,0:T(8,128)(2,1)}, f32[8,16,128]{2,1,0:T(8,128)S(1)}, f32[8,16,128]{2,1,0:T(8,128)S(1)}) custom-call(s32[1]{0:T(128)} %bitcast.1.z_ref, bf16[8,144,256]{2,1,0:T(8,128)(2,1)S(1)} %all-to-all-done.x_ref), custom_call_target="tpu_custom_call" | custom-call | tf_op jit(solution)/shard_map/pick_x/pallas_call | solution.py:135
  32.1 7.4 %all-to-all-start.2 = ((bf16[32,128,256]{2,1,0:T(8,128)(2,1)}), bf16[32,128,256]{2,1,0:T(8,128)(2,1)}, u32[]{:S(2)}, u32[]{:S(2)}) async-start(bf16[32,128,256]{2,1,0:T(8,128)(2,1)} %get-tuple-element.56), calls=%async_computation.2 | async-start | bytes 4194304 | tf_op jit(solution)/shard_map/all_to_all | solution.py:424
  40.7 2.1 %collective-permute-start.4 = (bf16[128,256]{1,0:T(8,128)(2,1)S(1)}, bf16[128,256]{1,0:T(8,128)(2,1)S(1)}, u32[]{:S(2)}, u32[]{:S(2)}) collective-permute-start(bf16[128,256]{1,0:T(8,128)(2,1)S(1)} %copy-done.2), channel_id=1, source_target_pairs={{0,160},{32,192},{64,224},{96,0},{128,32},{160,64},{192,96},{224,1... | collective-permute-start | bytes 196616 | tf_op jit(solution)/shard_map/ppermute | solution.py:429
  42.8 3.7 %collective-permute-start.3 = (bf16[128,256]{1,0:T(8,128)(2,1)S(1)}, bf16[128,256]{1,0:T(8,128)(2,1)S(1)}, u32[]{:S(2)}, u32[]{:S(2)}) collective-permute-start(bf16[128,256]{1,0:T(8,128)(2,1)S(1)} %copy-done.2), channel_id=1, source_target_pairs={{0,128},{32,160},{64,192},{96,224},{128,0},{160,32},{192,64},{224,... | collective-permute-start | bytes 196616 | tf_op jit(solution)/shard_map/ppermute | solution.py:429
  46.5 2.6 %collective-permute-start.2 = (bf16[128,256]{1,0:T(8,128)(2,1)S(1)}, bf16[128,256]{1,0:T(8,128)(2,1)S(1)}, u32[]{:S(2)}, u32[]{:S(2)}) collective-permute-start(bf16[128,256]{1,0:T(8,128)(2,1)S(1)} %copy-done.2), channel_id=1, source_target_pairs={{0,96},{32,128},{64,160},{96,192},{128,224},{160,0},{192,32},{224,... | collective-permute-start | bytes 196616 | tf_op jit(solution)/shard_map/ppermute | solution.py:429
  53.0 4.1 %collective-permute-done.2.refs_3_ = bf16[128,256]{1,0:T(8,128)(2,1)S(1)} collective-permute-done((bf16[128,256]{1,0:T(8,128)(2,1)S(1)}, bf16[128,256]{1,0:T(8,128)(2,1)S(1)}, u32[]{:S(2)}, u32[]{:S(2)}) %collective-permute-start.2) | collective-permute-done | bytes 65568 | tf_op jit(solution)/shard_map/ppermute | solution.py:429
  57.4 2.4 %collective-permute-done.refs_1_ = bf16[128,256]{1,0:T(8,128)(2,1)S(1)} collective-permute-done((bf16[128,256]{1,0:T(8,128)(2,1)S(1)}, bf16[128,256]{1,0:T(8,128)(2,1)S(1)}, u32[]{:S(2)}, u32[]{:S(2)}) %collective-permute-start) | collective-permute-done | bytes 65568 | tf_op jit(solution)/shard_map/ppermute | solution.py:429
  61.7 3.9 %all-to-all-done.2.x_ref = bf16[32,128,256]{2,1,0:T(8,128)(2,1)} async-done(((bf16[32,128,256]{2,1,0:T(8,128)(2,1)}), bf16[32,128,256]{2,1,0:T(8,128)(2,1)}, u32[]{:S(2)}, u32[]{:S(2)}) %all-to-all-start.2) | async-done | bytes 2097184 | tf_op jit(solution)/shard_map/all_to_all | solution.py:424
  65.7 7.1 %all-to-all-start.1 = ((bf16[32,128,256]{2,1,0:T(8,128)(2,1)}), bf16[32,128,256]{2,1,0:T(8,128)(2,1)}, u32[]{:S(2)}, u32[]{:S(2)}) async-start(bf16[32,128,256]{2,1,0:T(8,128)(2,1)} %pick_g.1), calls=%async_computation.1 | async-start | bytes 4194304 | tf_op jit(solution)/shard_map/all_to_all | solution.py:424
  77.0 7.8 %forward.1 = (bf16[32,128,256]{2,1,0:T(8,128)(2,1)S(1)}, f32[512,384]{1,0:T(8,128)S(1)}, f32[512,384]{1,0:T(8,128)S(1)}, bf16[512,384]{1,0:T(8,128)(2,1)S(1)}) custom-call(bf16[32,128,256]{2,1,0:T(8,128)(2,1)} %all-to-all-done.2.x_ref, bf16[1,2048,384]{2,1,0:T(8,128)(2,1)S(1)} %copy-done.3, bf16[1,2048,384]{2,1,0:T(8,128)(2,1)S(1)} %copy-done.5, ...), custom_call_target="tpu_custom_call" | custom-call | flops 2415919104 | bytes 11534336 | tf_op jit(solution)/shard_map/forward/pallas_call | solution.py:218
  87.0 11.9 %all-to-all-done.1.g_ref = bf16[32,128,256]{2,1,0:T(8,128)(2,1)} async-done(((bf16[32,128,256]{2,1,0:T(8,128)(2,1)}), bf16[32,128,256]{2,1,0:T(8,128)(2,1)}, u32[]{:S(2)}, u32[]{:S(2)}) %all-to-all-start.1) | async-done | bytes 2097184 | tf_op jit(solution)/shard_map/all_to_all | solution.py:424
  98.9 7.1 %all-to-all-start.4 = ((bf16[32,128,256]{2,1,0:T(8,128)(2,1)}), bf16[32,128,256]{2,1,0:T(8,128)(2,1)}, u32[]{:S(2)}, u32[]{:S(2)}) async-start(bf16[32,128,256]{2,1,0:T(8,128)(2,1)} %copy-done.1), calls=%async_computation.4 | async-start | bytes 4194304 | tf_op jit(solution)/shard_map/all_to_all | solution.py:424
  111.4 8.2 %backward.1 = (bf16[32,128,256]{2,1,0:T(8,128)(2,1)S(1)}, bf16[512,384]{1,0:T(8,128)(2,1)S(1)}, bf16[512,384]{1,0:T(8,128)(2,1)S(1)}) custom-call(bf16[32,128,256]{2,1,0:T(8,128)(2,1)} %all-to-all-done.1.g_ref, f32[512,384]{1,0:T(8,128)S(1)} %get-tuple-element.57.gate_ref, f32[512,384]{1,0:T(8,128)S(1)} %copy-done.10, bf16[1,2048,384]{2,1,0:T(8,128)(2,1)S(1)} %copy-done.4, ...), custom_call_target="tpu_custom_call" | custom-call | flops 2415919104 | bytes 11534336 | tf_op jit(solution)/shard_map/backward/pallas_call | solution.py:262
  120.9 8.7 %grads.1 = (bf16[1,2048,384]{2,1,0:T(8,128)(2,1)}, bf16[1,2048,384]{2,1,0:T(8,128)(2,1)}, bf16[1,384,2048]{2,1,0:T(8,128)(2,1)}) custom-call(bf16[32,128,256]{2,1,0:T(8,128)(2,1)} %all-to-all-done.2.x_ref, bf16[32,128,256]{2,1,0:T(8,128)(2,1)} %all-to-all-done.1.g_ref, bf16[512,384]{1,0:T(8,128)(2,1)S(1)} %get-tuple-element.60.hidden_ref, ...), custom_call_target="tpu_custom_call" | custom-call | flops 2415919104 | bytes 10485760 | tf_op jit(solution)/shard_map/grads/pallas_call | solution.py:295
  129.7 2.5 %all-to-all-done.4.back_ref = bf16[32,128,256]{2,1,0:T(8,128)(2,1)} async-done(((bf16[32,128,256]{2,1,0:T(8,128)(2,1)}), bf16[32,128,256]{2,1,0:T(8,128)(2,1)}, u32[]{:S(2)}, u32[]{:S(2)}) %all-to-all-start.4) | async-done | bytes 2097184 | tf_op jit(solution)/shard_map/all_to_all | solution.py:424
  132.2 7.1 %all-to-all-start.3 = ((bf16[32,128,256]{2,1,0:T(8,128)(2,1)}), bf16[32,128,256]{2,1,0:T(8,128)(2,1)S(1)}, u32[]{:S(2)}, u32[]{:S(2)}) async-start(bf16[32,128,256]{2,1,0:T(8,128)(2,1)} %copy-done), calls=%async_computation.3 | async-start | bytes 4194304 | tf_op jit(solution)/shard_map/all_to_all | solution.py:424
  139.3 2.6 %join_out.1 = (f32[128,256]{1,0:T(8,128)S(1)}, bf16[128,256]{1,0:T(8,128)(2,1)S(1)}, bf16[128,256]{1,0:T(8,128)(2,1)S(1)}, bf16[128,256]{1,0:T(8,128)(2,1)S(1)},...) custom-call(s32[1]{0:T(128)} %bitcast.1.z_ref, ...), custom_call_target="tpu_custom_call" | custom-call | tf_op jit(solution)/shard_map/join_out/pallas_call | solution.py:333
  142.8 2.7 %collective-permute-start.9 = (bf16[128,256]{1,0:T(8,128)(2,1)S(1)}, bf16[128,256]{1,0:T(8,128)(2,1)S(1)}, u32[]{:S(2)}, u32[]{:S(2)}) collective-permute-start(bf16[128,256]{1,0:T(8,128)(2,1)S(1)} %get-tuple-element.71), channel_id=1, source_target_pairs={{0,96},{32,128},{64,160},{96,192},{128,224},{160,0},{192,32},{224,... | collective-permute-start | bytes 196616 | tf_op jit(solution)/shard_map/ppermute | solution.py:429
  145.4 3.3 %collective-permute-start.10 = (bf16[128,256]{1,0:T(8,128)(2,1)S(1)}, bf16[128,256]{1,0:T(8,128)(2,1)S(1)}, u32[]{:S(2)}, u32[]{:S(2)}) collective-permute-start(bf16[128,256]{1,0:T(8,128)(2,1)S(1)} %get-tuple-element.72), channel_id=1, source_target_pairs={{0,128},{32,160},{64,192},{96,224},{128,0},{160,32},{192,64},{224,... | collective-permute-start | bytes 196616 | tf_op jit(solution)/shard_map/ppermute | solution.py:429
  150.0 3.3 %collective-permute-start.12 = (bf16[128,256]{1,0:T(8,128)(2,1)S(1)}, bf16[128,256]{1,0:T(8,128)(2,1)S(1)}, u32[]{:S(2)}, u32[]{:S(2)}) collective-permute-start(bf16[128,256]{1,0:T(8,128)(2,1)S(1)} %get-tuple-element.74), channel_id=1, source_target_pairs={{0,192},{32,224},{64,0},{96,32},{128,64},{160,96},{192,128},{224,1... | collective-permute-start | bytes 196616 | tf_op jit(solution)/shard_map/ppermute | solution.py:429
  153.3 2.1 %collective-permute-done.8.refs_2_ = bf16[128,256]{1,0:T(8,128)(2,1)S(1)} collective-permute-done((bf16[128,256]{1,0:T(8,128)(2,1)S(1)}, bf16[128,256]{1,0:T(8,128)(2,1)S(1)}, u32[]{:S(2)}, u32[]{:S(2)}) %collective-permute-start.8) | collective-permute-done | bytes 65568 | tf_op jit(solution)/shard_map/ppermute | solution.py:429
  155.4 2.7 %collective-permute-done.11.refs_5_ = bf16[128,256]{1,0:T(8,128)(2,1)S(1)} collective-permute-done((bf16[128,256]{1,0:T(8,128)(2,1)S(1)}, bf16[128,256]{1,0:T(8,128)(2,1)S(1)}, u32[]{:S(2)}, u32[]{:S(2)}) %collective-permute-start.11) | collective-permute-done | bytes 65568 | tf_op jit(solution)/shard_map/ppermute | solution.py:429
  158.1 3.2 %collective-permute-done.12.refs_6_ = bf16[128,256]{1,0:T(8,128)(2,1)S(1)} collective-permute-done((bf16[128,256]{1,0:T(8,128)(2,1)S(1)}, bf16[128,256]{1,0:T(8,128)(2,1)S(1)}, u32[]{:S(2)}, u32[]{:S(2)}) %collective-permute-start.12) | collective-permute-done | bytes 65568 | tf_op jit(solution)/shard_map/ppermute | solution.py:429
  162.6 2.8 %collective-permute-start.15 = (bf16[16,256]{1,0:T(8,128)(2,1)S(1)}, bf16[16,256]{1,0:T(8,128)(2,1)S(1)}, u32[]{:S(2)}, u32[]{:S(2)}) collective-permute-start(bf16[16,256]{1,0:T(8,128)(2,1)S(1)} %get-tuple-element.78), channel_id=1, source_target_pairs={{0,2},{1,3},{2,4},{3,5},{4,6},{5,7},{6,0},{7,1},{8,10},{9,11},{10,... | collective-permute-start | bytes 24584 | tf_op jit(solution)/shard_map/ppermute | solution.py:429
  165.4 2.4 %collective-permute-start.16 = (bf16[16,256]{1,0:T(8,128)(2,1)S(1)}, bf16[16,256]{1,0:T(8,128)(2,1)S(1)}, u32[]{:S(2)}, u32[]{:S(2)}) collective-permute-start(bf16[16,256]{1,0:T(8,128)(2,1)S(1)} %get-tuple-element.79), channel_id=1, source_target_pairs={{0,3},{1,4},{2,5},{3,6},{4,7},{5,0},{6,1},{7,2},{8,11},{9,12},{10,... | collective-permute-start | bytes 24584 | tf_op jit(solution)/shard_map/ppermute | solution.py:429
  167.7 2.5 %collective-permute-done.16.refs_3_ = bf16[16,256]{1,0:T(8,128)(2,1)S(1)} collective-permute-done((bf16[16,256]{1,0:T(8,128)(2,1)S(1)}, bf16[16,256]{1,0:T(8,128)(2,1)S(1)}, u32[]{:S(2)}, u32[]{:S(2)}) %collective-permute-start.16) | collective-permute-done | bytes 8224 | tf_op jit(solution)/shard_map/ppermute | solution.py:429
  171.9 10.5 %all-to-all-start.5 = ((bf16[64,16,256]{2,1,0:T(8,128)(2,1)}), bf16[64,16,256]{2,1,0:T(8,128)(2,1)S(1)}, u32[]{:S(2)}, u32[]{:S(2)}) async-start(bf16[64,16,256]{2,1,0:T(8,128)(2,1)} %join_in.1), calls=%async_computation.5 | async-start | bytes 1048576 | tf_op jit(solution)/shard_map/all_to_all | solution.py:424
  183.4 4.9 %collective-permute-start.19 = (bf16[16,256]{1,0:T(8,128)(2,1)S(1)}, bf16[16,256]{1,0:T(8,128)(2,1)S(1)}, u32[]{:S(2)}, u32[]{:S(2)}) collective-permute-start(bf16[16,256]{1,0:T(8,128)(2,1)S(1)} %get-tuple-element.91), channel_id=1, source_target_pairs={{0,6},{1,7},{2,0},{3,1},{4,2},{5,3},{6,4},{7,5},{8,14},{9,15},{10,... | collective-permute-start | bytes 24584 | tf_op jit(solution)/shard_map/ppermute | solution.py:429
  191.2 4.4 %collective-permute-done.20.refs_7_ = bf16[16,256]{1,0:T(8,128)(2,1)S(1)} collective-permute-done((bf16[16,256]{1,0:T(8,128)(2,1)S(1)}, bf16[16,256]{1,0:T(8,128)(2,1)S(1)}, u32[]{:S(2)}, u32[]{:S(2)}) %collective-permute-start.20) | collective-permute-done | bytes 8224 | tf_op jit(solution)/shard_map/ppermute | solution.py:429
  195.6 2.2 %all-to-all-done.5.refs_8_ = bf16[64,16,256]{2,1,0:T(8,128)(2,1)S(1)} async-done(((bf16[64,16,256]{2,1,0:T(8,128)(2,1)}), bf16[64,16,256]{2,1,0:T(8,128)(2,1)S(1)}, u32[]{:S(2)}, u32[]{:S(2)}) %all-to-all-start.5) | async-done | bytes 524320 | tf_op jit(solution)/shard_map/all_to_all | solution.py:424
  (54 shorter events, 31.8 us)
Async XLA Ops:
  2.4 27.4 %all-to-all-start = ((bf16[8,144,256]{2,1,0:T(8,128)(2,1)}), bf16[8,144,256]{2,1,0:T(8,128)(2,1)S(1)}, u32[]{:S(2)}, u32[]{:S(2)}) async-start(bf16[8,144,256]{2,1,0:T(8,128)(2,1)} %get-tuple-element.53), calls=%async_computation | async-start | bytes 1179648 | tf_op jit(solution)/shard_map/all_to_all | solution.py:424
  32.1 7.5 %copy-start.2 = (bf16[128,256]{1,0:T(8,128)(2,1)S(1)}, bf16[128,256]{1,0:T(8,128)(2,1)}, u32[]{:S(2)}) copy-start(bf16[128,256]{1,0:T(8,128)(2,1)} %get-tuple-element.52.refs_0_) | copy-start | bytes 196612
  32.1 33.6 %all-to-all-start.2 = ((bf16[32,128,256]{2,1,0:T(8,128)(2,1)}), bf16[32,128,256]{2,1,0:T(8,128)(2,1)}, u32[]{:S(2)}, u32[]{:S(2)}) async-start(bf16[32,128,256]{2,1,0:T(8,128)(2,1)} %get-tuple-element.56), calls=%async_computation.2 | async-start | bytes 4194304 | tf_op jit(solution)/shard_map/all_to_all | solution.py:424
  39.6 9.5 %collective-permute-start.6 = (bf16[128,256]{1,0:T(8,128)(2,1)S(1)}, bf16[128,256]{1,0:T(8,128)(2,1)S(1)}, u32[]{:S(2)}, u32[]{:S(2)}) collective-permute-start(bf16[128,256]{1,0:T(8,128)(2,1)S(1)} %copy-done.2), channel_id=1, source_target_pairs={{0,224},{32,0},{64,32},{96,64},{128,96},{160,128},{192,160},{224,1... | collective-permute-start | bytes 196616 | tf_op jit(solution)/shard_map/ppermute | solution.py:429
  39.7 10.4 %collective-permute-start.5 = (bf16[128,256]{1,0:T(8,128)(2,1)S(1)}, bf16[128,256]{1,0:T(8,128)(2,1)S(1)}, u32[]{:S(2)}, u32[]{:S(2)}) collective-permute-start(bf16[128,256]{1,0:T(8,128)(2,1)S(1)} %copy-done.2), channel_id=1, source_target_pairs={{0,192},{32,224},{64,0},{96,32},{128,64},{160,96},{192,128},{224,1... | collective-permute-start | bytes 196616 | tf_op jit(solution)/shard_map/ppermute | solution.py:429
  40.7 12.4 %collective-permute-start.4 = (bf16[128,256]{1,0:T(8,128)(2,1)S(1)}, bf16[128,256]{1,0:T(8,128)(2,1)S(1)}, u32[]{:S(2)}, u32[]{:S(2)}) collective-permute-start(bf16[128,256]{1,0:T(8,128)(2,1)S(1)} %copy-done.2), channel_id=1, source_target_pairs={{0,160},{32,192},{64,224},{96,0},{128,32},{160,64},{192,96},{224,1... | collective-permute-start | bytes 196616 | tf_op jit(solution)/shard_map/ppermute | solution.py:429
  42.8 10.2 %collective-permute-start.3 = (bf16[128,256]{1,0:T(8,128)(2,1)S(1)}, bf16[128,256]{1,0:T(8,128)(2,1)S(1)}, u32[]{:S(2)}, u32[]{:S(2)}) collective-permute-start(bf16[128,256]{1,0:T(8,128)(2,1)S(1)} %copy-done.2), channel_id=1, source_target_pairs={{0,128},{32,160},{64,192},{96,224},{128,0},{160,32},{192,64},{224,... | collective-permute-start | bytes 196616 | tf_op jit(solution)/shard_map/ppermute | solution.py:429
  46.5 10.7 %collective-permute-start.2 = (bf16[128,256]{1,0:T(8,128)(2,1)S(1)}, bf16[128,256]{1,0:T(8,128)(2,1)S(1)}, u32[]{:S(2)}, u32[]{:S(2)}) collective-permute-start(bf16[128,256]{1,0:T(8,128)(2,1)S(1)} %copy-done.2), channel_id=1, source_target_pairs={{0,96},{32,128},{64,160},{96,192},{128,224},{160,0},{192,32},{224,... | collective-permute-start | bytes 196616 | tf_op jit(solution)/shard_map/ppermute | solution.py:429
  49.1 8.4 %collective-permute-start.1 = (bf16[128,256]{1,0:T(8,128)(2,1)S(1)}, bf16[128,256]{1,0:T(8,128)(2,1)S(1)}, u32[]{:S(2)}, u32[]{:S(2)}) collective-permute-start(bf16[128,256]{1,0:T(8,128)(2,1)S(1)} %copy-done.2), channel_id=1, source_target_pairs={{0,64},{32,96},{64,128},{96,160},{128,192},{160,224},{192,0},{224,... | collective-permute-start | bytes 196616 | tf_op jit(solution)/shard_map/ppermute | solution.py:429
  50.1 9.8 %collective-permute-start = (bf16[128,256]{1,0:T(8,128)(2,1)S(1)}, bf16[128,256]{1,0:T(8,128)(2,1)S(1)}, u32[]{:S(2)}, u32[]{:S(2)}) collective-permute-start(bf16[128,256]{1,0:T(8,128)(2,1)S(1)} %copy-done.2), channel_id=1, source_target_pairs={{0,32},{32,64},{64,96},{96,128},{128,160},{160,192},{192,224},{224... | collective-permute-start | bytes 196616 | tf_op jit(solution)/shard_map/ppermute | solution.py:429
  65.7 33.3 %all-to-all-start.1 = ((bf16[32,128,256]{2,1,0:T(8,128)(2,1)}), bf16[32,128,256]{2,1,0:T(8,128)(2,1)}, u32[]{:S(2)}, u32[]{:S(2)}) async-start(bf16[32,128,256]{2,1,0:T(8,128)(2,1)} %pick_g.1), calls=%async_computation.1 | async-start | bytes 4194304 | tf_op jit(solution)/shard_map/all_to_all | solution.py:424
  72.8 1.4 copy-start.3
  98.9 33.3 %all-to-all-start.4 = ((bf16[32,128,256]{2,1,0:T(8,128)(2,1)}), bf16[32,128,256]{2,1,0:T(8,128)(2,1)}, u32[]{:S(2)}, u32[]{:S(2)}) async-start(bf16[32,128,256]{2,1,0:T(8,128)(2,1)} %copy-done.1), calls=%async_computation.4 | async-start | bytes 4194304 | tf_op jit(solution)/shard_map/all_to_all | solution.py:424
  106.1 1.4 copy-start.4
  107.5 1.4 copy-start.6
  108.9 1.4 copy-start.8
  132.2 35.5 %all-to-all-start.3 = ((bf16[32,128,256]{2,1,0:T(8,128)(2,1)}), bf16[32,128,256]{2,1,0:T(8,128)(2,1)S(1)}, u32[]{:S(2)}, u32[]{:S(2)}) async-start(bf16[32,128,256]{2,1,0:T(8,128)(2,1)} %copy-done), calls=%async_computation.3 | async-start | bytes 4194304 | tf_op jit(solution)/shard_map/all_to_all | solution.py:424
  141.9 8.1 %collective-permute-start.7 = (bf16[128,256]{1,0:T(8,128)(2,1)S(1)}, bf16[128,256]{1,0:T(8,128)(2,1)S(1)}, u32[]{:S(2)}, u32[]{:S(2)}) collective-permute-start(bf16[128,256]{1,0:T(8,128)(2,1)S(1)} %get-tuple-element.69), channel_id=1, source_target_pairs={{0,32},{32,64},{64,96},{96,128},{128,160},{160,192},{192,224},{224... | collective-permute-start | bytes 196616 | tf_op jit(solution)/shard_map/ppermute | solution.py:429
  142.7 12.6 %collective-permute-start.8 = (bf16[128,256]{1,0:T(8,128)(2,1)S(1)}, bf16[128,256]{1,0:T(8,128)(2,1)S(1)}, u32[]{:S(2)}, u32[]{:S(2)}) collective-permute-start(bf16[128,256]{1,0:T(8,128)(2,1)S(1)} %get-tuple-element.70), channel_id=1, source_target_pairs={{0,64},{32,96},{64,128},{96,160},{128,192},{160,224},{192,0},{224,... | collective-permute-start | bytes 196616 | tf_op jit(solution)/shard_map/ppermute | solution.py:429
  142.8 12.6 %collective-permute-start.9 = (bf16[128,256]{1,0:T(8,128)(2,1)S(1)}, bf16[128,256]{1,0:T(8,128)(2,1)S(1)}, u32[]{:S(2)}, u32[]{:S(2)}) collective-permute-start(bf16[128,256]{1,0:T(8,128)(2,1)S(1)} %get-tuple-element.71), channel_id=1, source_target_pairs={{0,96},{32,128},{64,160},{96,192},{128,224},{160,0},{192,32},{224,... | collective-permute-start | bytes 196616 | tf_op jit(solution)/shard_map/ppermute | solution.py:429
  145.4 9.9 %collective-permute-start.10 = (bf16[128,256]{1,0:T(8,128)(2,1)S(1)}, bf16[128,256]{1,0:T(8,128)(2,1)S(1)}, u32[]{:S(2)}, u32[]{:S(2)}) collective-permute-start(bf16[128,256]{1,0:T(8,128)(2,1)S(1)} %get-tuple-element.72), channel_id=1, source_target_pairs={{0,128},{32,160},{64,192},{96,224},{128,0},{160,32},{192,64},{224,... | collective-permute-start | bytes 196616 | tf_op jit(solution)/shard_map/ppermute | solution.py:429
  148.8 9.3 %collective-permute-start.11 = (bf16[128,256]{1,0:T(8,128)(2,1)S(1)}, bf16[128,256]{1,0:T(8,128)(2,1)S(1)}, u32[]{:S(2)}, u32[]{:S(2)}) collective-permute-start(bf16[128,256]{1,0:T(8,128)(2,1)S(1)} %get-tuple-element.73), channel_id=1, source_target_pairs={{0,160},{32,192},{64,224},{96,0},{128,32},{160,64},{192,96},{224,1... | collective-permute-start | bytes 196616 | tf_op jit(solution)/shard_map/ppermute | solution.py:429
  150.0 11.3 %collective-permute-start.12 = (bf16[128,256]{1,0:T(8,128)(2,1)S(1)}, bf16[128,256]{1,0:T(8,128)(2,1)S(1)}, u32[]{:S(2)}, u32[]{:S(2)}) collective-permute-start(bf16[128,256]{1,0:T(8,128)(2,1)S(1)} %get-tuple-element.74), channel_id=1, source_target_pairs={{0,192},{32,224},{64,0},{96,32},{128,64},{160,96},{192,128},{224,1... | collective-permute-start | bytes 196616 | tf_op jit(solution)/shard_map/ppermute | solution.py:429
  155.3 6.9 %collective-permute-start.13 = (bf16[128,256]{1,0:T(8,128)(2,1)S(1)}, bf16[128,256]{1,0:T(8,128)(2,1)S(1)}, u32[]{:S(2)}, u32[]{:S(2)}) collective-permute-start(bf16[128,256]{1,0:T(8,128)(2,1)S(1)} %get-tuple-element.75), channel_id=1, source_target_pairs={{0,224},{32,0},{64,32},{96,64},{128,96},{160,128},{192,160},{224,1... | collective-permute-start | bytes 196616 | tf_op jit(solution)/shard_map/ppermute | solution.py:429
  162.3 5.4 %collective-permute-start.14 = (bf16[16,256]{1,0:T(8,128)(2,1)S(1)}, bf16[16,256]{1,0:T(8,128)(2,1)S(1)}, u32[]{:S(2)}, u32[]{:S(2)}) collective-permute-start(bf16[16,256]{1,0:T(8,128)(2,1)S(1)} %get-tuple-element.77), channel_id=1, source_target_pairs={{0,1},{1,2},{2,3},{3,4},{4,5},{5,6},{6,7},{7,0},{8,9},{9,10},{10,1... | collective-permute-start | bytes 24584 | tf_op jit(solution)/shard_map/ppermute | solution.py:429
  162.6 5.2 %collective-permute-start.15 = (bf16[16,256]{1,0:T(8,128)(2,1)S(1)}, bf16[16,256]{1,0:T(8,128)(2,1)S(1)}, u32[]{:S(2)}, u32[]{:S(2)}) collective-permute-start(bf16[16,256]{1,0:T(8,128)(2,1)S(1)} %get-tuple-element.78), channel_id=1, source_target_pairs={{0,2},{1,3},{2,4},{3,5},{4,6},{5,7},{6,0},{7,1},{8,10},{9,11},{10,... | collective-permute-start | bytes 24584 | tf_op jit(solution)/shard_map/ppermute | solution.py:429
  165.4 4.9 %collective-permute-start.16 = (bf16[16,256]{1,0:T(8,128)(2,1)S(1)}, bf16[16,256]{1,0:T(8,128)(2,1)S(1)}, u32[]{:S(2)}, u32[]{:S(2)}) collective-permute-start(bf16[16,256]{1,0:T(8,128)(2,1)S(1)} %get-tuple-element.79), channel_id=1, source_target_pairs={{0,3},{1,4},{2,5},{3,6},{4,7},{5,0},{6,1},{7,2},{8,11},{9,12},{10,... | collective-permute-start | bytes 24584 | tf_op jit(solution)/shard_map/ppermute | solution.py:429
  171.9 25.9 %all-to-all-start.5 = ((bf16[64,16,256]{2,1,0:T(8,128)(2,1)}), bf16[64,16,256]{2,1,0:T(8,128)(2,1)S(1)}, u32[]{:S(2)}, u32[]{:S(2)}) async-start(bf16[64,16,256]{2,1,0:T(8,128)(2,1)} %join_in.1), calls=%async_computation.5 | async-start | bytes 1048576 | tf_op jit(solution)/shard_map/all_to_all | solution.py:424
  182.3 6.0 %collective-permute-start.17 = (bf16[16,256]{1,0:T(8,128)(2,1)S(1)}, bf16[16,256]{1,0:T(8,128)(2,1)S(1)}, u32[]{:S(2)}, u32[]{:S(2)}) collective-permute-start(bf16[16,256]{1,0:T(8,128)(2,1)S(1)} %get-tuple-element.89), channel_id=1, source_target_pairs={{0,4},{1,5},{2,6},{3,7},{4,0},{5,1},{6,2},{7,3},{8,12},{9,13},{10,... | collective-permute-start | bytes 24584 | tf_op jit(solution)/shard_map/ppermute | solution.py:429
  183.0 6.2 %collective-permute-start.18 = (bf16[16,256]{1,0:T(8,128)(2,1)S(1)}, bf16[16,256]{1,0:T(8,128)(2,1)S(1)}, u32[]{:S(2)}, u32[]{:S(2)}) collective-permute-start(bf16[16,256]{1,0:T(8,128)(2,1)S(1)} %get-tuple-element.90), channel_id=1, source_target_pairs={{0,5},{1,6},{2,7},{3,0},{4,1},{5,2},{6,3},{7,4},{8,13},{9,14},{10,... | collective-permute-start | bytes 24584 | tf_op jit(solution)/shard_map/ppermute | solution.py:429
  183.4 7.8 %collective-permute-start.19 = (bf16[16,256]{1,0:T(8,128)(2,1)S(1)}, bf16[16,256]{1,0:T(8,128)(2,1)S(1)}, u32[]{:S(2)}, u32[]{:S(2)}) collective-permute-start(bf16[16,256]{1,0:T(8,128)(2,1)S(1)} %get-tuple-element.91), channel_id=1, source_target_pairs={{0,6},{1,7},{2,0},{3,1},{4,2},{5,3},{6,4},{7,5},{8,14},{9,15},{10,... | collective-permute-start | bytes 24584 | tf_op jit(solution)/shard_map/ppermute | solution.py:429
  188.3 7.3 %collective-permute-start.20 = (bf16[16,256]{1,0:T(8,128)(2,1)S(1)}, bf16[16,256]{1,0:T(8,128)(2,1)S(1)}, u32[]{:S(2)}, u32[]{:S(2)}) collective-permute-start(bf16[16,256]{1,0:T(8,128)(2,1)S(1)} %get-tuple-element.92), channel_id=1, source_target_pairs={{0,7},{1,0},{2,1},{3,2},{4,3},{5,4},{6,5},{7,6},{8,15},{9,8},{10,9... | collective-permute-start | bytes 24584 | tf_op jit(solution)/shard_map/ppermute | solution.py:429
  (6 other events, 7.5 us)

commit v5 on v3

--- a/solution.py
+++ b/solution.py
@@ -11,6 +11,7 @@
 BF16 = jnp.bfloat16
 F32 = jnp.float32
 CAP = 16
+EARLY = (1, 2, 4, 6, 7)
 META = 16
 
 
@@ -34,26 +35,26 @@
     return pl.BlockSpec(shape, lambda *_: (0,) * len(shape))
 
 
-def route_kernel(col_ref, tok_ref, cot_ref, ids_ref, rw_ref, slot_ref, x_ref, g_ref):
+def route_kernel(col_ref, tok_ref, ids_ref, rw_ref, slot_ref, x_ref, slots_ref):
     ntok = tok_ref.shape[0]
-    g_ref[...] = cot_ref[...]
     table = jnp.broadcast_to(slot_ref[...], (8, slot_ref.shape[1]))
     slots = jnp.take_along_axis(table, ids_ref[...], axis=1, mode="promise_in_bounds").astype(F32)
+    slots_ref[...] = slots
     w = rw_ref[...]
     hi = w.astype(BF16).astype(F32)
     rest = w - hi
     mid = rest.astype(BF16).astype(F32)
     low = rest - mid
-    left = jnp.concatenate([slots, mid], axis=0)
-    right = jnp.concatenate([hi, low], axis=0)
-    tok, left, right = tok_ref[...], left.astype(BF16), right.astype(BF16)
+    tok = tok_ref[...]
+    left = jnp.concatenate([slots, mid], axis=0).astype(BF16)
+    right = jnp.concatenate([hi, low], axis=0).astype(BF16)
     for z in range(x_ref.shape[0]):
         x_ref[z, 0:ntok, :] = tok
         x_ref[z, ntok : ntok + META, 0:128] = left
         x_ref[z, ntok : ntok + META, 128:256] = right
 
 
-def route(col, tokens, cotangent, ids_t, rw_t, slot_row):
+def route(col, tokens, ids_t, rw_t, slot_row):
     ntok, width = tokens.shape
     cut = width // 8
     return pl.pallas_call(
@@ -62,21 +63,20 @@
             num_scalar_prefetch=1,
             grid=(1,),
             in_specs=[
-                pl.BlockSpec((ntok, cut), lambda i, c: (0, c[0])),
                 pl.BlockSpec((ntok, cut), lambda i, c: (0, c[0])),
                 whole(ids_t.shape),
                 whole(rw_t.shape),
                 whole(slot_row.shape),
             ],
-            out_specs=[whole((8, ntok + META, cut)), whole((ntok, cut))],
+            out_specs=[whole((8, ntok + META, cut)), whole(ids_t.shape)],
         ),
         out_shape=[
             jax.ShapeDtypeStruct((8, ntok + META, cut), BF16),
-            jax.ShapeDtypeStruct((ntok, cut), BF16),
+            jax.ShapeDtypeStruct(ids_t.shape, F32),
         ],
         compiler_params=params(60),
         name="route",
-    )(col, tokens, cotangent, ids_t, rw_t, slot_row)
+    )(col, tokens, ids_t, rw_t, slot_row)
 
 
 def one_hot(place):
@@ -103,26 +103,33 @@
         send_ref[2 * l + 1] = part
 
 
-def pick_x_kernel(z_ref, x_ref, send_ref, place_ref, weight_ref):
-    ntok = x_ref.shape[1] - META
-    first = (z_ref[0] * 16).astype(F32)
-    local = lax.broadcasted_iota(jnp.int32, (16, ntok), 0).astype(F32) + first
+def places(slots, w, local, earlier):
+    chosen = jnp.zeros(local.shape, F32)
+    weight = jnp.zeros(local.shape, F32)
+    for k in range(8):
+        same = local == slots[k : k + 1, :]
+        chosen = jnp.where(same, 1.0, chosen)
+        weight = jnp.where(same, w[k : k + 1, :], weight)
+    before = nn(chosen.astype(BF16), earlier)
+    return jnp.where(chosen > 0.0, before, -1.0), weight
+
+
+def earlier_tokens(ntok):
     row = lax.broadcasted_iota(jnp.int32, (ntok, ntok), 0)
     column = lax.broadcasted_iota(jnp.int32, (ntok, ntok), 1)
-    earlier = jnp.where(row < column, 1.0, 0.0).astype(BF16)
+    return jnp.where(row < column, 1.0, 0.0).astype(BF16)
+
+
+def pick_x_kernel(at_ref, x_ref, send_ref, place_ref, weight_ref):
+    ntok = x_ref.shape[1] - META
+    first = (at_ref[0] * 16).astype(F32)
+    local = lax.broadcasted_iota(jnp.int32, (16, ntok), 0).astype(F32) + first
+    earlier = earlier_tokens(ntok)
     for b in range(x_ref.shape[0]):
         left = x_ref[b, ntok : ntok + META, 0:128].astype(F32)
         right = x_ref[b, ntok : ntok + META, 128:256].astype(F32)
-        slots = left[0:8]
         w = right[0:8] + left[8:16] + right[8:16]
-        chosen = jnp.zeros((16, ntok), F32)
-        weight = jnp.zeros((16, ntok), F32)
-        for k in range(8):
-            same = local == slots[k : k + 1, :]
-            chosen = jnp.where(same, 1.0, chosen)
-            weight = jnp.where(same, w[k : k + 1, :], weight)
-        before = nn(chosen.astype(BF16), earlier)
-        place = jnp.where(chosen > 0.0, before, -1.0)
+        place, weight = places(left[0:8], w, local, earlier)
         place_ref[b] = place
         weight_ref[b] = weight
         rows = nn(as_bf16(one_hot(place)), x_ref[b, 0:ntok, :])
@@ -154,34 +161,72 @@
     )(zs, x_all)
 
 
-def pick_g_kernel(z_ref, *refs):
-    g_refs, (place_ref, weight_ref, send_ref) = refs[:8], refs[8:]
-    for shift, g_ref in enumerate(g_refs):
-        block = lax.rem(z_ref[0] + 8 - shift, 8)
-        hot = one_hot(place_ref[block])
-        rows = nn(as_bf16(hot), g_ref[...]) * row_weights(hot, weight_ref[block])
-        put_rows(rows.astype(BF16), send_ref.at[:, pl.ds(pl.multiple_of(block * CAP, CAP), CAP), :])
-
-
-def pick_g(zs, g_blocks, place, weight):
-    blocks = place.shape[0]
-    ntok, cut = g_blocks[0].shape
+ROUTES = ((0, 0), (1, 0), (2, 0), (2, 1), (3, 0), (3, 1))
+
+
+def pick_g_kernel(at_ref, cot_ref, slots_ref, rw_ref, *send_refs):
+    ntok, width = cot_ref.shape
+    earlier = earlier_tokens(ntok)
+    planes = lax.broadcasted_iota(jnp.int32, (8, ntok), 0)
+    for (away, over), send_ref in zip(ROUTES, send_refs):
+        local = planes * 16 + ((at_ref[1] ^ away) * 4 + ((at_ref[2] // 2) ^ (2 * over)))
+        place, weight = places(slots_ref[...], rw_ref[...], local.astype(F32), earlier)
+        hot = one_hot(place)
+        pick, scale = as_bf16(hot), row_weights(hot, weight)
+        begin = over * (width // 2)
+        for c in range(0, send_ref.shape[1], 512):
+            rows = nn(pick, cot_ref[:, begin + c : begin + c + 512]) * scale
+            send_ref[:, c : c + 512] = rows.astype(BF16)
+
+
+def pick_g(at, cotangent, slots, rw_t):
+    ntok, width = cotangent.shape
+    shapes = [(8 * CAP, width if away < 2 else width // 2) for away, _ in ROUTES]
     return pl.pallas_call(
         pick_g_kernel,
         grid_spec=pltpu.PrefetchScalarGridSpec(
             num_scalar_prefetch=1,
             grid=(1,),
-            in_specs=[whole((ntok, cut))] * 8 + [whole(place.shape), whole(weight.shape)],
-            out_specs=whole((32, blocks * CAP, cut)),
-        ),
-        out_shape=jax.ShapeDtypeStruct((32, blocks * CAP, cut), BF16),
+            in_specs=[whole(cotangent.shape), whole(slots.shape), whole(rw_t.shape)],
+            out_specs=[whole(shape) for shape in shapes],
+        ),
+        out_shape=[jax.ShapeDtypeStruct(shape, BF16) for shape in shapes],
         compiler_params=params(),
         name="pick_g",
-    )(zs, *g_blocks, place, weight)
+    )(at, cotangent, slots, rw_t)
+
+
+def turn_g_kernel(at_ref, *refs):
+    given, send_refs = refs[: len(ROUTES)], refs[len(ROUTES) :]
+    for shift, send_ref in enumerate(send_refs):
+        to = pl.ds(pl.multiple_of(lax.rem(at_ref[0] + shift, 8) * CAP, CAP), CAP)
+        for (away, over), rows in zip(ROUTES, given):
+            begin, count = over * (send_ref.shape[1] // 2), rows.shape[1]
+            send_ref[away * CAP : (away + 1) * CAP, begin : begin + count] = rows[to, :]
+
+
+def turn_g(at, given):
+    width = given[0].shape[1]
+    return pl.pallas_call(
+        turn_g_kernel,
+        grid_spec=pltpu.PrefetchScalarGridSpec(
+            num_scalar_prefetch=1,
+            grid=(1,),
+            in_specs=[whole(a.shape) for a in given],
+            out_specs=[whole((4 * CAP, width))] * 8,
+        ),
+        out_shape=[pltpu.HBM((4 * CAP, width), BF16)] * 8,
+        compiler_params=params(),
+        name="turn_g",
+    )(at, *given)
 
 
 def chunk(ref, e):
     return jnp.concatenate([ref[q * 8 + e] for q in range(4)], axis=0)
+
+
+def columns(ref, at):
+    return jnp.concatenate([ref[q, :, at] for q in range(4)], axis=0)
 
 
 def put_chunk(ref, e, rows):
@@ -231,14 +276,18 @@
     )(x_rows, wg, wu, wd)
 
 
-def backward_kernel(
-    g_ref, gate_ref, up_ref, wg_ref, wu_ref, wd_ref, in_ref, dgate_ref, dup_ref, back_ref
-):
-    cut = g_ref.shape[2]
+def backward_kernel(at_ref, *refs):
+    parts, (gate_ref, up_ref, wg_ref, wu_ref, wd_ref) = refs[:8], refs[8:13]
+    g_ref, in_ref, dgate_ref, dup_ref, back_ref = refs[13:]
+    cut = in_ref.shape[2]
+    for shift, part in enumerate(parts):
+        rows = pl.ds(pl.multiple_of(lax.rem(at_ref[0] + 8 - shift, 8) * CAP, CAP), CAP)
+        for away in range(4):
+            g_ref[at_ref[1] ^ away, rows, :] = part[away * CAP : (away + 1) * CAP, :]
 
     def first(e, _):
         at = pl.ds(pl.multiple_of(e * cut, cut), cut)
-        back_ref[...] += nt(chunk(g_ref, e), wd_ref[0, :, at])
+        back_ref[...] += nt(columns(g_ref, at), wd_ref[0, :, at])
         return 0
 
     back_ref[...] = jnp.zeros_like(back_ref)
@@ -257,22 +306,35 @@
     lax.fori_loop(0, 8, second, 0)
 
 
-def backward(g_rows, gate, up, wg, wu, wd):
+def backward(at, parts, gate, up, wg, wu, wd):
     rows, ff = gate.shape
+    width = wd.shape[2]
     return pl.pallas_call(
         backward_kernel,
+        grid_spec=pltpu.PrefetchScalarGridSpec(
+            num_scalar_prefetch=1,
+            grid=(1,),
+            in_specs=[whole(a.shape) for a in (*parts, gate, up, wg, wu, wd)],
+            out_specs=[
+                whole((4, rows // 4, width)),
+                whole((32, rows // 4, width // 8)),
+                whole((rows, ff)),
+                whole((rows, ff)),
+            ],
+            scratch_shapes=[pltpu.VMEM((rows, ff), F32)],
+        ),
         out_shape=[
-            jax.ShapeDtypeStruct(g_rows.shape, BF16),
+            jax.ShapeDtypeStruct((4, rows // 4, width), BF16),
+            jax.ShapeDtypeStruct((32, rows // 4, width // 8), BF16),
             jax.ShapeDtypeStruct((rows, ff), BF16),
             jax.ShapeDtypeStruct((rows, ff), BF16),
         ],
-        scratch_shapes=[pltpu.VMEM((rows, ff), F32)],
-        compiler_params=params(),
+        compiler_params=params(36),
         cost_estimate=pl.CostEstimate(
-            flops=6 * rows * 2048 * ff, bytes_accessed=11 * 2**20, transcendentals=rows * ff
+            flops=6 * rows * 2048 * ff, bytes_accessed=13 * 2**20, transcendentals=rows * ff
         ),
         name="backward",
-    )(g_rows, gate, up, wg, wu, wd)
+    )(at, *parts, gate, up, wg, wu, wd)
 
 
 def grads_kernel(x_ref, g_ref, hidden_ref, dgate_ref, dup_ref, gg_ref, gu_ref, gd_ref):
@@ -283,7 +345,7 @@
         x = chunk(x_ref, e)
         gg_ref[0, at, :] = tn(x, dgate_ref[...]).astype(BF16)
         gu_ref[0, at, :] = tn(x, dup_ref[...]).astype(BF16)
-        gd_ref[0, :, at] = tn(hidden_ref[...], chunk(g_ref, e)).astype(BF16)
+        gd_ref[0, :, at] = tn(hidden_ref[...], columns(g_ref, at)).astype(BF16)
         return 0
 
     lax.fori_loop(0, 8, step, 0)
@@ -431,23 +493,44 @@
     ]
 
 
+def in_hbm(array):
+    return pltpu.with_memory_space_constraint(array, pltpu.HBM)
+
+
+def after(value, others):
+    return lax.optimization_barrier((value, others))[0]
+
+
+def cross(arrays):
+    return [arrays[0]] + [
+        lax.ppermute(
+            array, ("xl", "core", "xh"), [(i, i ^ (2 * away + over)) for i in range(8)]
+        )
+        for (away, over), array in zip(ROUTES[1:], arrays[1:])
+    ]
+
+
 def on_device(
     tokens, expert_ids, route_weight, expert_slot, gate_weight, up_weight, down_weight, cotangent
 ):
     col = lax.axis_index(EX).astype(jnp.int32).reshape(1)
     zs = lax.axis_index("z").astype(jnp.int32).reshape(1)
-    x_cut, g_cut = route(
-        col, tokens, cotangent, expert_ids.T, route_weight.T, expert_slot.reshape(1, -1)
+    at = jnp.concatenate([zs, lax.axis_index(("xl", "core")).astype(jnp.int32).reshape(1), col])
+    rw_t = route_weight.T
+    x_cut, slots = route(col, tokens, expert_ids.T, rw_t, expert_slot.reshape(1, -1))
+    x_all = swap(x_cut, ("z",))
+    g_crossed = cross(pick_g(at, cotangent, slots, rw_t))
+    x_all = after(x_all, g_crossed)
+    g_turned = turn_g(at, g_crossed)
+    g_parts = [in_hbm(part) for part in spread(g_turned, ("z",))]
+    x_send, place, weight = pick_x(zs, x_all)
+    x_rows = after(swap(x_send, PLANE), g_turned)
+    out_send, gate, up, hidden = forward(x_rows, gate_weight, up_weight, down_weight)
+    out_send = after(out_send, [g_parts[s] for s in EARLY])
+    out_back = in_hbm(swap(out_send, PLANE))
+    g_rows, in_send, dgate, dup = backward(
+        at, g_parts, gate, up, gate_weight, up_weight, down_weight
     )
-    x_all = swap(x_cut, ("z",))
-    x_send, place, weight = pick_x(zs, x_all)
-    g_blocks = spread([g_cut] * 8, ("z",))
-    x_rows = swap(x_send, PLANE)
-    g_send = pick_g(zs, g_blocks, place, weight)
-    g_rows = swap(g_send, PLANE)
-    out_send, gate, up, hidden = forward(x_rows, gate_weight, up_weight, down_weight)
-    out_back = pltpu.with_memory_space_constraint(swap(out_send, PLANE), pltpu.HBM)
-    in_send, dgate, dup = backward(g_rows, gate, up, gate_weight, up_weight, down_weight)
     weight_grads = grads(x_rows, g_rows, hidden, dgate, dup)
     in_send, weight_grads = lax.optimization_barrier((in_send, weight_grads))
     in_back = swap(in_send, PLANE)

time: 195 us -> 201 us (1.031)
  starting transfers between devices: 79.9 us -> 91.2 us
  waiting for transfers between devices: 64.5 us -> 55.9 us
  local copies, waits for them, and re-layouts: 13.1 us -> 17.4 us
    all_to_all x6 -> x5, waiting for transfers between devices: 40.2 us -> 9.48 us  [swap(): return lax.all_to_all(buffer, axes, split_axis=0, concat_axis=0, tiled=True)]
    ppermute x21, waiting for transfers between devices: 24.3 us -> 36.4 us  [spread(): lax.ppermute(arrays[shift], axes, [(i, (i + shift) % 8) for i in range(8)])]
    ppermute x0 -> x5, waiting for transfers between devices: none -> 10 us  [cross(): lax.ppermute(array, ('xl', 'core', 'xh'), [(i, i ^ 2 * away + over) for i...]
    ppermute x21, starting transfers between devices: 35.1 us -> 43.5 us  [spread(): lax.ppermute(arrays[shift], axes, [(i, (i + shift) % 8) for i in range(8)])]
    ppermute x0 -> x5, starting transfers between devices: none -> 4.56 us  [cross(): lax.ppermute(array, ('xl', 'core', 'xh'), [(i, i ^ 2 * away + over) for i...]
    unnamed x22 -> x46, local copies, waits for them, and re-layouts: 13.1 us -> 17.4 us
    pallas_call x1 -> x2, Pallas kernels: 8.18 us -> 10.8 us  [the longest x1 8.79 us: backward(): pl.pallas_call(backward_kernel, grid_spec=pltpu.PrefetchScalarGridSpec(nu...]
    pallas_call x1, Pallas kernels: 8.74 us -> 6.62 us  [grads(): pl.pallas_call(grads_kernel, out_shape=[jax.ShapeDtypeStruct((1, width, f...]
  transfers between devices with their start and end apart: 27 -> 31, of which waited for: 16 -> 16; matrix products, arithmetic and copies ran while one was open for 0% -> 0% of each run, Pallas kernels for 15% -> 14%
where the time goes in v5:
time: 201 us; the launch traced here: 200 us
  starting transfers between devices  91.2 us (45%)
  waiting for transfers between devices  55.9 us (28%)
  Pallas kernels  34.8 us (17%)
  local copies, waits for them, and re-layouts  17.4 us (9%)
    ppermute x21, starting transfers between devices, spread(): lax.ppermute(arrays[shift], axes, [(i, (i + shift) % 8) for i in range(8)])  43.5 us
    all_to_all x5, starting transfers between devices, swap(): return lax.all_to_all(buffer, axes, split_axis=0, concat_axis=0, tiled=True)  43.1 us
    ppermute x21, waiting for transfers between devices, spread(): lax.ppermute(arrays[shift], axes, [(i, (i + shift) % 8) for i in range(8)])  36.4 us
    unnamed x46, local copies, waits for them, and re-layouts  17.4 us
    ppermute x5, waiting for transfers between devices, cross(): lax.ppermute(array, ('xl', 'core', 'xh'), [(i, i ^ 2 * away + over) for i...  10 us
    all_to_all x5, waiting for transfers between devices, swap(): return lax.all_to_all(buffer, axes, split_axis=0, concat_axis=0, tiled=True)  9.48 us
    pallas_call x1, Pallas kernels, backward(): pl.pallas_call(backward_kernel, grid_spec=pltpu.PrefetchScalarGridSpec(nu...  8.79 us
    pallas_call x1, Pallas kernels, grads(): pl.pallas_call(grads_kernel, out_shape=[jax.ShapeDtypeStruct((1, width, f...  6.62 us
  transfers between devices with their start and end apart: 31, of which 16 were waited for; matrix products, arithmetic and copies ran while one was open for 0% of the time, Pallas kernels for 14%

profile of v5, /device:TPU:28, one launch (start us, length us, event | category | flops | bytes accessed | tf_op | source)
XLA Modules:
  0.0 200.3 jit_solution(17682213523909919061)
XLA Ops:
  2.5 8.5 %all-to-all-start = ((bf16[8,144,256]{2,1,0:T(8,128)(2,1)}), bf16[8,144,256]{2,1,0:T(8,128)(2,1)S(1)}, u32[]{:S(2)}, u32[]{:S(2)}) async-start(bf16[8,144,256]{2,1,0:T(8,128)(2,1)} %get-tuple-element.84), calls=%async_computation | async-start | bytes 1179648 | tf_op jit(solution)/shard_map/all_to_all | solution.py:486
  12.4 2.0 %pick_g.1 = (bf16[128,2048]{1,0:T(8,128)(2,1)S(1)}, bf16[128,2048]{1,0:T(8,128)(2,1)S(1)}, bf16[128,1024]{1,0:T(8,128)(2,1)S(1)}, bf16[128,1024]{1,0:T(8,128)(2,...) custom-call(s32[3]{0:T(128)S(1)} %pad_add_fusion.at_ref, bf16[128,2048]{1,0:T(8,128)(2,1)S(1)} %copy-done.2, ...), custom_call_target="tpu_custom_call" | custom-call | tf_op jit(solution)/shard_map/pick_g/pallas_call | solution.py:185
  19.0 4.7 %collective-permute-done.1.refs_2_ = bf16[128,1024]{1,0:T(8,128)(2,1)S(1)} collective-permute-done((bf16[128,1024]{1,0:T(8,128)(2,1)S(1)}, bf16[128,1024]{1,0:T(8,128)(2,1)S(1)}, u32[]{:S(2)}, u32[]{:S(2)}) %collective-permute-start.1) | collective-permute-done | bytes 262176 | tf_op jit(solution)/shard_map/ppermute | solution.py:506
  25.0 3.4 %collective-permute-done.3.refs_4_ = bf16[128,1024]{1,0:T(8,128)(2,1)S(1)} collective-permute-done((bf16[128,1024]{1,0:T(8,128)(2,1)S(1)}, bf16[128,1024]{1,0:T(8,128)(2,1)S(1)}, u32[]{:S(2)}, u32[]{:S(2)}) %collective-permute-start.3) | collective-permute-done | bytes 262176 | tf_op jit(solution)/shard_map/ppermute | solution.py:506
  29.8 2.3 %pick_x.1 = (bf16[32,128,256]{2,1,0:T(8,128)(2,1)}, f32[8,16,128]{2,1,0:T(8,128)S(1)}, f32[8,16,128]{2,1,0:T(8,128)S(1)}) custom-call(s32[1]{0:T(128)} %bitcast.1.at_ref.z_ref, bf16[8,144,256]{2,1,0:T(8,128)(2,1)S(1)} %all-to-all-done.x_ref), custom_call_target="tpu_custom_call" | custom-call | tf_op jit(solution)/shard_map/pick_x/pallas_call | solution.py:142
  32.1 7.9 %all-to-all-start.1 = ((bf16[32,128,256]{2,1,0:T(8,128)(2,1)}), bf16[32,128,256]{2,1,0:T(8,128)(2,1)S(1)}, u32[]{:S(2)}, u32[]{:S(2)}) async-start(bf16[32,128,256]{2,1,0:T(8,128)(2,1)} %get-tuple-element.86), calls=%async_computation.1 | async-start | bytes 4194304 | tf_op jit(solution)/shard_map/all_to_all | solution.py:486
  44.9 2.0 %collective-permute-start.5 = (bf16[64,2048]{1,0:T(8,128)(2,1)}, bf16[64,2048]{1,0:T(8,128)(2,1)}, u32[]{:S(2)}, u32[]{:S(2)}) collective-permute-start(bf16[64,2048]{1,0:T(8,128)(2,1)} %get-tuple-element.77), channel_id=1, source_target_pairs={{0,32},{32,64},{64,96},{96,128},{128,160},{160,192},{192,224},{224... | collective-permute-start | bytes 786440 | tf_op jit(solution)/shard_map/ppermute | solution.py:491
  46.9 2.4 %collective-permute-start.6 = (bf16[64,2048]{1,0:T(8,128)(2,1)}, bf16[64,2048]{1,0:T(8,128)(2,1)}, u32[]{:S(2)}, u32[]{:S(2)}) collective-permute-start(bf16[64,2048]{1,0:T(8,128)(2,1)} %get-tuple-element.78), channel_id=1, source_target_pairs={{0,64},{32,96},{64,128},{96,160},{128,192},{160,224},{192,0},{224,... | collective-permute-start | bytes 786440 | tf_op jit(solution)/shard_map/ppermute | solution.py:491
  49.3 2.7 %collective-permute-start.8 = (bf16[64,2048]{1,0:T(8,128)(2,1)}, bf16[64,2048]{1,0:T(8,128)(2,1)}, u32[]{:S(2)}, u32[]{:S(2)}) collective-permute-start(bf16[64,2048]{1,0:T(8,128)(2,1)} %get-tuple-element.80), channel_id=1, source_target_pairs={{0,128},{32,160},{64,192},{96,224},{128,0},{160,32},{192,64},{224,... | collective-permute-start | bytes 786440 | tf_op jit(solution)/shard_map/ppermute | solution.py:491
  52.0 3.6 %collective-permute-start.10 = (bf16[64,2048]{1,0:T(8,128)(2,1)}, bf16[64,2048]{1,0:T(8,128)(2,1)}, u32[]{:S(2)}, u32[]{:S(2)}) collective-permute-start(bf16[64,2048]{1,0:T(8,128)(2,1)} %get-tuple-element.82), channel_id=1, source_target_pairs={{0,192},{32,224},{64,0},{96,32},{128,64},{160,96},{192,128},{224,1... | collective-permute-start | bytes 786440 | tf_op jit(solution)/shard_map/ppermute | solution.py:491
  57.0 9.1 %all-to-all-done.1.x_ref = bf16[32,128,256]{2,1,0:T(8,128)(2,1)S(1)} async-done(((bf16[32,128,256]{2,1,0:T(8,128)(2,1)}), bf16[32,128,256]{2,1,0:T(8,128)(2,1)S(1)}, u32[]{:S(2)}, u32[]{:S(2)}) %all-to-all-start.1) | async-done | bytes 2097184 | tf_op jit(solution)/shard_map/all_to_all | solution.py:486
  70.4 6.2 %forward.1 = (bf16[32,128,256]{2,1,0:T(8,128)(2,1)S(1)}, f32[512,384]{1,0:T(8,128)S(1)}, f32[512,384]{1,0:T(8,128)S(1)}, bf16[512,384]{1,0:T(8,128)(2,1)S(1)}) custom-call(bf16[32,128,256]{2,1,0:T(8,128)(2,1)S(1)} %all-to-all-done.1.x_ref, bf16[1,2048,384]{2,1,0:T(8,128)(2,1)S(1)} %copy-done.11, bf16[1,2048,384]{2,1,0:T(8,128)(2,1)S(1)} %copy-done.13, ...), custom_call_target="tpu_custom_call" | custom-call | flops 2415919104 | bytes 11534336 | tf_op jit(solution)/shard_map/forward/pallas_call | solution.py:263
  78.8 2.0 collective-permute-done.11.refs_7_
  80.8 7.4 %all-to-all-start.3 = ((bf16[32,128,256]{2,1,0:T(8,128)(2,1)}), bf16[32,128,256]{2,1,0:T(8,128)(2,1)}, u32[]{:S(2)}, u32[]{:S(2)}) async-start(bf16[32,128,256]{2,1,0:T(8,128)(2,1)} %copy-done.1), calls=%async_computation.3 | async-start | bytes 4194304 | tf_op jit(solution)/shard_map/all_to_all | solution.py:486
  88.2 5.1 %collective-permute-start.7 = (bf16[64,2048]{1,0:T(8,128)(2,1)}, bf16[64,2048]{1,0:T(8,128)(2,1)S(1)}, u32[]{:S(2)}, u32[]{:S(2)}) collective-permute-start(bf16[64,2048]{1,0:T(8,128)(2,1)} %get-tuple-element.79), channel_id=1, source_target_pairs={{0,96},{32,128},{64,160},{96,192},{128,224},{160,0},{192,32},{224,... | collective-permute-start | bytes 786440 | tf_op jit(solution)/shard_map/ppermute | solution.py:491
  93.4 17.6 %collective-permute-done.7.refs_3_ = bf16[64,2048]{1,0:T(8,128)(2,1)S(1)} collective-permute-done((bf16[64,2048]{1,0:T(8,128)(2,1)}, bf16[64,2048]{1,0:T(8,128)(2,1)S(1)}, u32[]{:S(2)}, u32[]{:S(2)}) %collective-permute-start.7) | collective-permute-done | bytes 262176 | tf_op jit(solution)/shard_map/ppermute | solution.py:491
  118.3 8.8 %backward.1 = (bf16[4,128,2048]{2,1,0:T(8,128)(2,1)S(1)}, bf16[32,128,256]{2,1,0:T(8,128)(2,1)S(1)}, bf16[512,384]{1,0:T(8,128)(2,1)S(1)}, bf16[512,384]{1,0:T(8,128)(2,1)S(1)}) custom-call(s32[3]{0:T(128)S(1)} %pad_add_fusion.at_ref, bf16[64,2048]{1,0:T(8,128)(2,1)} %get-tuple-element.76.refs_0_, bf16[64,2048]{1,0:T(8,128)(2,1)} %collective-permute-done.5.refs_1_, ...), custom_call_target="tpu_custom_call" | custom-call | flops 2415919104 | bytes 13631488 | tf_op jit(solution)/shard_map/backward/pallas_call | solution.py:312
  127.1 6.6 %grads.1 = (bf16[1,2048,384]{2,1,0:T(8,128)(2,1)}, bf16[1,2048,384]{2,1,0:T(8,128)(2,1)}, bf16[1,384,2048]{2,1,0:T(8,128)(2,1)}) custom-call(bf16[32,128,256]{2,1,0:T(8,128)(2,1)S(1)} %all-to-all-done.1.x_ref, bf16[4,128,2048]{2,1,0:T(8,128)(2,1)S(1)} %get-tuple-element.91.g_ref, bf16[512,384]{1,0:T(8,128)(2,1)S(1)} %copy-done.20, ...), custom_call_target="tpu_custom_call" | custom-call | flops 2415919104 | bytes 10485760 | tf_op jit(solution)/shard_map/grads/pallas_call | solution.py:357
  133.7 7.4 %all-to-all-start.2 = ((bf16[32,128,256]{2,1,0:T(8,128)(2,1)}), bf16[32,128,256]{2,1,0:T(8,128)(2,1)S(1)}, u32[]{:S(2)}, u32[]{:S(2)}) async-start(bf16[32,128,256]{2,1,0:T(8,128)(2,1)} %copy-done), calls=%async_computation.2 | async-start | bytes 4194304 | tf_op jit(solution)/shard_map/all_to_all | solution.py:486
  141.1 2.6 %join_out.1 = (f32[128,256]{1,0:T(8,128)S(1)}, bf16[128,256]{1,0:T(8,128)(2,1)S(1)}, bf16[128,256]{1,0:T(8,128)(2,1)S(1)}, bf16[128,256]{1,0:T(8,128)(2,1)S(1)},...) custom-call(s32[1]{0:T(128)} %bitcast.1.at_ref.z_ref, ...), custom_call_target="tpu_custom_call" | custom-call | tf_op jit(solution)/shard_map/join_out/pallas_call | solution.py:395
  143.7 4.9 %collective-permute-start.12 = (bf16[128,256]{1,0:T(8,128)(2,1)S(1)}, bf16[128,256]{1,0:T(8,128)(2,1)S(1)}, u32[]{:S(2)}, u32[]{:S(2)}) collective-permute-start(bf16[128,256]{1,0:T(8,128)(2,1)S(1)} %get-tuple-element.104), channel_id=1, source_target_pairs={{0,32},{32,64},{64,96},{96,128},{128,160},{160,192},{192,224},{224... | collective-permute-start | bytes 196616 | tf_op jit(solution)/shard_map/ppermute | solution.py:491
  148.7 3.1 %collective-permute-start.14 = (bf16[128,256]{1,0:T(8,128)(2,1)S(1)}, bf16[128,256]{1,0:T(8,128)(2,1)S(1)}, u32[]{:S(2)}, u32[]{:S(2)}) collective-permute-start(bf16[128,256]{1,0:T(8,128)(2,1)S(1)} %get-tuple-element.106), channel_id=1, source_target_pairs={{0,96},{32,128},{64,160},{96,192},{128,224},{160,0},{192,32},{224,... | collective-permute-start | bytes 196616 | tf_op jit(solution)/shard_map/ppermute | solution.py:491
  151.8 2.9 %collective-permute-start.15 = (bf16[128,256]{1,0:T(8,128)(2,1)S(1)}, bf16[128,256]{1,0:T(8,128)(2,1)S(1)}, u32[]{:S(2)}, u32[]{:S(2)}) collective-permute-start(bf16[128,256]{1,0:T(8,128)(2,1)S(1)} %get-tuple-element.107), channel_id=1, source_target_pairs={{0,128},{32,160},{64,192},{96,224},{128,0},{160,32},{192,64},{224,... | collective-permute-start | bytes 196616 | tf_op jit(solution)/shard_map/ppermute | solution.py:491
  159.3 3.8 %collective-permute-done.15.refs_4_ = bf16[128,256]{1,0:T(8,128)(2,1)S(1)} collective-permute-done((bf16[128,256]{1,0:T(8,128)(2,1)S(1)}, bf16[128,256]{1,0:T(8,128)(2,1)S(1)}, u32[]{:S(2)}, u32[]{:S(2)}) %collective-permute-start.15) | collective-permute-done | bytes 65568 | tf_op jit(solution)/shard_map/ppermute | solution.py:491
  163.1 3.8 %collective-permute-done.17.refs_6_ = bf16[128,256]{1,0:T(8,128)(2,1)S(1)} collective-permute-done((bf16[128,256]{1,0:T(8,128)(2,1)S(1)}, bf16[128,256]{1,0:T(8,128)(2,1)S(1)}, u32[]{:S(2)}, u32[]{:S(2)}) %collective-permute-start.17) | collective-permute-done | bytes 65568 | tf_op jit(solution)/shard_map/ppermute | solution.py:491
  168.8 11.9 %all-to-all-start.4 = ((bf16[64,16,256]{2,1,0:T(8,128)(2,1)}), bf16[64,16,256]{2,1,0:T(8,128)(2,1)S(1)}, u32[]{:S(2)}, u32[]{:S(2)}) async-start(bf16[64,16,256]{2,1,0:T(8,128)(2,1)} %join_in.1), calls=%async_computation.4 | async-start | bytes 1048576 | tf_op jit(solution)/shard_map/all_to_all | solution.py:486
  181.3 2.5 %collective-permute-start.20 = (bf16[16,256]{1,0:T(8,128)(2,1)S(1)}, bf16[16,256]{1,0:T(8,128)(2,1)S(1)}, u32[]{:S(2)}, u32[]{:S(2)}) collective-permute-start(bf16[16,256]{1,0:T(8,128)(2,1)S(1)} %get-tuple-element.121), channel_id=1, source_target_pairs={{0,2},{1,3},{2,4},{3,5},{4,6},{5,7},{6,0},{7,1},{8,10},{9,11},{10,... | collective-permute-start | bytes 24584 | tf_op jit(solution)/shard_map/ppermute | solution.py:491
  183.8 2.4 %collective-permute-start.21 = (bf16[16,256]{1,0:T(8,128)(2,1)S(1)}, bf16[16,256]{1,0:T(8,128)(2,1)S(1)}, u32[]{:S(2)}, u32[]{:S(2)}) collective-permute-start(bf16[16,256]{1,0:T(8,128)(2,1)S(1)} %get-tuple-element.122), channel_id=1, source_target_pairs={{0,3},{1,4},{2,5},{3,6},{4,7},{5,0},{6,1},{7,2},{8,11},{9,12},{10,... | collective-permute-start | bytes 24584 | tf_op jit(solution)/shard_map/ppermute | solution.py:491
  186.8 3.2 %collective-permute-start.23 = (bf16[16,256]{1,0:T(8,128)(2,1)S(1)}, bf16[16,256]{1,0:T(8,128)(2,1)S(1)}, u32[]{:S(2)}, u32[]{:S(2)}) collective-permute-start(bf16[16,256]{1,0:T(8,128)(2,1)S(1)} %get-tuple-element.124), channel_id=1, source_target_pairs={{0,5},{1,6},{2,7},{3,0},{4,1},{5,2},{6,3},{7,4},{8,13},{9,14},{10,... | collective-permute-start | bytes 24584 | tf_op jit(solution)/shard_map/ppermute | solution.py:491
  190.0 2.4 %collective-permute-start.24 = (bf16[16,256]{1,0:T(8,128)(2,1)S(1)}, bf16[16,256]{1,0:T(8,128)(2,1)S(1)}, u32[]{:S(2)}, u32[]{:S(2)}) collective-permute-start(bf16[16,256]{1,0:T(8,128)(2,1)S(1)} %get-tuple-element.125), channel_id=1, source_target_pairs={{0,6},{1,7},{2,0},{3,1},{4,2},{5,3},{6,4},{7,5},{8,14},{9,15},{10,... | collective-permute-start | bytes 24584 | tf_op jit(solution)/shard_map/ppermute | solution.py:491
  192.9 4.7 %collective-permute-done.24.refs_6_ = bf16[16,256]{1,0:T(8,128)(2,1)S(1)} collective-permute-done((bf16[16,256]{1,0:T(8,128)(2,1)S(1)}, bf16[16,256]{1,0:T(8,128)(2,1)S(1)}, u32[]{:S(2)}, u32[]{:S(2)}) %collective-permute-start.24) | collective-permute-done | bytes 8224 | tf_op jit(solution)/shard_map/ppermute | solution.py:491
  197.6 2.1 %collective-permute-done.25.refs_7_ = bf16[16,256]{1,0:T(8,128)(2,1)S(1)} collective-permute-done((bf16[16,256]{1,0:T(8,128)(2,1)S(1)}, bf16[16,256]{1,0:T(8,128)(2,1)S(1)}, u32[]{:S(2)}, u32[]{:S(2)}) %collective-permute-start.25) | collective-permute-done | bytes 8224 | tf_op jit(solution)/shard_map/ppermute | solution.py:491
  (88 shorter events, 39.5 us)
Async XLA Ops:
  0.6 10.4 %copy-start.2 = (bf16[128,2048]{1,0:T(8,128)(2,1)S(1)}, bf16[128,2048]{1,0:T(8,128)(2,1)}, u32[]{:S(2)}) copy-start(bf16[128,2048]{1,0:T(8,128)(2,1)} %cot_ref.1) | copy-start | bytes 1572868
  2.5 27.4 %all-to-all-start = ((bf16[8,144,256]{2,1,0:T(8,128)(2,1)}), bf16[8,144,256]{2,1,0:T(8,128)(2,1)S(1)}, u32[]{:S(2)}, u32[]{:S(2)}) async-start(bf16[8,144,256]{2,1,0:T(8,128)(2,1)} %get-tuple-element.84), calls=%async_computation | async-start | bytes 1179648 | tf_op jit(solution)/shard_map/all_to_all | solution.py:486
  14.4 15.3 %collective-permute-start = (bf16[128,2048]{1,0:T(8,128)(2,1)S(1)}, bf16[128,2048]{1,0:T(8,128)(2,1)S(1)}, u32[]{:S(2)}, u32[]{:S(2)}) collective-permute-start(bf16[128,2048]{1,0:T(8,128)(2,1)S(1)} %get-tuple-element.71), channel_id=1, source_target_pairs={{0,8},{4,12},{8,0},{12,4},{16,24},{20,28},{24,16},{28,20},{1,9},{5... | collective-permute-start | bytes 1572872 | tf_op jit(solution)/shard_map/ppermute | solution.py:506
  14.5 9.2 %collective-permute-start.1 = (bf16[128,1024]{1,0:T(8,128)(2,1)S(1)}, bf16[128,1024]{1,0:T(8,128)(2,1)S(1)}, u32[]{:S(2)}, u32[]{:S(2)}) collective-permute-start(bf16[128,1024]{1,0:T(8,128)(2,1)S(1)} %get-tuple-element.72), channel_id=1, source_target_pairs={{0,16},{4,20},{8,24},{12,28},{16,0},{20,4},{24,8},{28,12},{1,17},{... | collective-permute-start | bytes 786440 | tf_op jit(solution)/shard_map/ppermute | solution.py:506
  15.8 9.2 %collective-permute-start.2 = (bf16[128,1024]{1,0:T(8,128)(2,1)S(1)}, bf16[128,1024]{1,0:T(8,128)(2,1)S(1)}, u32[]{:S(2)}, u32[]{:S(2)}) collective-permute-start(bf16[128,1024]{1,0:T(8,128)(2,1)S(1)} %get-tuple-element.73), channel_id=1, source_target_pairs={{0,20},{4,16},{8,28},{12,24},{16,4},{20,0},{24,12},{28,8},{1,21},{... | collective-permute-start | bytes 786440 | tf_op jit(solution)/shard_map/ppermute | solution.py:506
  15.8 12.6 %collective-permute-start.3 = (bf16[128,1024]{1,0:T(8,128)(2,1)S(1)}, bf16[128,1024]{1,0:T(8,128)(2,1)S(1)}, u32[]{:S(2)}, u32[]{:S(2)}) collective-permute-start(bf16[128,1024]{1,0:T(8,128)(2,1)S(1)} %get-tuple-element.74), channel_id=1, source_target_pairs={{0,24},{4,28},{8,16},{12,20},{16,8},{20,12},{24,0},{28,4},{1,25},{... | collective-permute-start | bytes 786440 | tf_op jit(solution)/shard_map/ppermute | solution.py:506
  17.3 11.7 %collective-permute-start.4 = (bf16[128,1024]{1,0:T(8,128)(2,1)S(1)}, bf16[128,1024]{1,0:T(8,128)(2,1)S(1)}, u32[]{:S(2)}, u32[]{:S(2)}) collective-permute-start(bf16[128,1024]{1,0:T(8,128)(2,1)S(1)} %get-tuple-element.75), channel_id=1, source_target_pairs={{0,28},{4,24},{8,20},{12,16},{16,12},{20,8},{24,4},{28,0},{1,29},{... | collective-permute-start | bytes 786440 | tf_op jit(solution)/shard_map/ppermute | solution.py:506
  32.1 34.0 %all-to-all-start.1 = ((bf16[32,128,256]{2,1,0:T(8,128)(2,1)}), bf16[32,128,256]{2,1,0:T(8,128)(2,1)S(1)}, u32[]{:S(2)}, u32[]{:S(2)}) async-start(bf16[32,128,256]{2,1,0:T(8,128)(2,1)} %get-tuple-element.86), calls=%async_computation.1 | async-start | bytes 4194304 | tf_op jit(solution)/shard_map/all_to_all | solution.py:486
  44.9 33.9 %collective-permute-start.5 = (bf16[64,2048]{1,0:T(8,128)(2,1)}, bf16[64,2048]{1,0:T(8,128)(2,1)}, u32[]{:S(2)}, u32[]{:S(2)}) collective-permute-start(bf16[64,2048]{1,0:T(8,128)(2,1)} %get-tuple-element.77), channel_id=1, source_target_pairs={{0,32},{32,64},{64,96},{96,128},{128,160},{160,192},{192,224},{224... | collective-permute-start | bytes 786440 | tf_op jit(solution)/shard_map/ppermute | solution.py:491
  46.9 31.9 %collective-permute-start.6 = (bf16[64,2048]{1,0:T(8,128)(2,1)}, bf16[64,2048]{1,0:T(8,128)(2,1)}, u32[]{:S(2)}, u32[]{:S(2)}) collective-permute-start(bf16[64,2048]{1,0:T(8,128)(2,1)} %get-tuple-element.78), channel_id=1, source_target_pairs={{0,64},{32,96},{64,128},{96,160},{128,192},{160,224},{192,0},{224,... | collective-permute-start | bytes 786440 | tf_op jit(solution)/shard_map/ppermute | solution.py:491
  49.3 29.5 %collective-permute-start.8 = (bf16[64,2048]{1,0:T(8,128)(2,1)}, bf16[64,2048]{1,0:T(8,128)(2,1)}, u32[]{:S(2)}, u32[]{:S(2)}) collective-permute-start(bf16[64,2048]{1,0:T(8,128)(2,1)} %get-tuple-element.80), channel_id=1, source_target_pairs={{0,128},{32,160},{64,192},{96,224},{128,0},{160,32},{192,64},{224,... | collective-permute-start | bytes 786440 | tf_op jit(solution)/shard_map/ppermute | solution.py:491
  52.0 26.8 %collective-permute-start.10 = (bf16[64,2048]{1,0:T(8,128)(2,1)}, bf16[64,2048]{1,0:T(8,128)(2,1)}, u32[]{:S(2)}, u32[]{:S(2)}) collective-permute-start(bf16[64,2048]{1,0:T(8,128)(2,1)} %get-tuple-element.82), channel_id=1, source_target_pairs={{0,192},{32,224},{64,0},{96,32},{128,64},{160,96},{192,128},{224,1... | collective-permute-start | bytes 786440 | tf_op jit(solution)/shard_map/ppermute | solution.py:491
  55.6 25.3 %collective-permute-start.11 = (bf16[64,2048]{1,0:T(8,128)(2,1)}, bf16[64,2048]{1,0:T(8,128)(2,1)}, u32[]{:S(2)}, u32[]{:S(2)}) collective-permute-start(bf16[64,2048]{1,0:T(8,128)(2,1)} %get-tuple-element.83), channel_id=1, source_target_pairs={{0,224},{32,0},{64,32},{96,64},{128,96},{160,128},{192,160},{224,1... | collective-permute-start | bytes 786440 | tf_op jit(solution)/shard_map/ppermute | solution.py:491
  80.8 52.9 %all-to-all-start.3 = ((bf16[32,128,256]{2,1,0:T(8,128)(2,1)}), bf16[32,128,256]{2,1,0:T(8,128)(2,1)}, u32[]{:S(2)}, u32[]{:S(2)}) async-start(bf16[32,128,256]{2,1,0:T(8,128)(2,1)} %copy-done.1), calls=%async_computation.3 | async-start | bytes 4194304 | tf_op jit(solution)/shard_map/all_to_all | solution.py:486
  88.2 22.7 %collective-permute-start.7 = (bf16[64,2048]{1,0:T(8,128)(2,1)}, bf16[64,2048]{1,0:T(8,128)(2,1)S(1)}, u32[]{:S(2)}, u32[]{:S(2)}) collective-permute-start(bf16[64,2048]{1,0:T(8,128)(2,1)} %get-tuple-element.79), channel_id=1, source_target_pairs={{0,96},{32,128},{64,160},{96,192},{128,224},{160,0},{192,32},{224,... | collective-permute-start | bytes 786440 | tf_op jit(solution)/shard_map/ppermute | solution.py:491
  93.4 18.8 %collective-permute-start.9 = (bf16[64,2048]{1,0:T(8,128)(2,1)}, bf16[64,2048]{1,0:T(8,128)(2,1)S(1)}, u32[]{:S(2)}, u32[]{:S(2)}) collective-permute-start(bf16[64,2048]{1,0:T(8,128)(2,1)} %get-tuple-element.81), channel_id=1, source_target_pairs={{0,160},{32,192},{64,224},{96,0},{128,32},{160,64},{192,96},{224,1... | collective-permute-start | bytes 786440 | tf_op jit(solution)/shard_map/ppermute | solution.py:491
  133.7 33.4 %all-to-all-start.2 = ((bf16[32,128,256]{2,1,0:T(8,128)(2,1)}), bf16[32,128,256]{2,1,0:T(8,128)(2,1)S(1)}, u32[]{:S(2)}, u32[]{:S(2)}) async-start(bf16[32,128,256]{2,1,0:T(8,128)(2,1)} %copy-done), calls=%async_computation.2 | async-start | bytes 4194304 | tf_op jit(solution)/shard_map/all_to_all | solution.py:486
  143.7 12.6 %collective-permute-start.12 = (bf16[128,256]{1,0:T(8,128)(2,1)S(1)}, bf16[128,256]{1,0:T(8,128)(2,1)S(1)}, u32[]{:S(2)}, u32[]{:S(2)}) collective-permute-start(bf16[128,256]{1,0:T(8,128)(2,1)S(1)} %get-tuple-element.104), channel_id=1, source_target_pairs={{0,32},{32,64},{64,96},{96,128},{128,160},{160,192},{192,224},{224... | collective-permute-start | bytes 196616 | tf_op jit(solution)/shard_map/ppermute | solution.py:491
  148.7 10.0 %collective-permute-start.13 = (bf16[128,256]{1,0:T(8,128)(2,1)S(1)}, bf16[128,256]{1,0:T(8,128)(2,1)S(1)}, u32[]{:S(2)}, u32[]{:S(2)}) collective-permute-start(bf16[128,256]{1,0:T(8,128)(2,1)S(1)} %get-tuple-element.105), channel_id=1, source_target_pairs={{0,64},{32,96},{64,128},{96,160},{128,192},{160,224},{192,0},{224,... | collective-permute-start | bytes 196616 | tf_op jit(solution)/shard_map/ppermute | solution.py:491
  148.7 10.6 %collective-permute-start.14 = (bf16[128,256]{1,0:T(8,128)(2,1)S(1)}, bf16[128,256]{1,0:T(8,128)(2,1)S(1)}, u32[]{:S(2)}, u32[]{:S(2)}) collective-permute-start(bf16[128,256]{1,0:T(8,128)(2,1)S(1)} %get-tuple-element.106), channel_id=1, source_target_pairs={{0,96},{32,128},{64,160},{96,192},{128,224},{160,0},{192,32},{224,... | collective-permute-start | bytes 196616 | tf_op jit(solution)/shard_map/ppermute | solution.py:491
  151.8 11.3 %collective-permute-start.15 = (bf16[128,256]{1,0:T(8,128)(2,1)S(1)}, bf16[128,256]{1,0:T(8,128)(2,1)S(1)}, u32[]{:S(2)}, u32[]{:S(2)}) collective-permute-start(bf16[128,256]{1,0:T(8,128)(2,1)S(1)} %get-tuple-element.107), channel_id=1, source_target_pairs={{0,128},{32,160},{64,192},{96,224},{128,0},{160,32},{192,64},{224,... | collective-permute-start | bytes 196616 | tf_op jit(solution)/shard_map/ppermute | solution.py:491
  154.7 8.4 %collective-permute-start.16 = (bf16[128,256]{1,0:T(8,128)(2,1)S(1)}, bf16[128,256]{1,0:T(8,128)(2,1)S(1)}, u32[]{:S(2)}, u32[]{:S(2)}) collective-permute-start(bf16[128,256]{1,0:T(8,128)(2,1)S(1)} %get-tuple-element.108), channel_id=1, source_target_pairs={{0,160},{32,192},{64,224},{96,0},{128,32},{160,64},{192,96},{224,1... | collective-permute-start | bytes 196616 | tf_op jit(solution)/shard_map/ppermute | solution.py:491
  156.3 10.5 %collective-permute-start.17 = (bf16[128,256]{1,0:T(8,128)(2,1)S(1)}, bf16[128,256]{1,0:T(8,128)(2,1)S(1)}, u32[]{:S(2)}, u32[]{:S(2)}) collective-permute-start(bf16[128,256]{1,0:T(8,128)(2,1)S(1)} %get-tuple-element.109), channel_id=1, source_target_pairs={{0,192},{32,224},{64,0},{96,32},{128,64},{160,96},{192,128},{224,1... | collective-permute-start | bytes 196616 | tf_op jit(solution)/shard_map/ppermute | solution.py:491
  158.7 8.2 %collective-permute-start.18 = (bf16[128,256]{1,0:T(8,128)(2,1)S(1)}, bf16[128,256]{1,0:T(8,128)(2,1)S(1)}, u32[]{:S(2)}, u32[]{:S(2)}) collective-permute-start(bf16[128,256]{1,0:T(8,128)(2,1)S(1)} %get-tuple-element.110), channel_id=1, source_target_pairs={{0,224},{32,0},{64,32},{96,64},{128,96},{160,128},{192,160},{224,1... | collective-permute-start | bytes 196616 | tf_op jit(solution)/shard_map/ppermute | solution.py:491
  168.8 30.8 %all-to-all-start.4 = ((bf16[64,16,256]{2,1,0:T(8,128)(2,1)}), bf16[64,16,256]{2,1,0:T(8,128)(2,1)S(1)}, u32[]{:S(2)}, u32[]{:S(2)}) async-start(bf16[64,16,256]{2,1,0:T(8,128)(2,1)} %join_in.1), calls=%async_computation.4 | async-start | bytes 1048576 | tf_op jit(solution)/shard_map/all_to_all | solution.py:486
  180.8 9.2 %collective-permute-start.19 = (bf16[16,256]{1,0:T(8,128)(2,1)S(1)}, bf16[16,256]{1,0:T(8,128)(2,1)S(1)}, u32[]{:S(2)}, u32[]{:S(2)}) collective-permute-start(bf16[16,256]{1,0:T(8,128)(2,1)S(1)} %get-tuple-element.120), channel_id=1, source_target_pairs={{0,1},{1,2},{2,3},{3,4},{4,5},{5,6},{6,7},{7,0},{8,9},{9,10},{10,1... | collective-permute-start | bytes 24584 | tf_op jit(solution)/shard_map/ppermute | solution.py:491
  181.3 11.0 %collective-permute-start.20 = (bf16[16,256]{1,0:T(8,128)(2,1)S(1)}, bf16[16,256]{1,0:T(8,128)(2,1)S(1)}, u32[]{:S(2)}, u32[]{:S(2)}) collective-permute-start(bf16[16,256]{1,0:T(8,128)(2,1)S(1)} %get-tuple-element.121), channel_id=1, source_target_pairs={{0,2},{1,3},{2,4},{3,5},{4,6},{5,7},{6,0},{7,1},{8,10},{9,11},{10,... | collective-permute-start | bytes 24584 | tf_op jit(solution)/shard_map/ppermute | solution.py:491
  183.8 8.6 %collective-permute-start.21 = (bf16[16,256]{1,0:T(8,128)(2,1)S(1)}, bf16[16,256]{1,0:T(8,128)(2,1)S(1)}, u32[]{:S(2)}, u32[]{:S(2)}) collective-permute-start(bf16[16,256]{1,0:T(8,128)(2,1)S(1)} %get-tuple-element.122), channel_id=1, source_target_pairs={{0,3},{1,4},{2,5},{3,6},{4,7},{5,0},{6,1},{7,2},{8,11},{9,12},{10,... | collective-permute-start | bytes 24584 | tf_op jit(solution)/shard_map/ppermute | solution.py:491
  186.2 6.2 %collective-permute-start.22 = (bf16[16,256]{1,0:T(8,128)(2,1)S(1)}, bf16[16,256]{1,0:T(8,128)(2,1)S(1)}, u32[]{:S(2)}, u32[]{:S(2)}) collective-permute-start(bf16[16,256]{1,0:T(8,128)(2,1)S(1)} %get-tuple-element.123), channel_id=1, source_target_pairs={{0,4},{1,5},{2,6},{3,7},{4,0},{5,1},{6,2},{7,3},{8,12},{9,13},{10,... | collective-permute-start | bytes 24584 | tf_op jit(solution)/shard_map/ppermute | solution.py:491
  186.8 6.1 %collective-permute-start.23 = (bf16[16,256]{1,0:T(8,128)(2,1)S(1)}, bf16[16,256]{1,0:T(8,128)(2,1)S(1)}, u32[]{:S(2)}, u32[]{:S(2)}) collective-permute-start(bf16[16,256]{1,0:T(8,128)(2,1)S(1)} %get-tuple-element.124), channel_id=1, source_target_pairs={{0,5},{1,6},{2,7},{3,0},{4,1},{5,2},{6,3},{7,4},{8,13},{9,14},{10,... | collective-permute-start | bytes 24584 | tf_op jit(solution)/shard_map/ppermute | solution.py:491
  190.0 7.6 %collective-permute-start.24 = (bf16[16,256]{1,0:T(8,128)(2,1)S(1)}, bf16[16,256]{1,0:T(8,128)(2,1)S(1)}, u32[]{:S(2)}, u32[]{:S(2)}) collective-permute-start(bf16[16,256]{1,0:T(8,128)(2,1)S(1)} %get-tuple-element.125), channel_id=1, source_target_pairs={{0,6},{1,7},{2,0},{3,1},{4,2},{5,3},{6,4},{7,5},{8,14},{9,15},{10,... | collective-permute-start | bytes 24584 | tf_op jit(solution)/shard_map/ppermute | solution.py:491
  192.4 7.3 %collective-permute-start.25 = (bf16[16,256]{1,0:T(8,128)(2,1)S(1)}, bf16[16,256]{1,0:T(8,128)(2,1)S(1)}, u32[]{:S(2)}, u32[]{:S(2)}) collective-permute-start(bf16[16,256]{1,0:T(8,128)(2,1)S(1)} %get-tuple-element.126), channel_id=1, source_target_pairs={{0,7},{1,0},{2,1},{3,2},{4,3},{5,4},{6,5},{7,6},{8,15},{9,8},{10,9... | collective-permute-start | bytes 24584 | tf_op jit(solution)/shard_map/ppermute | solution.py:491
  (22 other events, 47.0 us)

commit v6 on v5

--- a/solution.py
+++ b/solution.py
@@ -11,7 +11,7 @@
 BF16 = jnp.bfloat16
 F32 = jnp.float32
 CAP = 16
-EARLY = (1, 2, 4, 6, 7)
+EARLY = (1, 2, 3, 5, 6, 7)
 META = 16
 
 
@@ -263,10 +263,10 @@
     return pl.pallas_call(
         forward_kernel,
         out_shape=[
-            jax.ShapeDtypeStruct(x_rows.shape, BF16),
-            jax.ShapeDtypeStruct((rows, ff), F32),
-            jax.ShapeDtypeStruct((rows, ff), F32),
-            jax.ShapeDtypeStruct((rows, ff), BF16),
+            pltpu.HBM(x_rows.shape, BF16),
+            pltpu.HBM((rows, ff), F32),
+            pltpu.HBM((rows, ff), F32),
+            pltpu.HBM((rows, ff), BF16),
         ],
         compiler_params=params(),
         cost_estimate=pl.CostEstimate(
@@ -324,10 +324,10 @@
             scratch_shapes=[pltpu.VMEM((rows, ff), F32)],
         ),
         out_shape=[
-            jax.ShapeDtypeStruct((4, rows // 4, width), BF16),
-            jax.ShapeDtypeStruct((32, rows // 4, width // 8), BF16),
-            jax.ShapeDtypeStruct((rows, ff), BF16),
-            jax.ShapeDtypeStruct((rows, ff), BF16),
+            pltpu.HBM((4, rows // 4, width), BF16),
+            pltpu.HBM((32, rows // 4, width // 8), BF16),
+            pltpu.HBM((rows, ff), BF16),
+            pltpu.HBM((rows, ff), BF16),
         ],
         compiler_params=params(36),
         cost_estimate=pl.CostEstimate(
@@ -519,7 +519,8 @@
     rw_t = route_weight.T
     x_cut, slots = route(col, tokens, expert_ids.T, rw_t, expert_slot.reshape(1, -1))
     x_all = swap(x_cut, ("z",))
-    g_crossed = cross(pick_g(at, cotangent, slots, rw_t))
+    gate_weight, up_weight, down_weight = map(in_hbm, (gate_weight, up_weight, down_weight))
+    g_crossed = [in_hbm(rows) for rows in cross(pick_g(at, cotangent, slots, rw_t))]
     x_all = after(x_all, g_crossed)
     g_turned = turn_g(at, g_crossed)
     g_parts = [in_hbm(part) for part in spread(g_turned, ("z",))]
@@ -531,10 +532,10 @@
     g_rows, in_send, dgate, dup = backward(
         at, g_parts, gate, up, gate_weight, up_weight, down_weight
     )
+    in_back = swap(in_send, PLANE)
     weight_grads = grads(x_rows, g_rows, hidden, dgate, dup)
-    in_send, weight_grads = lax.optimization_barrier((in_send, weight_grads))
-    in_back = swap(in_send, PLANE)
     y_parts = spread(join_out(zs, place, weight, out_back), ("z",))
+    y_parts[0] = after(y_parts[0], weight_grads)
     pieces = total(col, y_parts)
     in_back, pieces = lax.optimization_barrier((in_back, pieces))
     dx_part = join_in(place, in_back)

time: 201 us -> 192 us (0.955)
  local copies, waits for them, and re-layouts: 17.4 us -> 4.54 us
  Pallas kernels: 34.8 us -> 44.5 us
  starting transfers between devices: 91.2 us -> 85.6 us
    unnamed x46 -> x48, local copies, waits for them, and re-layouts: 17.4 us -> 4.54 us
    pallas_call x1, Pallas kernels: 6.21 us -> 11 us  [forward(): pl.pallas_call(forward_kernel, out_shape=[pltpu.HBM(x_rows.shape, BF16),...]
    pallas_call x1, Pallas kernels: 8.79 us -> 12 us  [backward(): pl.pallas_call(backward_kernel, grid_spec=pltpu.PrefetchScalarGridSpec(nu...]
    ppermute x21, starting transfers between devices: 43.5 us -> 40.3 us  [spread(): lax.ppermute(arrays[shift], axes, [(i, (i + shift) % 8) for i in range(8)])]
    all_to_all x5, starting transfers between devices: 43.1 us -> 40.9 us  [swap(): return lax.all_to_all(buffer, axes, split_axis=0, concat_axis=0, tiled=True)]
  transfers between devices with their start and end apart: 31 -> 31, of which waited for: 16 -> 13; matrix products, arithmetic and copies ran while one was open for 0% -> 0% of each run, Pallas kernels for 14% -> 20%
where the time goes in v6:
time: 192 us; the launch traced here: 191 us
  starting transfers between devices  85.6 us (45%)
  waiting for transfers between devices  55.9 us (29%)
  Pallas kernels  44.5 us (23%)
  local copies, waits for them, and re-layouts  4.54 us (2%)
    all_to_all x5, starting transfers between devices, swap(): return lax.all_to_all(buffer, axes, split_axis=0, concat_axis=0, tiled=True)  40.9 us
    ppermute x21, starting transfers between devices, spread(): lax.ppermute(arrays[shift], axes, [(i, (i + shift) % 8) for i in range(8)])  40.3 us
    ppermute x21, waiting for transfers between devices, spread(): lax.ppermute(arrays[shift], axes, [(i, (i + shift) % 8) for i in range(8)])  35.3 us
    pallas_call x1, Pallas kernels, backward(): pl.pallas_call(backward_kernel, grid_spec=pltpu.PrefetchScalarGridSpec(nu...  12 us
    pallas_call x1, Pallas kernels, forward(): pl.pallas_call(forward_kernel, out_shape=[pltpu.HBM(x_rows.shape, BF16),...  11 us
    all_to_all x5, waiting for transfers between devices, swap(): return lax.all_to_all(buffer, axes, split_axis=0, concat_axis=0, tiled=True)  10.5 us
    ppermute x5, waiting for transfers between devices, cross(): lax.ppermute(array, ('xl', 'core', 'xh'), [(i, i ^ 2 * away + over) for i...  10.2 us
    pallas_call x1, Pallas kernels, grads(): pl.pallas_call(grads_kernel, out_shape=[jax.ShapeDtypeStruct((1, width, f...  6.54 us
  transfers between devices with their start and end apart: 31, of which 13 were waited for; matrix products, arithmetic and copies ran while one was open for 0% of the time, Pallas kernels for 20%

profile of v6, /device:TPU:28, one launch (start us, length us, event | category | flops | bytes accessed | tf_op | source)
XLA Modules:
  0.0 191.4 jit_solution(2252379807939137596)
XLA Ops:
  2.5 8.5 %all-to-all-start = ((bf16[8,144,256]{2,1,0:T(8,128)(2,1)}), bf16[8,144,256]{2,1,0:T(8,128)(2,1)S(1)}, u32[]{:S(2)}, u32[]{:S(2)}) async-start(bf16[8,144,256]{2,1,0:T(8,128)(2,1)} %get-tuple-element.81), calls=%async_computation | async-start | bytes 1179648 | tf_op jit(solution)/shard_map/all_to_all | solution.py:486
  12.4 2.0 %pick_g.1 = (bf16[128,2048]{1,0:T(8,128)(2,1)S(1)}, bf16[128,2048]{1,0:T(8,128)(2,1)S(1)}, bf16[128,1024]{1,0:T(8,128)(2,1)S(1)}, bf16[128,1024]{1,0:T(8,128)(2,...) custom-call(s32[3]{0:T(128)S(1)} %pad_add_fusion.at_ref, bf16[128,2048]{1,0:T(8,128)(2,1)S(1)} %copy-done.3, ...), custom_call_target="tpu_custom_call" | custom-call | tf_op jit(solution)/shard_map/pick_g/pallas_call | solution.py:185
  19.6 4.7 %collective-permute-done.1.refs_2_ = bf16[128,1024]{1,0:T(8,128)(2,1)S(1)} collective-permute-done((bf16[128,1024]{1,0:T(8,128)(2,1)S(1)}, bf16[128,1024]{1,0:T(8,128)(2,1)S(1)}, u32[]{:S(2)}, u32[]{:S(2)}) %collective-permute-start.1) | collective-permute-done | bytes 262176 | tf_op jit(solution)/shard_map/ppermute | solution.py:506
  25.6 3.6 %collective-permute-done.3.refs_4_ = bf16[128,1024]{1,0:T(8,128)(2,1)S(1)} collective-permute-done((bf16[128,1024]{1,0:T(8,128)(2,1)S(1)}, bf16[128,1024]{1,0:T(8,128)(2,1)S(1)}, u32[]{:S(2)}, u32[]{:S(2)}) %collective-permute-start.3) | collective-permute-done | bytes 262176 | tf_op jit(solution)/shard_map/ppermute | solution.py:506
  29.8 2.3 %pick_x.1 = (bf16[32,128,256]{2,1,0:T(8,128)(2,1)}, f32[8,16,128]{2,1,0:T(8,128)S(1)}, f32[8,16,128]{2,1,0:T(8,128)S(1)}) custom-call(s32[1]{0:T(128)} %bitcast.1.at_ref.z_ref, bf16[8,144,256]{2,1,0:T(8,128)(2,1)S(1)} %all-to-all-done.x_ref), custom_call_target="tpu_custom_call" | custom-call | tf_op jit(solution)/shard_map/pick_x/pallas_call | solution.py:142
  32.2 7.9 %all-to-all-start.1 = ((bf16[32,128,256]{2,1,0:T(8,128)(2,1)}), bf16[32,128,256]{2,1,0:T(8,128)(2,1)S(1)}, u32[]{:S(2)}, u32[]{:S(2)}) async-start(bf16[32,128,256]{2,1,0:T(8,128)(2,1)} %get-tuple-element.83), calls=%async_computation.1 | async-start | bytes 4194304 | tf_op jit(solution)/shard_map/all_to_all | solution.py:486
  40.1 3.5 %turn_g.1 = (bf16[64,2048]{1,0:T(8,128)(2,1)}, bf16[64,2048]{1,0:T(8,128)(2,1)}, bf16[64,2048]{1,0:T(8,128)(2,1)}, bf16[64,2048]{1,0:T(8,128)(2,1)}, bf16[64,204...) custom-call(s32[3]{0:T(128)S(1)} %pad_add_fusion.at_ref, ...), custom_call_target="tpu_custom_call" | custom-call | tf_op jit(solution)/shard_map/turn_g/pallas_call | solution.py:210
  43.6 2.0 %collective-permute-start.5 = (bf16[64,2048]{1,0:T(8,128)(2,1)}, bf16[64,2048]{1,0:T(8,128)(2,1)S(1)}, u32[]{:S(2)}, u32[]{:S(2)}) collective-permute-start(bf16[64,2048]{1,0:T(8,128)(2,1)} %get-tuple-element.74), channel_id=1, source_target_pairs={{0,32},{32,64},{64,96},{96,128},{128,160},{160,192},{192,224},{224... | collective-permute-start | bytes 786440 | tf_op jit(solution)/shard_map/ppermute | solution.py:491
  45.6 2.4 %collective-permute-start.6 = (bf16[64,2048]{1,0:T(8,128)(2,1)}, bf16[64,2048]{1,0:T(8,128)(2,1)S(1)}, u32[]{:S(2)}, u32[]{:S(2)}) collective-permute-start(bf16[64,2048]{1,0:T(8,128)(2,1)} %get-tuple-element.75), channel_id=1, source_target_pairs={{0,64},{32,96},{64,128},{96,160},{128,192},{160,224},{192,0},{224,... | collective-permute-start | bytes 786440 | tf_op jit(solution)/shard_map/ppermute | solution.py:491
  48.0 2.7 %collective-permute-start.7 = (bf16[64,2048]{1,0:T(8,128)(2,1)}, bf16[64,2048]{1,0:T(8,128)(2,1)S(1)}, u32[]{:S(2)}, u32[]{:S(2)}) collective-permute-start(bf16[64,2048]{1,0:T(8,128)(2,1)} %get-tuple-element.76), channel_id=1, source_target_pairs={{0,96},{32,128},{64,160},{96,192},{128,224},{160,0},{192,32},{224,... | collective-permute-start | bytes 786440 | tf_op jit(solution)/shard_map/ppermute | solution.py:491
  50.7 2.4 %collective-permute-start.9 = (bf16[64,2048]{1,0:T(8,128)(2,1)}, bf16[64,2048]{1,0:T(8,128)(2,1)S(1)}, u32[]{:S(2)}, u32[]{:S(2)}) collective-permute-start(bf16[64,2048]{1,0:T(8,128)(2,1)} %get-tuple-element.78), channel_id=1, source_target_pairs={{0,160},{32,192},{64,224},{96,0},{128,32},{160,64},{192,96},{224,1... | collective-permute-start | bytes 786440 | tf_op jit(solution)/shard_map/ppermute | solution.py:491
  56.7 9.5 %all-to-all-done.1.x_ref = bf16[32,128,256]{2,1,0:T(8,128)(2,1)S(1)} async-done(((bf16[32,128,256]{2,1,0:T(8,128)(2,1)}), bf16[32,128,256]{2,1,0:T(8,128)(2,1)S(1)}, u32[]{:S(2)}, u32[]{:S(2)}) %all-to-all-start.1) | async-done | bytes 2097184 | tf_op jit(solution)/shard_map/all_to_all | solution.py:486
  66.2 11.0 %forward.1 = (bf16[32,128,256]{2,1,0:T(8,128)(2,1)}, f32[512,384]{1,0:T(8,128)}, f32[512,384]{1,0:T(8,128)}, bf16[512,384]{1,0:T(8,128)(2,1)}) custom-call(bf16[32,128,256]{2,1,0:T(8,128)(2,1)S(1)} %all-to-all-done.1.x_ref, bf16[1,2048,384]{2,1,0:T(8,128)(2,1)} %refs_10_.1, bf16[1,2048,384]{2,1,0:T(8,128)(2,1)} %refs_11_.1, bf16[1,384,2048]{2,1,0:T(8,128)(2,1)} %refs_12_.1), custom_call_target="tpu_custom_call" | custom-call | flops 2415919104 | bytes 11534336 | tf_op jit(solution)/shard_map/forward/pallas_call | solution.py:263
  77.2 5.4 %collective-permute-done.7.refs_3_ = bf16[64,2048]{1,0:T(8,128)(2,1)S(1)} collective-permute-done((bf16[64,2048]{1,0:T(8,128)(2,1)}, bf16[64,2048]{1,0:T(8,128)(2,1)S(1)}, u32[]{:S(2)}, u32[]{:S(2)}) %collective-permute-start.7) | collective-permute-done | bytes 262176 | tf_op jit(solution)/shard_map/ppermute | solution.py:491
  83.9 4.7 %collective-permute-done.11.refs_7_ = bf16[64,2048]{1,0:T(8,128)(2,1)} collective-permute-done((bf16[64,2048]{1,0:T(8,128)(2,1)}, bf16[64,2048]{1,0:T(8,128)(2,1)}, u32[]{:S(2)}, u32[]{:S(2)}) %collective-permute-start.11) | collective-permute-done | bytes 262176 | tf_op jit(solution)/shard_map/ppermute | solution.py:491
  88.7 7.6 %all-to-all-start.3 = ((bf16[32,128,256]{2,1,0:T(8,128)(2,1)}), bf16[32,128,256]{2,1,0:T(8,128)(2,1)}, u32[]{:S(2)}, u32[]{:S(2)}) async-start(bf16[32,128,256]{2,1,0:T(8,128)(2,1)} %get-tuple-element.91), calls=%async_computation.3 | async-start | bytes 4194304 | tf_op jit(solution)/shard_map/all_to_all | solution.py:486
  97.8 16.6 %collective-permute-done.8.refs_4_ = bf16[64,2048]{1,0:T(8,128)(2,1)S(1)} collective-permute-done((bf16[64,2048]{1,0:T(8,128)(2,1)S(1)}, bf16[64,2048]{1,0:T(8,128)(2,1)S(1)}, u32[]{:S(2)}, u32[]{:S(2)}) %collective-permute-start.8) | collective-permute-done | bytes 262176 | tf_op jit(solution)/shard_map/ppermute | solution.py:491
  115.1 12.0 %backward.1 = (bf16[4,128,2048]{2,1,0:T(8,128)(2,1)}, bf16[32,128,256]{2,1,0:T(8,128)(2,1)}, bf16[512,384]{1,0:T(8,128)(2,1)}, bf16[512,384]{1,0:T(8,128)(2,1)}) custom-call(s32[3]{0:T(128)S(1)} %pad_add_fusion.at_ref, bf16[64,2048]{1,0:T(8,128)(2,1)} %get-tuple-element.73.refs_0_, bf16[64,2048]{1,0:T(8,128)(2,1)} %copy-done.18, ...), custom_call_target="tpu_custom_call" | custom-call | flops 2415919104 | bytes 13631488 | tf_op jit(solution)/shard_map/backward/pallas_call | solution.py:312
  127.2 7.5 %all-to-all-start.2 = ((bf16[32,128,256]{2,1,0:T(8,128)(2,1)}), bf16[32,128,256]{2,1,0:T(8,128)(2,1)S(1)}, u32[]{:S(2)}, u32[]{:S(2)}) async-start(bf16[32,128,256]{2,1,0:T(8,128)(2,1)} %get-tuple-element.87), calls=%async_computation.2 | async-start | bytes 4194304 | tf_op jit(solution)/shard_map/all_to_all | solution.py:486
  134.7 2.8 %join_out.1 = (f32[128,256]{1,0:T(8,128)S(1)}, bf16[128,256]{1,0:T(8,128)(2,1)S(1)}, bf16[128,256]{1,0:T(8,128)(2,1)S(1)}, bf16[128,256]{1,0:T(8,128)(2,1)S(1)},...) custom-call(s32[1]{0:T(128)} %bitcast.1.at_ref.z_ref, ...), custom_call_target="tpu_custom_call" | custom-call | tf_op jit(solution)/shard_map/join_out/pallas_call | solution.py:395
  137.6 2.0 %collective-permute-start.13 = (bf16[128,256]{1,0:T(8,128)(2,1)S(1)}, bf16[128,256]{1,0:T(8,128)(2,1)S(1)}, u32[]{:S(2)}, u32[]{:S(2)}) collective-permute-start(bf16[128,256]{1,0:T(8,128)(2,1)S(1)} %get-tuple-element.102), channel_id=1, source_target_pairs={{0,64},{32,96},{64,128},{96,160},{128,192},{160,224},{192,0},{224,... | collective-permute-start | bytes 196616 | tf_op jit(solution)/shard_map/ppermute | solution.py:491
  140.1 4.0 %collective-permute-start.15 = (bf16[128,256]{1,0:T(8,128)(2,1)S(1)}, bf16[128,256]{1,0:T(8,128)(2,1)S(1)}, u32[]{:S(2)}, u32[]{:S(2)}) collective-permute-start(bf16[128,256]{1,0:T(8,128)(2,1)S(1)} %get-tuple-element.104), channel_id=1, source_target_pairs={{0,128},{32,160},{64,192},{96,224},{128,0},{160,32},{192,64},{224,... | collective-permute-start | bytes 196616 | tf_op jit(solution)/shard_map/ppermute | solution.py:491
  144.1 4.1 %collective-permute-start.16 = (bf16[128,256]{1,0:T(8,128)(2,1)S(1)}, bf16[128,256]{1,0:T(8,128)(2,1)S(1)}, u32[]{:S(2)}, u32[]{:S(2)}) collective-permute-start(bf16[128,256]{1,0:T(8,128)(2,1)S(1)} %get-tuple-element.105), channel_id=1, source_target_pairs={{0,160},{32,192},{64,224},{96,0},{128,32},{160,64},{192,96},{224,1... | collective-permute-start | bytes 196616 | tf_op jit(solution)/shard_map/ppermute | solution.py:491
  148.2 3.3 %collective-permute-start.18 = (bf16[128,256]{1,0:T(8,128)(2,1)S(1)}, bf16[128,256]{1,0:T(8,128)(2,1)S(1)}, u32[]{:S(2)}, u32[]{:S(2)}) collective-permute-start(bf16[128,256]{1,0:T(8,128)(2,1)S(1)} %get-tuple-element.107), channel_id=1, source_target_pairs={{0,224},{32,0},{64,32},{96,64},{128,96},{160,128},{192,160},{224,1... | collective-permute-start | bytes 196616 | tf_op jit(solution)/shard_map/ppermute | solution.py:491
  153.2 6.5 %grads.1 = (bf16[1,2048,384]{2,1,0:T(8,128)(2,1)}, bf16[1,2048,384]{2,1,0:T(8,128)(2,1)}, bf16[1,384,2048]{2,1,0:T(8,128)(2,1)}) custom-call(bf16[32,128,256]{2,1,0:T(8,128)(2,1)S(1)} %copy-done.1, bf16[4,128,2048]{2,1,0:T(8,128)(2,1)S(1)} %copy-done.6, bf16[512,384]{1,0:T(8,128)(2,1)S(1)} %copy-done.11, bf16[512,384]{1,0:T(8,128)(2,1)S(1)} %copy-done.9, ...), custom_call_target="tpu_custom_call" | custom-call | flops 2415919104 | bytes 10485760 | tf_op jit(solution)/shard_map/grads/pallas_call | solution.py:357
  162.5 9.4 %all-to-all-start.4 = ((bf16[64,16,256]{2,1,0:T(8,128)(2,1)}), bf16[64,16,256]{2,1,0:T(8,128)(2,1)S(1)}, u32[]{:S(2)}, u32[]{:S(2)}) async-start(bf16[64,16,256]{2,1,0:T(8,128)(2,1)} %join_in.1), calls=%async_computation.4 | async-start | bytes 1048576 | tf_op jit(solution)/shard_map/all_to_all | solution.py:486
  172.4 2.5 %collective-permute-start.20 = (bf16[16,256]{1,0:T(8,128)(2,1)S(1)}, bf16[16,256]{1,0:T(8,128)(2,1)S(1)}, u32[]{:S(2)}, u32[]{:S(2)}) collective-permute-start(bf16[16,256]{1,0:T(8,128)(2,1)S(1)} %get-tuple-element.118), channel_id=1, source_target_pairs={{0,2},{1,3},{2,4},{3,5},{4,6},{5,7},{6,0},{7,1},{8,10},{9,11},{10,... | collective-permute-start | bytes 24584 | tf_op jit(solution)/shard_map/ppermute | solution.py:491
  174.9 2.4 %collective-permute-start.21 = (bf16[16,256]{1,0:T(8,128)(2,1)S(1)}, bf16[16,256]{1,0:T(8,128)(2,1)S(1)}, u32[]{:S(2)}, u32[]{:S(2)}) collective-permute-start(bf16[16,256]{1,0:T(8,128)(2,1)S(1)} %get-tuple-element.119), channel_id=1, source_target_pairs={{0,3},{1,4},{2,5},{3,6},{4,7},{5,0},{6,1},{7,2},{8,11},{9,12},{10,... | collective-permute-start | bytes 24584 | tf_op jit(solution)/shard_map/ppermute | solution.py:491
  177.9 3.2 %collective-permute-start.23 = (bf16[16,256]{1,0:T(8,128)(2,1)S(1)}, bf16[16,256]{1,0:T(8,128)(2,1)S(1)}, u32[]{:S(2)}, u32[]{:S(2)}) collective-permute-start(bf16[16,256]{1,0:T(8,128)(2,1)S(1)} %get-tuple-element.121), channel_id=1, source_target_pairs={{0,5},{1,6},{2,7},{3,0},{4,1},{5,2},{6,3},{7,4},{8,13},{9,14},{10,... | collective-permute-start | bytes 24584 | tf_op jit(solution)/shard_map/ppermute | solution.py:491
  181.1 2.4 %collective-permute-start.24 = (bf16[16,256]{1,0:T(8,128)(2,1)S(1)}, bf16[16,256]{1,0:T(8,128)(2,1)S(1)}, u32[]{:S(2)}, u32[]{:S(2)}) collective-permute-start(bf16[16,256]{1,0:T(8,128)(2,1)S(1)} %get-tuple-element.122), channel_id=1, source_target_pairs={{0,6},{1,7},{2,0},{3,1},{4,2},{5,3},{6,4},{7,5},{8,14},{9,15},{10,... | collective-permute-start | bytes 24584 | tf_op jit(solution)/shard_map/ppermute | solution.py:491
  183.9 4.7 %collective-permute-done.24.refs_6_ = bf16[16,256]{1,0:T(8,128)(2,1)S(1)} collective-permute-done((bf16[16,256]{1,0:T(8,128)(2,1)S(1)}, bf16[16,256]{1,0:T(8,128)(2,1)S(1)}, u32[]{:S(2)}, u32[]{:S(2)}) %collective-permute-start.24) | collective-permute-done | bytes 8224 | tf_op jit(solution)/shard_map/ppermute | solution.py:491
  188.7 2.1 %collective-permute-done.25.refs_7_ = bf16[16,256]{1,0:T(8,128)(2,1)S(1)} collective-permute-done((bf16[16,256]{1,0:T(8,128)(2,1)S(1)}, bf16[16,256]{1,0:T(8,128)(2,1)S(1)}, u32[]{:S(2)}, u32[]{:S(2)}) %collective-permute-start.25) | collective-permute-done | bytes 8224 | tf_op jit(solution)/shard_map/ppermute | solution.py:491
  (90 shorter events, 24.8 us)
Async XLA Ops:
  2.5 27.4 %all-to-all-start = ((bf16[8,144,256]{2,1,0:T(8,128)(2,1)}), bf16[8,144,256]{2,1,0:T(8,128)(2,1)S(1)}, u32[]{:S(2)}, u32[]{:S(2)}) async-start(bf16[8,144,256]{2,1,0:T(8,128)(2,1)} %get-tuple-element.81), calls=%async_computation | async-start | bytes 1179648 | tf_op jit(solution)/shard_map/all_to_all | solution.py:486
  15.2 14.6 %collective-permute-start = (bf16[128,2048]{1,0:T(8,128)(2,1)S(1)}, bf16[128,2048]{1,0:T(8,128)(2,1)S(1)}, u32[]{:S(2)}, u32[]{:S(2)}) collective-permute-start(bf16[128,2048]{1,0:T(8,128)(2,1)S(1)} %get-tuple-element.68), channel_id=1, source_target_pairs={{0,8},{4,12},{8,0},{12,4},{16,24},{20,28},{24,16},{28,20},{1,9},{5... | collective-permute-start | bytes 1572872 | tf_op jit(solution)/shard_map/ppermute | solution.py:506
  15.2 9.1 %collective-permute-start.1 = (bf16[128,1024]{1,0:T(8,128)(2,1)S(1)}, bf16[128,1024]{1,0:T(8,128)(2,1)S(1)}, u32[]{:S(2)}, u32[]{:S(2)}) collective-permute-start(bf16[128,1024]{1,0:T(8,128)(2,1)S(1)} %get-tuple-element.69), channel_id=1, source_target_pairs={{0,16},{4,20},{8,24},{12,28},{16,0},{20,4},{24,8},{28,12},{1,17},{... | collective-permute-start | bytes 786440 | tf_op jit(solution)/shard_map/ppermute | solution.py:506
  16.4 9.1 %collective-permute-start.2 = (bf16[128,1024]{1,0:T(8,128)(2,1)S(1)}, bf16[128,1024]{1,0:T(8,128)(2,1)S(1)}, u32[]{:S(2)}, u32[]{:S(2)}) collective-permute-start(bf16[128,1024]{1,0:T(8,128)(2,1)S(1)} %get-tuple-element.70), channel_id=1, source_target_pairs={{0,20},{4,16},{8,28},{12,24},{16,4},{20,0},{24,12},{28,8},{1,21},{... | collective-permute-start | bytes 786440 | tf_op jit(solution)/shard_map/ppermute | solution.py:506
  16.4 12.7 %collective-permute-start.3 = (bf16[128,1024]{1,0:T(8,128)(2,1)S(1)}, bf16[128,1024]{1,0:T(8,128)(2,1)S(1)}, u32[]{:S(2)}, u32[]{:S(2)}) collective-permute-start(bf16[128,1024]{1,0:T(8,128)(2,1)S(1)} %get-tuple-element.71), channel_id=1, source_target_pairs={{0,24},{4,28},{8,16},{12,20},{16,8},{20,12},{24,0},{28,4},{1,25},{... | collective-permute-start | bytes 786440 | tf_op jit(solution)/shard_map/ppermute | solution.py:506
  17.9 11.8 %collective-permute-start.4 = (bf16[128,1024]{1,0:T(8,128)(2,1)S(1)}, bf16[128,1024]{1,0:T(8,128)(2,1)S(1)}, u32[]{:S(2)}, u32[]{:S(2)}) collective-permute-start(bf16[128,1024]{1,0:T(8,128)(2,1)S(1)} %get-tuple-element.72), channel_id=1, source_target_pairs={{0,28},{4,24},{8,20},{12,16},{16,12},{20,8},{24,4},{28,0},{1,29},{... | collective-permute-start | bytes 786440 | tf_op jit(solution)/shard_map/ppermute | solution.py:506
  32.2 34.0 %all-to-all-start.1 = ((bf16[32,128,256]{2,1,0:T(8,128)(2,1)}), bf16[32,128,256]{2,1,0:T(8,128)(2,1)S(1)}, u32[]{:S(2)}, u32[]{:S(2)}) async-start(bf16[32,128,256]{2,1,0:T(8,128)(2,1)} %get-tuple-element.83), calls=%async_computation.1 | async-start | bytes 4194304 | tf_op jit(solution)/shard_map/all_to_all | solution.py:486
  43.6 11.2 %collective-permute-start.5 = (bf16[64,2048]{1,0:T(8,128)(2,1)}, bf16[64,2048]{1,0:T(8,128)(2,1)S(1)}, u32[]{:S(2)}, u32[]{:S(2)}) collective-permute-start(bf16[64,2048]{1,0:T(8,128)(2,1)} %get-tuple-element.74), channel_id=1, source_target_pairs={{0,32},{32,64},{64,96},{96,128},{128,160},{160,192},{192,224},{224... | collective-permute-start | bytes 786440 | tf_op jit(solution)/shard_map/ppermute | solution.py:491
  45.6 31.6 %collective-permute-start.6 = (bf16[64,2048]{1,0:T(8,128)(2,1)}, bf16[64,2048]{1,0:T(8,128)(2,1)S(1)}, u32[]{:S(2)}, u32[]{:S(2)}) collective-permute-start(bf16[64,2048]{1,0:T(8,128)(2,1)} %get-tuple-element.75), channel_id=1, source_target_pairs={{0,64},{32,96},{64,128},{96,160},{128,192},{160,224},{192,0},{224,... | collective-permute-start | bytes 786440 | tf_op jit(solution)/shard_map/ppermute | solution.py:491
  48.0 34.6 %collective-permute-start.7 = (bf16[64,2048]{1,0:T(8,128)(2,1)}, bf16[64,2048]{1,0:T(8,128)(2,1)S(1)}, u32[]{:S(2)}, u32[]{:S(2)}) collective-permute-start(bf16[64,2048]{1,0:T(8,128)(2,1)} %get-tuple-element.76), channel_id=1, source_target_pairs={{0,96},{32,128},{64,160},{96,192},{128,224},{160,0},{192,32},{224,... | collective-permute-start | bytes 786440 | tf_op jit(solution)/shard_map/ppermute | solution.py:491
  50.7 32.0 %collective-permute-start.9 = (bf16[64,2048]{1,0:T(8,128)(2,1)}, bf16[64,2048]{1,0:T(8,128)(2,1)S(1)}, u32[]{:S(2)}, u32[]{:S(2)}) collective-permute-start(bf16[64,2048]{1,0:T(8,128)(2,1)} %get-tuple-element.78), channel_id=1, source_target_pairs={{0,160},{32,192},{64,224},{96,0},{128,32},{160,64},{192,96},{224,1... | collective-permute-start | bytes 786440 | tf_op jit(solution)/shard_map/ppermute | solution.py:491
  53.0 30.8 %collective-permute-start.10 = (bf16[64,2048]{1,0:T(8,128)(2,1)}, bf16[64,2048]{1,0:T(8,128)(2,1)S(1)}, u32[]{:S(2)}, u32[]{:S(2)}) collective-permute-start(bf16[64,2048]{1,0:T(8,128)(2,1)} %get-tuple-element.79), channel_id=1, source_target_pairs={{0,192},{32,224},{64,0},{96,32},{128,64},{160,96},{192,128},{224,1... | collective-permute-start | bytes 786440 | tf_op jit(solution)/shard_map/ppermute | solution.py:491
  54.8 33.8 %collective-permute-start.11 = (bf16[64,2048]{1,0:T(8,128)(2,1)}, bf16[64,2048]{1,0:T(8,128)(2,1)}, u32[]{:S(2)}, u32[]{:S(2)}) collective-permute-start(bf16[64,2048]{1,0:T(8,128)(2,1)} %get-tuple-element.80), channel_id=1, source_target_pairs={{0,224},{32,0},{64,32},{96,64},{128,96},{160,128},{192,160},{224,1... | collective-permute-start | bytes 786440 | tf_op jit(solution)/shard_map/ppermute | solution.py:491
  88.6 26.5 %copy-start.8 = (f32[512,384]{1,0:T(8,128)S(1)}, f32[512,384]{1,0:T(8,128)}, u32[]{:S(2)}) copy-start(f32[512,384]{1,0:T(8,128)} %get-tuple-element.86.refs_9_) | copy-start | bytes 2359300
  88.7 38.5 %all-to-all-start.3 = ((bf16[32,128,256]{2,1,0:T(8,128)(2,1)}), bf16[32,128,256]{2,1,0:T(8,128)(2,1)}, u32[]{:S(2)}, u32[]{:S(2)}) async-start(bf16[32,128,256]{2,1,0:T(8,128)(2,1)} %get-tuple-element.91), calls=%async_computation.3 | async-start | bytes 4194304 | tf_op jit(solution)/shard_map/all_to_all | solution.py:486
  96.2 18.2 %collective-permute-start.8 = (bf16[64,2048]{1,0:T(8,128)(2,1)S(1)}, bf16[64,2048]{1,0:T(8,128)(2,1)S(1)}, u32[]{:S(2)}, u32[]{:S(2)}) collective-permute-start(bf16[64,2048]{1,0:T(8,128)(2,1)S(1)} %copy-done.17), channel_id=1, source_target_pairs={{0,128},{32,160},{64,192},{96,224},{128,0},{160,32},{192,64},{224,... | collective-permute-start | bytes 786440 | tf_op jit(solution)/shard_map/ppermute | solution.py:491
  127.2 33.6 %all-to-all-start.2 = ((bf16[32,128,256]{2,1,0:T(8,128)(2,1)}), bf16[32,128,256]{2,1,0:T(8,128)(2,1)S(1)}, u32[]{:S(2)}, u32[]{:S(2)}) async-start(bf16[32,128,256]{2,1,0:T(8,128)(2,1)} %get-tuple-element.87), calls=%async_computation.2 | async-start | bytes 4194304 | tf_op jit(solution)/shard_map/all_to_all | solution.py:486
  137.5 10.7 %collective-permute-start.12 = (bf16[128,256]{1,0:T(8,128)(2,1)S(1)}, bf16[128,256]{1,0:T(8,128)(2,1)S(1)}, u32[]{:S(2)}, u32[]{:S(2)}) collective-permute-start(bf16[128,256]{1,0:T(8,128)(2,1)S(1)} %get-tuple-element.101), channel_id=1, source_target_pairs={{0,32},{32,64},{64,96},{96,128},{128,160},{160,192},{192,224},{224... | collective-permute-start | bytes 196616 | tf_op jit(solution)/shard_map/ppermute | solution.py:491
  137.6 10.6 %collective-permute-start.13 = (bf16[128,256]{1,0:T(8,128)(2,1)S(1)}, bf16[128,256]{1,0:T(8,128)(2,1)S(1)}, u32[]{:S(2)}, u32[]{:S(2)}) collective-permute-start(bf16[128,256]{1,0:T(8,128)(2,1)S(1)} %get-tuple-element.102), channel_id=1, source_target_pairs={{0,64},{32,96},{64,128},{96,160},{128,192},{160,224},{192,0},{224,... | collective-permute-start | bytes 196616 | tf_op jit(solution)/shard_map/ppermute | solution.py:491
  139.6 20.2 %collective-permute-start.14 = (bf16[128,256]{1,0:T(8,128)(2,1)S(1)}, bf16[128,256]{1,0:T(8,128)(2,1)S(1)}, u32[]{:S(2)}, u32[]{:S(2)}) collective-permute-start(bf16[128,256]{1,0:T(8,128)(2,1)S(1)} %get-tuple-element.103), channel_id=1, source_target_pairs={{0,96},{32,128},{64,160},{96,192},{128,224},{160,0},{192,32},{224,... | collective-permute-start | bytes 196616 | tf_op jit(solution)/shard_map/ppermute | solution.py:491
  140.1 19.6 %collective-permute-start.15 = (bf16[128,256]{1,0:T(8,128)(2,1)S(1)}, bf16[128,256]{1,0:T(8,128)(2,1)S(1)}, u32[]{:S(2)}, u32[]{:S(2)}) collective-permute-start(bf16[128,256]{1,0:T(8,128)(2,1)S(1)} %get-tuple-element.104), channel_id=1, source_target_pairs={{0,128},{32,160},{64,192},{96,224},{128,0},{160,32},{192,64},{224,... | collective-permute-start | bytes 196616 | tf_op jit(solution)/shard_map/ppermute | solution.py:491
  144.1 15.6 %collective-permute-start.16 = (bf16[128,256]{1,0:T(8,128)(2,1)S(1)}, bf16[128,256]{1,0:T(8,128)(2,1)S(1)}, u32[]{:S(2)}, u32[]{:S(2)}) collective-permute-start(bf16[128,256]{1,0:T(8,128)(2,1)S(1)} %get-tuple-element.105), channel_id=1, source_target_pairs={{0,160},{32,192},{64,224},{96,0},{128,32},{160,64},{192,96},{224,1... | collective-permute-start | bytes 196616 | tf_op jit(solution)/shard_map/ppermute | solution.py:491
  148.2 11.5 %collective-permute-start.17 = (bf16[128,256]{1,0:T(8,128)(2,1)S(1)}, bf16[128,256]{1,0:T(8,128)(2,1)S(1)}, u32[]{:S(2)}, u32[]{:S(2)}) collective-permute-start(bf16[128,256]{1,0:T(8,128)(2,1)S(1)} %get-tuple-element.106), channel_id=1, source_target_pairs={{0,192},{32,224},{64,0},{96,32},{128,64},{160,96},{192,128},{224,1... | collective-permute-start | bytes 196616 | tf_op jit(solution)/shard_map/ppermute | solution.py:491
  148.2 11.5 %collective-permute-start.18 = (bf16[128,256]{1,0:T(8,128)(2,1)S(1)}, bf16[128,256]{1,0:T(8,128)(2,1)S(1)}, u32[]{:S(2)}, u32[]{:S(2)}) collective-permute-start(bf16[128,256]{1,0:T(8,128)(2,1)S(1)} %get-tuple-element.107), channel_id=1, source_target_pairs={{0,224},{32,0},{64,32},{96,64},{128,96},{160,128},{192,160},{224,1... | collective-permute-start | bytes 196616 | tf_op jit(solution)/shard_map/ppermute | solution.py:491
  162.5 28.3 %all-to-all-start.4 = ((bf16[64,16,256]{2,1,0:T(8,128)(2,1)}), bf16[64,16,256]{2,1,0:T(8,128)(2,1)S(1)}, u32[]{:S(2)}, u32[]{:S(2)}) async-start(bf16[64,16,256]{2,1,0:T(8,128)(2,1)} %join_in.1), calls=%async_computation.4 | async-start | bytes 1048576 | tf_op jit(solution)/shard_map/all_to_all | solution.py:486
  171.9 9.2 %collective-permute-start.19 = (bf16[16,256]{1,0:T(8,128)(2,1)S(1)}, bf16[16,256]{1,0:T(8,128)(2,1)S(1)}, u32[]{:S(2)}, u32[]{:S(2)}) collective-permute-start(bf16[16,256]{1,0:T(8,128)(2,1)S(1)} %get-tuple-element.117), channel_id=1, source_target_pairs={{0,1},{1,2},{2,3},{3,4},{4,5},{5,6},{6,7},{7,0},{8,9},{9,10},{10,1... | collective-permute-start | bytes 24584 | tf_op jit(solution)/shard_map/ppermute | solution.py:491
  172.4 11.0 %collective-permute-start.20 = (bf16[16,256]{1,0:T(8,128)(2,1)S(1)}, bf16[16,256]{1,0:T(8,128)(2,1)S(1)}, u32[]{:S(2)}, u32[]{:S(2)}) collective-permute-start(bf16[16,256]{1,0:T(8,128)(2,1)S(1)} %get-tuple-element.118), channel_id=1, source_target_pairs={{0,2},{1,3},{2,4},{3,5},{4,6},{5,7},{6,0},{7,1},{8,10},{9,11},{10,... | collective-permute-start | bytes 24584 | tf_op jit(solution)/shard_map/ppermute | solution.py:491
  174.9 8.6 %collective-permute-start.21 = (bf16[16,256]{1,0:T(8,128)(2,1)S(1)}, bf16[16,256]{1,0:T(8,128)(2,1)S(1)}, u32[]{:S(2)}, u32[]{:S(2)}) collective-permute-start(bf16[16,256]{1,0:T(8,128)(2,1)S(1)} %get-tuple-element.119), channel_id=1, source_target_pairs={{0,3},{1,4},{2,5},{3,6},{4,7},{5,0},{6,1},{7,2},{8,11},{9,12},{10,... | collective-permute-start | bytes 24584 | tf_op jit(solution)/shard_map/ppermute | solution.py:491
  177.3 6.2 %collective-permute-start.22 = (bf16[16,256]{1,0:T(8,128)(2,1)S(1)}, bf16[16,256]{1,0:T(8,128)(2,1)S(1)}, u32[]{:S(2)}, u32[]{:S(2)}) collective-permute-start(bf16[16,256]{1,0:T(8,128)(2,1)S(1)} %get-tuple-element.120), channel_id=1, source_target_pairs={{0,4},{1,5},{2,6},{3,7},{4,0},{5,1},{6,2},{7,3},{8,12},{9,13},{10,... | collective-permute-start | bytes 24584 | tf_op jit(solution)/shard_map/ppermute | solution.py:491
  177.9 6.1 %collective-permute-start.23 = (bf16[16,256]{1,0:T(8,128)(2,1)S(1)}, bf16[16,256]{1,0:T(8,128)(2,1)S(1)}, u32[]{:S(2)}, u32[]{:S(2)}) collective-permute-start(bf16[16,256]{1,0:T(8,128)(2,1)S(1)} %get-tuple-element.121), channel_id=1, source_target_pairs={{0,5},{1,6},{2,7},{3,0},{4,1},{5,2},{6,3},{7,4},{8,13},{9,14},{10,... | collective-permute-start | bytes 24584 | tf_op jit(solution)/shard_map/ppermute | solution.py:491
  181.1 7.6 %collective-permute-start.24 = (bf16[16,256]{1,0:T(8,128)(2,1)S(1)}, bf16[16,256]{1,0:T(8,128)(2,1)S(1)}, u32[]{:S(2)}, u32[]{:S(2)}) collective-permute-start(bf16[16,256]{1,0:T(8,128)(2,1)S(1)} %get-tuple-element.122), channel_id=1, source_target_pairs={{0,6},{1,7},{2,0},{3,1},{4,2},{5,3},{6,4},{7,5},{8,14},{9,15},{10,... | collective-permute-start | bytes 24584 | tf_op jit(solution)/shard_map/ppermute | solution.py:491
  183.5 7.3 %collective-permute-start.25 = (bf16[16,256]{1,0:T(8,128)(2,1)S(1)}, bf16[16,256]{1,0:T(8,128)(2,1)S(1)}, u32[]{:S(2)}, u32[]{:S(2)}) collective-permute-start(bf16[16,256]{1,0:T(8,128)(2,1)S(1)} %get-tuple-element.123), channel_id=1, source_target_pairs={{0,7},{1,0},{2,1},{3,2},{4,3},{5,4},{6,5},{7,6},{8,15},{9,8},{10,9... | collective-permute-start | bytes 24584 | tf_op jit(solution)/shard_map/ppermute | solution.py:491
  (23 other events, 222.7 us)

commit v7 on v6

--- a/solution.py
+++ b/solution.py
@@ -11,7 +11,7 @@
 BF16 = jnp.bfloat16
 F32 = jnp.float32
 CAP = 16
-EARLY = (1, 2, 3, 5, 6, 7)
+EARLY = (1, 2, 4, 6, 7)
 META = 16
 
 
@@ -246,7 +246,7 @@
 
     gate_ref[...] = jnp.zeros_like(gate_ref)
     up_ref[...] = jnp.zeros_like(up_ref)
-    lax.fori_loop(0, 8, first, 0)
+    lax.fori_loop(0, 8, first, 0, unroll=8)
     gate = gate_ref[...]
     hidden_ref[...] = (gate * jax.nn.sigmoid(gate) * up_ref[...]).astype(BF16)
 
@@ -255,7 +255,7 @@
         put_chunk(out_ref, e, nn(hidden_ref[...], wd_ref[0, :, at]).astype(BF16))
         return 0
 
-    lax.fori_loop(0, 8, second, 0)
+    lax.fori_loop(0, 8, second, 0, unroll=8)
 
 
 def forward(x_rows, wg, wu, wd):
@@ -291,7 +291,7 @@
         return 0
 
     back_ref[...] = jnp.zeros_like(back_ref)
-    lax.fori_loop(0, 8, first, 0)
+    lax.fori_loop(0, 8, first, 0, unroll=8)
     back, gate = back_ref[...], gate_ref[...]
     sigma = jax.nn.sigmoid(gate)
     dgate_ref[...] = (back * up_ref[...] * sigma * (1.0 + gate * (1.0 - sigma))).astype(BF16)
@@ -303,7 +303,7 @@
         put_chunk(in_ref, e, piece.astype(BF16))
         return 0
 
-    lax.fori_loop(0, 8, second, 0)
+    lax.fori_loop(0, 8, second, 0, unroll=8)
 
 
 def backward(at, parts, gate, up, wg, wu, wd):

time: 192 us -> 190 us (0.990)
  Pallas kernels: 44.5 us -> 38 us
  starting transfers between devices: 85.6 us -> 92.1 us
  waiting for transfers between devices: 55.9 us -> 52.6 us
    ppermute x21, starting transfers between devices: 40.3 us -> 44 us  [spread(): lax.ppermute(arrays[shift], axes, [(i, (i + shift) % 8) for i in range(8)])]
    pallas_call x1, Pallas kernels: 12 us -> 8.69 us  [backward(): pl.pallas_call(backward_kernel, grid_spec=pltpu.PrefetchScalarGridSpec(nu...]
    ppermute x21, waiting for transfers between devices: 35.3 us -> 32 us  [spread(): lax.ppermute(arrays[shift], axes, [(i, (i + shift) % 8) for i in range(8)])]
    pallas_call x1, Pallas kernels: 11 us -> 7.88 us  [forward(): pl.pallas_call(forward_kernel, out_shape=[pltpu.HBM(x_rows.shape, BF16),...]
    all_to_all x5, starting transfers between devices: 40.9 us -> 43.7 us  [swap(): return lax.all_to_all(buffer, axes, split_axis=0, concat_axis=0, tiled=True)]
    unnamed x48 -> x52, local copies, waits for them, and re-layouts: 4.54 us -> 5.2 us
  transfers between devices with their start and end apart: 31 -> 31, of which waited for: 13 -> 13; matrix products, arithmetic and copies ran while one was open for 0% -> 0% of each run, Pallas kernels for 20% -> 17%
where the time goes in v7:
time: 190 us; the launch traced here: 189 us
  starting transfers between devices  92.1 us (48%)
  waiting for transfers between devices  52.6 us (28%)
  Pallas kernels  38 us (20%)
  local copies, waits for them, and re-layouts  5.2 us (3%)
    ppermute x21, starting transfers between devices, spread(): lax.ppermute(arrays[shift], axes, [(i, (i + shift) % 8) for i in range(8)])  44 us
    all_to_all x5, starting transfers between devices, swap(): return lax.all_to_all(buffer, axes, split_axis=0, concat_axis=0, tiled=True)  43.7 us
    ppermute x21, waiting for transfers between devices, spread(): lax.ppermute(arrays[shift], axes, [(i, (i + shift) % 8) for i in range(8)])  32 us
    all_to_all x5, waiting for transfers between devices, swap(): return lax.all_to_all(buffer, axes, split_axis=0, concat_axis=0, tiled=True)  10.5 us
    ppermute x5, waiting for transfers between devices, cross(): lax.ppermute(array, ('xl', 'core', 'xh'), [(i, i ^ 2 * away + over) for i...  10.2 us
    pallas_call x1, Pallas kernels, backward(): pl.pallas_call(backward_kernel, grid_spec=pltpu.PrefetchScalarGridSpec(nu...  8.69 us
    pallas_call x1, Pallas kernels, forward(): pl.pallas_call(forward_kernel, out_shape=[pltpu.HBM(x_rows.shape, BF16),...  7.88 us
    pallas_call x1, Pallas kernels, grads(): pl.pallas_call(grads_kernel, out_shape=[jax.ShapeDtypeStruct((1, width, f...  6.55 us
  transfers between devices with their start and end apart: 31, of which 13 were waited for; matrix products, arithmetic and copies ran while one was open for 0% of the time, Pallas kernels for 17%

profile of v7, /device:TPU:28, one launch (start us, length us, event | category | flops | bytes accessed | tf_op | source)
XLA Modules:
  0.0 188.9 jit_solution(13521363694236172478)
XLA Ops:
  2.5 8.5 %all-to-all-start = ((bf16[8,144,256]{2,1,0:T(8,128)(2,1)}), bf16[8,144,256]{2,1,0:T(8,128)(2,1)S(1)}, u32[]{:S(2)}, u32[]{:S(2)}) async-start(bf16[8,144,256]{2,1,0:T(8,128)(2,1)} %get-tuple-element.81), calls=%async_computation | async-start | bytes 1179648 | tf_op jit(solution)/shard_map/all_to_all | solution.py:486
  12.4 2.0 %pick_g.1 = (bf16[128,2048]{1,0:T(8,128)(2,1)S(1)}, bf16[128,2048]{1,0:T(8,128)(2,1)S(1)}, bf16[128,1024]{1,0:T(8,128)(2,1)S(1)}, bf16[128,1024]{1,0:T(8,128)(2,...) custom-call(s32[3]{0:T(128)S(1)} %pad_add_fusion.at_ref, bf16[128,2048]{1,0:T(8,128)(2,1)S(1)} %copy-done.3, ...), custom_call_target="tpu_custom_call" | custom-call | tf_op jit(solution)/shard_map/pick_g/pallas_call | solution.py:185
  19.6 4.7 %collective-permute-done.1.refs_2_ = bf16[128,1024]{1,0:T(8,128)(2,1)S(1)} collective-permute-done((bf16[128,1024]{1,0:T(8,128)(2,1)S(1)}, bf16[128,1024]{1,0:T(8,128)(2,1)S(1)}, u32[]{:S(2)}, u32[]{:S(2)}) %collective-permute-start.1) | collective-permute-done | bytes 262176 | tf_op jit(solution)/shard_map/ppermute | solution.py:506
  25.6 3.6 %collective-permute-done.3.refs_4_ = bf16[128,1024]{1,0:T(8,128)(2,1)S(1)} collective-permute-done((bf16[128,1024]{1,0:T(8,128)(2,1)S(1)}, bf16[128,1024]{1,0:T(8,128)(2,1)S(1)}, u32[]{:S(2)}, u32[]{:S(2)}) %collective-permute-start.3) | collective-permute-done | bytes 262176 | tf_op jit(solution)/shard_map/ppermute | solution.py:506
  29.8 2.3 %pick_x.1 = (bf16[32,128,256]{2,1,0:T(8,128)(2,1)}, f32[8,16,128]{2,1,0:T(8,128)S(1)}, f32[8,16,128]{2,1,0:T(8,128)S(1)}) custom-call(s32[1]{0:T(128)} %bitcast.1.at_ref.z_ref, bf16[8,144,256]{2,1,0:T(8,128)(2,1)S(1)} %all-to-all-done.x_ref), custom_call_target="tpu_custom_call" | custom-call | tf_op jit(solution)/shard_map/pick_x/pallas_call | solution.py:142
  32.1 7.9 %all-to-all-start.1 = ((bf16[32,128,256]{2,1,0:T(8,128)(2,1)}), bf16[32,128,256]{2,1,0:T(8,128)(2,1)S(1)}, u32[]{:S(2)}, u32[]{:S(2)}) async-start(bf16[32,128,256]{2,1,0:T(8,128)(2,1)} %get-tuple-element.83), calls=%async_computation.1 | async-start | bytes 4194304 | tf_op jit(solution)/shard_map/all_to_all | solution.py:486
  40.1 3.5 %turn_g.1 = (bf16[64,2048]{1,0:T(8,128)(2,1)}, bf16[64,2048]{1,0:T(8,128)(2,1)}, bf16[64,2048]{1,0:T(8,128)(2,1)}, bf16[64,2048]{1,0:T(8,128)(2,1)}, bf16[64,204...) custom-call(s32[3]{0:T(128)S(1)} %pad_add_fusion.at_ref, ...), custom_call_target="tpu_custom_call" | custom-call | tf_op jit(solution)/shard_map/turn_g/pallas_call | solution.py:210
  43.6 2.0 %collective-permute-start.5 = (bf16[64,2048]{1,0:T(8,128)(2,1)}, bf16[64,2048]{1,0:T(8,128)(2,1)S(1)}, u32[]{:S(2)}, u32[]{:S(2)}) collective-permute-start(bf16[64,2048]{1,0:T(8,128)(2,1)} %get-tuple-element.74), channel_id=1, source_target_pairs={{0,32},{32,64},{64,96},{96,128},{128,160},{160,192},{192,224},{224... | collective-permute-start | bytes 786440 | tf_op jit(solution)/shard_map/ppermute | solution.py:491
  45.6 2.4 %collective-permute-start.6 = (bf16[64,2048]{1,0:T(8,128)(2,1)}, bf16[64,2048]{1,0:T(8,128)(2,1)S(1)}, u32[]{:S(2)}, u32[]{:S(2)}) collective-permute-start(bf16[64,2048]{1,0:T(8,128)(2,1)} %get-tuple-element.75), channel_id=1, source_target_pairs={{0,64},{32,96},{64,128},{96,160},{128,192},{160,224},{192,0},{224,... | collective-permute-start | bytes 786440 | tf_op jit(solution)/shard_map/ppermute | solution.py:491
  48.0 2.7 %collective-permute-start.8 = (bf16[64,2048]{1,0:T(8,128)(2,1)}, bf16[64,2048]{1,0:T(8,128)(2,1)S(1)}, u32[]{:S(2)}, u32[]{:S(2)}) collective-permute-start(bf16[64,2048]{1,0:T(8,128)(2,1)} %get-tuple-element.77), channel_id=1, source_target_pairs={{0,128},{32,160},{64,192},{96,224},{128,0},{160,32},{192,64},{224,... | collective-permute-start | bytes 786440 | tf_op jit(solution)/shard_map/ppermute | solution.py:491
  50.7 3.6 %collective-permute-start.10 = (bf16[64,2048]{1,0:T(8,128)(2,1)}, bf16[64,2048]{1,0:T(8,128)(2,1)S(1)}, u32[]{:S(2)}, u32[]{:S(2)}) collective-permute-start(bf16[64,2048]{1,0:T(8,128)(2,1)} %get-tuple-element.79), channel_id=1, source_target_pairs={{0,192},{32,224},{64,0},{96,32},{128,64},{160,96},{192,128},{224,1... | collective-permute-start | bytes 786440 | tf_op jit(solution)/shard_map/ppermute | solution.py:491
  55.7 10.5 %all-to-all-done.1.x_ref = bf16[32,128,256]{2,1,0:T(8,128)(2,1)S(1)} async-done(((bf16[32,128,256]{2,1,0:T(8,128)(2,1)}), bf16[32,128,256]{2,1,0:T(8,128)(2,1)S(1)}, u32[]{:S(2)}, u32[]{:S(2)}) %all-to-all-start.1) | async-done | bytes 2097184 | tf_op jit(solution)/shard_map/all_to_all | solution.py:486
  66.2 7.9 %forward.1 = (bf16[32,128,256]{2,1,0:T(8,128)(2,1)}, f32[512,384]{1,0:T(8,128)}, f32[512,384]{1,0:T(8,128)}, bf16[512,384]{1,0:T(8,128)(2,1)}) custom-call(bf16[32,128,256]{2,1,0:T(8,128)(2,1)S(1)} %all-to-all-done.1.x_ref, bf16[1,2048,384]{2,1,0:T(8,128)(2,1)} %refs_10_.1, bf16[1,2048,384]{2,1,0:T(8,128)(2,1)} %refs_11_.1, bf16[1,384,2048]{2,1,0:T(8,128)(2,1)} %refs_12_.1), custom_call_target="tpu_custom_call" | custom-call | flops 2415919104 | bytes 11534336 | tf_op jit(solution)/shard_map/forward/pallas_call | solution.py:263
  74.1 1.9 %collective-permute-done.10.refs_6_ = bf16[64,2048]{1,0:T(8,128)(2,1)S(1)} collective-permute-done((bf16[64,2048]{1,0:T(8,128)(2,1)}, bf16[64,2048]{1,0:T(8,128)(2,1)S(1)}, u32[]{:S(2)}, u32[]{:S(2)}) %collective-permute-start.10) | collective-permute-done | bytes 262176 | tf_op jit(solution)/shard_map/ppermute | solution.py:491
  76.0 3.4 %collective-permute-done.11.refs_7_ = bf16[64,2048]{1,0:T(8,128)(2,1)S(1)} collective-permute-done((bf16[64,2048]{1,0:T(8,128)(2,1)}, bf16[64,2048]{1,0:T(8,128)(2,1)S(1)}, u32[]{:S(2)}, u32[]{:S(2)}) %collective-permute-start.11) | collective-permute-done | bytes 262176 | tf_op jit(solution)/shard_map/ppermute | solution.py:491
  80.2 7.6 %all-to-all-start.3 = ((bf16[32,128,256]{2,1,0:T(8,128)(2,1)}), bf16[32,128,256]{2,1,0:T(8,128)(2,1)}, u32[]{:S(2)}, u32[]{:S(2)}) async-start(bf16[32,128,256]{2,1,0:T(8,128)(2,1)} %get-tuple-element.91), calls=%async_computation.3 | async-start | bytes 4194304 | tf_op jit(solution)/shard_map/all_to_all | solution.py:486
  87.8 5.2 %collective-permute-start.7 = (bf16[64,2048]{1,0:T(8,128)(2,1)S(1)}, bf16[64,2048]{1,0:T(8,128)(2,1)S(1)}, u32[]{:S(2)}, u32[]{:S(2)}) collective-permute-start(bf16[64,2048]{1,0:T(8,128)(2,1)S(1)} %copy-done.19), channel_id=1, source_target_pairs={{0,96},{32,128},{64,160},{96,192},{128,224},{160,0},{192,32},{224,... | collective-permute-start | bytes 786440 | tf_op jit(solution)/shard_map/ppermute | solution.py:491
  93.1 17.2 %collective-permute-done.7.refs_3_ = bf16[64,2048]{1,0:T(8,128)(2,1)S(1)} collective-permute-done((bf16[64,2048]{1,0:T(8,128)(2,1)S(1)}, bf16[64,2048]{1,0:T(8,128)(2,1)S(1)}, u32[]{:S(2)}, u32[]{:S(2)}) %collective-permute-start.7) | collective-permute-done | bytes 262176 | tf_op jit(solution)/shard_map/ppermute | solution.py:491
  112.3 8.7 %backward.1 = (bf16[4,128,2048]{2,1,0:T(8,128)(2,1)}, bf16[32,128,256]{2,1,0:T(8,128)(2,1)}, bf16[512,384]{1,0:T(8,128)(2,1)}, bf16[512,384]{1,0:T(8,128)(2,1)}) custom-call(s32[3]{0:T(128)S(1)} %pad_add_fusion.at_ref, bf16[64,2048]{1,0:T(8,128)(2,1)} %get-tuple-element.73.refs_0_, bf16[64,2048]{1,0:T(8,128)(2,1)} %copy-done.18, ...), custom_call_target="tpu_custom_call" | custom-call | flops 2415919104 | bytes 13631488 | tf_op jit(solution)/shard_map/backward/pallas_call | solution.py:312
  121.0 7.5 %all-to-all-start.2 = ((bf16[32,128,256]{2,1,0:T(8,128)(2,1)}), bf16[32,128,256]{2,1,0:T(8,128)(2,1)S(1)}, u32[]{:S(2)}, u32[]{:S(2)}) async-start(bf16[32,128,256]{2,1,0:T(8,128)(2,1)} %get-tuple-element.87), calls=%async_computation.2 | async-start | bytes 4194304 | tf_op jit(solution)/shard_map/all_to_all | solution.py:486
  128.5 2.8 %join_out.1 = (f32[128,256]{1,0:T(8,128)S(1)}, bf16[128,256]{1,0:T(8,128)(2,1)S(1)}, bf16[128,256]{1,0:T(8,128)(2,1)S(1)}, bf16[128,256]{1,0:T(8,128)(2,1)S(1)},...) custom-call(s32[1]{0:T(128)} %bitcast.1.at_ref.z_ref, ...), custom_call_target="tpu_custom_call" | custom-call | tf_op jit(solution)/shard_map/join_out/pallas_call | solution.py:395
  131.3 5.0 %collective-permute-start.12 = (bf16[128,256]{1,0:T(8,128)(2,1)S(1)}, bf16[128,256]{1,0:T(8,128)(2,1)S(1)}, u32[]{:S(2)}, u32[]{:S(2)}) collective-permute-start(bf16[128,256]{1,0:T(8,128)(2,1)S(1)} %get-tuple-element.101), channel_id=1, source_target_pairs={{0,32},{32,64},{64,96},{96,128},{128,160},{160,192},{192,224},{224... | collective-permute-start | bytes 196616 | tf_op jit(solution)/shard_map/ppermute | solution.py:491
  136.3 3.1 %collective-permute-start.14 = (bf16[128,256]{1,0:T(8,128)(2,1)S(1)}, bf16[128,256]{1,0:T(8,128)(2,1)S(1)}, u32[]{:S(2)}, u32[]{:S(2)}) collective-permute-start(bf16[128,256]{1,0:T(8,128)(2,1)S(1)} %get-tuple-element.103), channel_id=1, source_target_pairs={{0,96},{32,128},{64,160},{96,192},{128,224},{160,0},{192,32},{224,... | collective-permute-start | bytes 196616 | tf_op jit(solution)/shard_map/ppermute | solution.py:491
  139.4 3.0 %collective-permute-start.15 = (bf16[128,256]{1,0:T(8,128)(2,1)S(1)}, bf16[128,256]{1,0:T(8,128)(2,1)S(1)}, u32[]{:S(2)}, u32[]{:S(2)}) collective-permute-start(bf16[128,256]{1,0:T(8,128)(2,1)S(1)} %get-tuple-element.104), channel_id=1, source_target_pairs={{0,128},{32,160},{64,192},{96,224},{128,0},{160,32},{192,64},{224,... | collective-permute-start | bytes 196616 | tf_op jit(solution)/shard_map/ppermute | solution.py:491
  148.6 6.5 %grads.1 = (bf16[1,2048,384]{2,1,0:T(8,128)(2,1)}, bf16[1,2048,384]{2,1,0:T(8,128)(2,1)}, bf16[1,384,2048]{2,1,0:T(8,128)(2,1)}) custom-call(bf16[32,128,256]{2,1,0:T(8,128)(2,1)S(1)} %copy-done.1, bf16[4,128,2048]{2,1,0:T(8,128)(2,1)S(1)} %copy-done.6, bf16[512,384]{1,0:T(8,128)(2,1)S(1)} %copy-done.11, bf16[512,384]{1,0:T(8,128)(2,1)S(1)} %copy-done.9, ...), custom_call_target="tpu_custom_call" | custom-call | flops 2415919104 | bytes 10485760 | tf_op jit(solution)/shard_map/grads/pallas_call | solution.py:357
  156.9 12.2 %all-to-all-start.4 = ((bf16[64,16,256]{2,1,0:T(8,128)(2,1)}), bf16[64,16,256]{2,1,0:T(8,128)(2,1)S(1)}, u32[]{:S(2)}, u32[]{:S(2)}) async-start(bf16[64,16,256]{2,1,0:T(8,128)(2,1)} %join_in.1), calls=%async_computation.4 | async-start | bytes 1048576 | tf_op jit(solution)/shard_map/all_to_all | solution.py:486
  169.9 2.5 %collective-permute-start.20 = (bf16[16,256]{1,0:T(8,128)(2,1)S(1)}, bf16[16,256]{1,0:T(8,128)(2,1)S(1)}, u32[]{:S(2)}, u32[]{:S(2)}) collective-permute-start(bf16[16,256]{1,0:T(8,128)(2,1)S(1)} %get-tuple-element.118), channel_id=1, source_target_pairs={{0,2},{1,3},{2,4},{3,5},{4,6},{5,7},{6,0},{7,1},{8,10},{9,11},{10,... | collective-permute-start | bytes 24584 | tf_op jit(solution)/shard_map/ppermute | solution.py:491
  172.4 2.4 %collective-permute-start.21 = (bf16[16,256]{1,0:T(8,128)(2,1)S(1)}, bf16[16,256]{1,0:T(8,128)(2,1)S(1)}, u32[]{:S(2)}, u32[]{:S(2)}) collective-permute-start(bf16[16,256]{1,0:T(8,128)(2,1)S(1)} %get-tuple-element.119), channel_id=1, source_target_pairs={{0,3},{1,4},{2,5},{3,6},{4,7},{5,0},{6,1},{7,2},{8,11},{9,12},{10,... | collective-permute-start | bytes 24584 | tf_op jit(solution)/shard_map/ppermute | solution.py:491
  175.4 3.2 %collective-permute-start.23 = (bf16[16,256]{1,0:T(8,128)(2,1)S(1)}, bf16[16,256]{1,0:T(8,128)(2,1)S(1)}, u32[]{:S(2)}, u32[]{:S(2)}) collective-permute-start(bf16[16,256]{1,0:T(8,128)(2,1)S(1)} %get-tuple-element.121), channel_id=1, source_target_pairs={{0,5},{1,6},{2,7},{3,0},{4,1},{5,2},{6,3},{7,4},{8,13},{9,14},{10,... | collective-permute-start | bytes 24584 | tf_op jit(solution)/shard_map/ppermute | solution.py:491
  178.6 2.4 %collective-permute-start.24 = (bf16[16,256]{1,0:T(8,128)(2,1)S(1)}, bf16[16,256]{1,0:T(8,128)(2,1)S(1)}, u32[]{:S(2)}, u32[]{:S(2)}) collective-permute-start(bf16[16,256]{1,0:T(8,128)(2,1)S(1)} %get-tuple-element.122), channel_id=1, source_target_pairs={{0,6},{1,7},{2,0},{3,1},{4,2},{5,3},{6,4},{7,5},{8,14},{9,15},{10,... | collective-permute-start | bytes 24584 | tf_op jit(solution)/shard_map/ppermute | solution.py:491
  181.5 4.7 %collective-permute-done.24.refs_6_ = bf16[16,256]{1,0:T(8,128)(2,1)S(1)} collective-permute-done((bf16[16,256]{1,0:T(8,128)(2,1)S(1)}, bf16[16,256]{1,0:T(8,128)(2,1)S(1)}, u32[]{:S(2)}, u32[]{:S(2)}) %collective-permute-start.24) | collective-permute-done | bytes 8224 | tf_op jit(solution)/shard_map/ppermute | solution.py:491
  186.2 2.1 %collective-permute-done.25.refs_7_ = bf16[16,256]{1,0:T(8,128)(2,1)S(1)} collective-permute-done((bf16[16,256]{1,0:T(8,128)(2,1)S(1)}, bf16[16,256]{1,0:T(8,128)(2,1)S(1)}, u32[]{:S(2)}, u32[]{:S(2)}) %collective-permute-start.25) | collective-permute-done | bytes 8224 | tf_op jit(solution)/shard_map/ppermute | solution.py:491
  (94 shorter events, 25.1 us)
Async XLA Ops:
  2.5 27.4 %all-to-all-start = ((bf16[8,144,256]{2,1,0:T(8,128)(2,1)}), bf16[8,144,256]{2,1,0:T(8,128)(2,1)S(1)}, u32[]{:S(2)}, u32[]{:S(2)}) async-start(bf16[8,144,256]{2,1,0:T(8,128)(2,1)} %get-tuple-element.81), calls=%async_computation | async-start | bytes 1179648 | tf_op jit(solution)/shard_map/all_to_all | solution.py:486
  15.2 14.6 %collective-permute-start = (bf16[128,2048]{1,0:T(8,128)(2,1)S(1)}, bf16[128,2048]{1,0:T(8,128)(2,1)S(1)}, u32[]{:S(2)}, u32[]{:S(2)}) collective-permute-start(bf16[128,2048]{1,0:T(8,128)(2,1)S(1)} %get-tuple-element.68), channel_id=1, source_target_pairs={{0,8},{4,12},{8,0},{12,4},{16,24},{20,28},{24,16},{28,20},{1,9},{5... | collective-permute-start | bytes 1572872 | tf_op jit(solution)/shard_map/ppermute | solution.py:506
  15.2 9.1 %collective-permute-start.1 = (bf16[128,1024]{1,0:T(8,128)(2,1)S(1)}, bf16[128,1024]{1,0:T(8,128)(2,1)S(1)}, u32[]{:S(2)}, u32[]{:S(2)}) collective-permute-start(bf16[128,1024]{1,0:T(8,128)(2,1)S(1)} %get-tuple-element.69), channel_id=1, source_target_pairs={{0,16},{4,20},{8,24},{12,28},{16,0},{20,4},{24,8},{28,12},{1,17},{... | collective-permute-start | bytes 786440 | tf_op jit(solution)/shard_map/ppermute | solution.py:506
  16.4 9.1 %collective-permute-start.2 = (bf16[128,1024]{1,0:T(8,128)(2,1)S(1)}, bf16[128,1024]{1,0:T(8,128)(2,1)S(1)}, u32[]{:S(2)}, u32[]{:S(2)}) collective-permute-start(bf16[128,1024]{1,0:T(8,128)(2,1)S(1)} %get-tuple-element.70), channel_id=1, source_target_pairs={{0,20},{4,16},{8,28},{12,24},{16,4},{20,0},{24,12},{28,8},{1,21},{... | collective-permute-start | bytes 786440 | tf_op jit(solution)/shard_map/ppermute | solution.py:506
  16.4 12.7 %collective-permute-start.3 = (bf16[128,1024]{1,0:T(8,128)(2,1)S(1)}, bf16[128,1024]{1,0:T(8,128)(2,1)S(1)}, u32[]{:S(2)}, u32[]{:S(2)}) collective-permute-start(bf16[128,1024]{1,0:T(8,128)(2,1)S(1)} %get-tuple-element.71), channel_id=1, source_target_pairs={{0,24},{4,28},{8,16},{12,20},{16,8},{20,12},{24,0},{28,4},{1,25},{... | collective-permute-start | bytes 786440 | tf_op jit(solution)/shard_map/ppermute | solution.py:506
  17.9 11.8 %collective-permute-start.4 = (bf16[128,1024]{1,0:T(8,128)(2,1)S(1)}, bf16[128,1024]{1,0:T(8,128)(2,1)S(1)}, u32[]{:S(2)}, u32[]{:S(2)}) collective-permute-start(bf16[128,1024]{1,0:T(8,128)(2,1)S(1)} %get-tuple-element.72), channel_id=1, source_target_pairs={{0,28},{4,24},{8,20},{12,16},{16,12},{20,8},{24,4},{28,0},{1,29},{... | collective-permute-start | bytes 786440 | tf_op jit(solution)/shard_map/ppermute | solution.py:506
  32.1 34.0 %all-to-all-start.1 = ((bf16[32,128,256]{2,1,0:T(8,128)(2,1)}), bf16[32,128,256]{2,1,0:T(8,128)(2,1)S(1)}, u32[]{:S(2)}, u32[]{:S(2)}) async-start(bf16[32,128,256]{2,1,0:T(8,128)(2,1)} %get-tuple-element.83), calls=%async_computation.1 | async-start | bytes 4194304 | tf_op jit(solution)/shard_map/all_to_all | solution.py:486
  43.6 30.4 %collective-permute-start.5 = (bf16[64,2048]{1,0:T(8,128)(2,1)}, bf16[64,2048]{1,0:T(8,128)(2,1)S(1)}, u32[]{:S(2)}, u32[]{:S(2)}) collective-permute-start(bf16[64,2048]{1,0:T(8,128)(2,1)} %get-tuple-element.74), channel_id=1, source_target_pairs={{0,32},{32,64},{64,96},{96,128},{128,160},{160,192},{192,224},{224... | collective-permute-start | bytes 786440 | tf_op jit(solution)/shard_map/ppermute | solution.py:491
  45.6 28.4 %collective-permute-start.6 = (bf16[64,2048]{1,0:T(8,128)(2,1)}, bf16[64,2048]{1,0:T(8,128)(2,1)S(1)}, u32[]{:S(2)}, u32[]{:S(2)}) collective-permute-start(bf16[64,2048]{1,0:T(8,128)(2,1)} %get-tuple-element.75), channel_id=1, source_target_pairs={{0,64},{32,96},{64,128},{96,160},{128,192},{160,224},{192,0},{224,... | collective-permute-start | bytes 786440 | tf_op jit(solution)/shard_map/ppermute | solution.py:491
  48.0 26.1 %collective-permute-start.8 = (bf16[64,2048]{1,0:T(8,128)(2,1)}, bf16[64,2048]{1,0:T(8,128)(2,1)S(1)}, u32[]{:S(2)}, u32[]{:S(2)}) collective-permute-start(bf16[64,2048]{1,0:T(8,128)(2,1)} %get-tuple-element.77), channel_id=1, source_target_pairs={{0,128},{32,160},{64,192},{96,224},{128,0},{160,32},{192,64},{224,... | collective-permute-start | bytes 786440 | tf_op jit(solution)/shard_map/ppermute | solution.py:491
  50.7 25.3 %collective-permute-start.10 = (bf16[64,2048]{1,0:T(8,128)(2,1)}, bf16[64,2048]{1,0:T(8,128)(2,1)S(1)}, u32[]{:S(2)}, u32[]{:S(2)}) collective-permute-start(bf16[64,2048]{1,0:T(8,128)(2,1)} %get-tuple-element.79), channel_id=1, source_target_pairs={{0,192},{32,224},{64,0},{96,32},{128,64},{160,96},{192,128},{224,1... | collective-permute-start | bytes 786440 | tf_op jit(solution)/shard_map/ppermute | solution.py:491
  54.3 25.2 %collective-permute-start.11 = (bf16[64,2048]{1,0:T(8,128)(2,1)}, bf16[64,2048]{1,0:T(8,128)(2,1)S(1)}, u32[]{:S(2)}, u32[]{:S(2)}) collective-permute-start(bf16[64,2048]{1,0:T(8,128)(2,1)} %get-tuple-element.80), channel_id=1, source_target_pairs={{0,224},{32,0},{64,32},{96,64},{128,96},{160,128},{192,160},{224,1... | collective-permute-start | bytes 786440 | tf_op jit(solution)/shard_map/ppermute | solution.py:491
  79.5 32.8 %copy-start.7 = (f32[512,384]{1,0:T(8,128)S(1)}, f32[512,384]{1,0:T(8,128)}, u32[]{:S(2)}) copy-start(f32[512,384]{1,0:T(8,128)} %get-tuple-element.85.refs_8_) | copy-start | bytes 2359300
  80.2 40.8 %all-to-all-start.3 = ((bf16[32,128,256]{2,1,0:T(8,128)(2,1)}), bf16[32,128,256]{2,1,0:T(8,128)(2,1)}, u32[]{:S(2)}, u32[]{:S(2)}) async-start(bf16[32,128,256]{2,1,0:T(8,128)(2,1)} %get-tuple-element.91), calls=%async_computation.3 | async-start | bytes 4194304 | tf_op jit(solution)/shard_map/all_to_all | solution.py:486
  87.8 22.5 %collective-permute-start.7 = (bf16[64,2048]{1,0:T(8,128)(2,1)S(1)}, bf16[64,2048]{1,0:T(8,128)(2,1)S(1)}, u32[]{:S(2)}, u32[]{:S(2)}) collective-permute-start(bf16[64,2048]{1,0:T(8,128)(2,1)S(1)} %copy-done.19), channel_id=1, source_target_pairs={{0,96},{32,128},{64,160},{96,192},{128,224},{160,0},{192,32},{224,... | collective-permute-start | bytes 786440 | tf_op jit(solution)/shard_map/ppermute | solution.py:491
  93.0 18.6 %collective-permute-start.9 = (bf16[64,2048]{1,0:T(8,128)(2,1)S(1)}, bf16[64,2048]{1,0:T(8,128)(2,1)S(1)}, u32[]{:S(2)}, u32[]{:S(2)}) collective-permute-start(bf16[64,2048]{1,0:T(8,128)(2,1)S(1)} %copy-done.17), channel_id=1, source_target_pairs={{0,160},{32,192},{64,224},{96,0},{128,32},{160,64},{192,96},{224,1... | collective-permute-start | bytes 786440 | tf_op jit(solution)/shard_map/ppermute | solution.py:491
  121.0 34.3 %all-to-all-start.2 = ((bf16[32,128,256]{2,1,0:T(8,128)(2,1)}), bf16[32,128,256]{2,1,0:T(8,128)(2,1)S(1)}, u32[]{:S(2)}, u32[]{:S(2)}) async-start(bf16[32,128,256]{2,1,0:T(8,128)(2,1)} %get-tuple-element.87), calls=%async_computation.2 | async-start | bytes 4194304 | tf_op jit(solution)/shard_map/all_to_all | solution.py:486
  131.3 12.7 %collective-permute-start.12 = (bf16[128,256]{1,0:T(8,128)(2,1)S(1)}, bf16[128,256]{1,0:T(8,128)(2,1)S(1)}, u32[]{:S(2)}, u32[]{:S(2)}) collective-permute-start(bf16[128,256]{1,0:T(8,128)(2,1)S(1)} %get-tuple-element.101), channel_id=1, source_target_pairs={{0,32},{32,64},{64,96},{96,128},{128,160},{160,192},{192,224},{224... | collective-permute-start | bytes 196616 | tf_op jit(solution)/shard_map/ppermute | solution.py:491
  136.3 10.0 %collective-permute-start.13 = (bf16[128,256]{1,0:T(8,128)(2,1)S(1)}, bf16[128,256]{1,0:T(8,128)(2,1)S(1)}, u32[]{:S(2)}, u32[]{:S(2)}) collective-permute-start(bf16[128,256]{1,0:T(8,128)(2,1)S(1)} %get-tuple-element.102), channel_id=1, source_target_pairs={{0,64},{32,96},{64,128},{96,160},{128,192},{160,224},{192,0},{224,... | collective-permute-start | bytes 196616 | tf_op jit(solution)/shard_map/ppermute | solution.py:491
  136.3 18.8 %collective-permute-start.14 = (bf16[128,256]{1,0:T(8,128)(2,1)S(1)}, bf16[128,256]{1,0:T(8,128)(2,1)S(1)}, u32[]{:S(2)}, u32[]{:S(2)}) collective-permute-start(bf16[128,256]{1,0:T(8,128)(2,1)S(1)} %get-tuple-element.103), channel_id=1, source_target_pairs={{0,96},{32,128},{64,160},{96,192},{128,224},{160,0},{192,32},{224,... | collective-permute-start | bytes 196616 | tf_op jit(solution)/shard_map/ppermute | solution.py:491
  139.4 15.7 %collective-permute-start.15 = (bf16[128,256]{1,0:T(8,128)(2,1)S(1)}, bf16[128,256]{1,0:T(8,128)(2,1)S(1)}, u32[]{:S(2)}, u32[]{:S(2)}) collective-permute-start(bf16[128,256]{1,0:T(8,128)(2,1)S(1)} %get-tuple-element.104), channel_id=1, source_target_pairs={{0,128},{32,160},{64,192},{96,224},{128,0},{160,32},{192,64},{224,... | collective-permute-start | bytes 196616 | tf_op jit(solution)/shard_map/ppermute | solution.py:491
  142.4 12.8 %collective-permute-start.16 = (bf16[128,256]{1,0:T(8,128)(2,1)S(1)}, bf16[128,256]{1,0:T(8,128)(2,1)S(1)}, u32[]{:S(2)}, u32[]{:S(2)}) collective-permute-start(bf16[128,256]{1,0:T(8,128)(2,1)S(1)} %get-tuple-element.105), channel_id=1, source_target_pairs={{0,160},{32,192},{64,224},{96,0},{128,32},{160,64},{192,96},{224,1... | collective-permute-start | bytes 196616 | tf_op jit(solution)/shard_map/ppermute | solution.py:491
  144.0 11.2 %collective-permute-start.17 = (bf16[128,256]{1,0:T(8,128)(2,1)S(1)}, bf16[128,256]{1,0:T(8,128)(2,1)S(1)}, u32[]{:S(2)}, u32[]{:S(2)}) collective-permute-start(bf16[128,256]{1,0:T(8,128)(2,1)S(1)} %get-tuple-element.106), channel_id=1, source_target_pairs={{0,192},{32,224},{64,0},{96,32},{128,64},{160,96},{192,128},{224,1... | collective-permute-start | bytes 196616 | tf_op jit(solution)/shard_map/ppermute | solution.py:491
  146.3 8.8 %collective-permute-start.18 = (bf16[128,256]{1,0:T(8,128)(2,1)S(1)}, bf16[128,256]{1,0:T(8,128)(2,1)S(1)}, u32[]{:S(2)}, u32[]{:S(2)}) collective-permute-start(bf16[128,256]{1,0:T(8,128)(2,1)S(1)} %get-tuple-element.107), channel_id=1, source_target_pairs={{0,224},{32,0},{64,32},{96,64},{128,96},{160,128},{192,160},{224,1... | collective-permute-start | bytes 196616 | tf_op jit(solution)/shard_map/ppermute | solution.py:491
  156.9 31.3 %all-to-all-start.4 = ((bf16[64,16,256]{2,1,0:T(8,128)(2,1)}), bf16[64,16,256]{2,1,0:T(8,128)(2,1)S(1)}, u32[]{:S(2)}, u32[]{:S(2)}) async-start(bf16[64,16,256]{2,1,0:T(8,128)(2,1)} %join_in.1), calls=%async_computation.4 | async-start | bytes 1048576 | tf_op jit(solution)/shard_map/all_to_all | solution.py:486
  169.2 9.4 %collective-permute-start.19 = (bf16[16,256]{1,0:T(8,128)(2,1)S(1)}, bf16[16,256]{1,0:T(8,128)(2,1)S(1)}, u32[]{:S(2)}, u32[]{:S(2)}) collective-permute-start(bf16[16,256]{1,0:T(8,128)(2,1)S(1)} %get-tuple-element.117), channel_id=1, source_target_pairs={{0,1},{1,2},{2,3},{3,4},{4,5},{5,6},{6,7},{7,0},{8,9},{9,10},{10,1... | collective-permute-start | bytes 24584 | tf_op jit(solution)/shard_map/ppermute | solution.py:491
  169.9 11.0 %collective-permute-start.20 = (bf16[16,256]{1,0:T(8,128)(2,1)S(1)}, bf16[16,256]{1,0:T(8,128)(2,1)S(1)}, u32[]{:S(2)}, u32[]{:S(2)}) collective-permute-start(bf16[16,256]{1,0:T(8,128)(2,1)S(1)} %get-tuple-element.118), channel_id=1, source_target_pairs={{0,2},{1,3},{2,4},{3,5},{4,6},{5,7},{6,0},{7,1},{8,10},{9,11},{10,... | collective-permute-start | bytes 24584 | tf_op jit(solution)/shard_map/ppermute | solution.py:491
  172.4 8.6 %collective-permute-start.21 = (bf16[16,256]{1,0:T(8,128)(2,1)S(1)}, bf16[16,256]{1,0:T(8,128)(2,1)S(1)}, u32[]{:S(2)}, u32[]{:S(2)}) collective-permute-start(bf16[16,256]{1,0:T(8,128)(2,1)S(1)} %get-tuple-element.119), channel_id=1, source_target_pairs={{0,3},{1,4},{2,5},{3,6},{4,7},{5,0},{6,1},{7,2},{8,11},{9,12},{10,... | collective-permute-start | bytes 24584 | tf_op jit(solution)/shard_map/ppermute | solution.py:491
  174.8 6.2 %collective-permute-start.22 = (bf16[16,256]{1,0:T(8,128)(2,1)S(1)}, bf16[16,256]{1,0:T(8,128)(2,1)S(1)}, u32[]{:S(2)}, u32[]{:S(2)}) collective-permute-start(bf16[16,256]{1,0:T(8,128)(2,1)S(1)} %get-tuple-element.120), channel_id=1, source_target_pairs={{0,4},{1,5},{2,6},{3,7},{4,0},{5,1},{6,2},{7,3},{8,12},{9,13},{10,... | collective-permute-start | bytes 24584 | tf_op jit(solution)/shard_map/ppermute | solution.py:491
  175.4 6.1 %collective-permute-start.23 = (bf16[16,256]{1,0:T(8,128)(2,1)S(1)}, bf16[16,256]{1,0:T(8,128)(2,1)S(1)}, u32[]{:S(2)}, u32[]{:S(2)}) collective-permute-start(bf16[16,256]{1,0:T(8,128)(2,1)S(1)} %get-tuple-element.121), channel_id=1, source_target_pairs={{0,5},{1,6},{2,7},{3,0},{4,1},{5,2},{6,3},{7,4},{8,13},{9,14},{10,... | collective-permute-start | bytes 24584 | tf_op jit(solution)/shard_map/ppermute | solution.py:491
  178.6 7.6 %collective-permute-start.24 = (bf16[16,256]{1,0:T(8,128)(2,1)S(1)}, bf16[16,256]{1,0:T(8,128)(2,1)S(1)}, u32[]{:S(2)}, u32[]{:S(2)}) collective-permute-start(bf16[16,256]{1,0:T(8,128)(2,1)S(1)} %get-tuple-element.122), channel_id=1, source_target_pairs={{0,6},{1,7},{2,0},{3,1},{4,2},{5,3},{6,4},{7,5},{8,14},{9,15},{10,... | collective-permute-start | bytes 24584 | tf_op jit(solution)/shard_map/ppermute | solution.py:491
  181.0 7.3 %collective-permute-start.25 = (bf16[16,256]{1,0:T(8,128)(2,1)S(1)}, bf16[16,256]{1,0:T(8,128)(2,1)S(1)}, u32[]{:S(2)}, u32[]{:S(2)}) collective-permute-start(bf16[16,256]{1,0:T(8,128)(2,1)S(1)} %get-tuple-element.123), channel_id=1, source_target_pairs={{0,7},{1,0},{2,1},{3,2},{4,3},{5,4},{6,5},{7,6},{8,15},{9,8},{10,9... | collective-permute-start | bytes 24584 | tf_op jit(solution)/shard_map/ppermute | solution.py:491
  (25 other events, 217.6 us)

commit v8 on v7

--- a/solution.py
+++ b/solution.py
@@ -348,7 +348,7 @@
         gd_ref[0, :, at] = tn(hidden_ref[...], columns(g_ref, at)).astype(BF16)
         return 0
 
-    lax.fori_loop(0, 8, step, 0)
+    lax.fori_loop(0, 8, step, 0, unroll=8)
 
 
 def grads(x_rows, g_rows, hidden, dgate, dup):

time: 190 us -> 188 us (0.989)
  transfers between devices with their start and end apart: 31 -> 31, of which waited for: 13 -> 14; matrix products, arithmetic and copies ran while one was open for 0% -> 0% of each run, Pallas kernels for 17% -> 16%
where the time goes in v8:
time: 188 us
  starting transfers between devices  91.6 us (49%)
  waiting for transfers between devices  53.3 us (28%)
  Pallas kernels  36.7 us (20%)
  local copies, waits for them, and re-layouts  5.2 us (3%)
    ppermute x21, starting transfers between devices, spread(): lax.ppermute(arrays[shift], axes, [(i, (i + shift) % 8) for i in range(8)])  43.8 us
    all_to_all x5, starting transfers between devices, swap(): return lax.all_to_all(buffer, axes, split_axis=0, concat_axis=0, tiled=True)  43.4 us
    ppermute x21, waiting for transfers between devices, spread(): lax.ppermute(arrays[shift], axes, [(i, (i + shift) % 8) for i in range(8)])  32.6 us
    all_to_all x5, waiting for transfers between devices, swap(): return lax.all_to_all(buffer, axes, split_axis=0, concat_axis=0, tiled=True)  10.5 us
    ppermute x5, waiting for transfers between devices, cross(): lax.ppermute(array, ('xl', 'core', 'xh'), [(i, i ^ 2 * away + over) for i...  10.2 us
    pallas_call x1, Pallas kernels, backward(): pl.pallas_call(backward_kernel, grid_spec=pltpu.PrefetchScalarGridSpec(nu...  8.69 us
    pallas_call x1, Pallas kernels, forward(): pl.pallas_call(forward_kernel, out_shape=[pltpu.HBM(x_rows.shape, BF16),...  7.88 us
    pallas_call x1, Pallas kernels, grads(): pl.pallas_call(grads_kernel, out_shape=[jax.ShapeDtypeStruct((1, width, f...  5.24 us
  transfers between devices with their start and end apart: 31, of which 14 were waited for; matrix products, arithmetic and copies ran while one was open for 0% of the time, Pallas kernels for 16%

profile of v8, /device:TPU:28, one launch (start us, length us, event | category | flops | bytes accessed | tf_op | source)
XLA Modules:
  0.0 187.8 jit_solution(8290059548226669489)
XLA Ops:
  2.5 8.5 %all-to-all-start = ((bf16[8,144,256]{2,1,0:T(8,128)(2,1)}), bf16[8,144,256]{2,1,0:T(8,128)(2,1)S(1)}, u32[]{:S(2)}, u32[]{:S(2)}) async-start(bf16[8,144,256]{2,1,0:T(8,128)(2,1)} %get-tuple-element.81), calls=%async_computation | async-start | bytes 1179648 | tf_op jit(solution)/shard_map/all_to_all | solution.py:486
  12.4 2.0 %pick_g.1 = (bf16[128,2048]{1,0:T(8,128)(2,1)S(1)}, bf16[128,2048]{1,0:T(8,128)(2,1)S(1)}, bf16[128,1024]{1,0:T(8,128)(2,1)S(1)}, bf16[128,1024]{1,0:T(8,128)(2,...) custom-call(s32[3]{0:T(128)S(1)} %pad_add_fusion.at_ref, bf16[128,2048]{1,0:T(8,128)(2,1)S(1)} %copy-done.3, ...), custom_call_target="tpu_custom_call" | custom-call | tf_op jit(solution)/shard_map/pick_g/pallas_call | solution.py:185
  19.6 4.7 %collective-permute-done.1.refs_2_ = bf16[128,1024]{1,0:T(8,128)(2,1)S(1)} collective-permute-done((bf16[128,1024]{1,0:T(8,128)(2,1)S(1)}, bf16[128,1024]{1,0:T(8,128)(2,1)S(1)}, u32[]{:S(2)}, u32[]{:S(2)}) %collective-permute-start.1) | collective-permute-done | bytes 262176 | tf_op jit(solution)/shard_map/ppermute | solution.py:506
  25.6 3.6 %collective-permute-done.3.refs_4_ = bf16[128,1024]{1,0:T(8,128)(2,1)S(1)} collective-permute-done((bf16[128,1024]{1,0:T(8,128)(2,1)S(1)}, bf16[128,1024]{1,0:T(8,128)(2,1)S(1)}, u32[]{:S(2)}, u32[]{:S(2)}) %collective-permute-start.3) | collective-permute-done | bytes 262176 | tf_op jit(solution)/shard_map/ppermute | solution.py:506
  29.8 2.3 %pick_x.1 = (bf16[32,128,256]{2,1,0:T(8,128)(2,1)}, f32[8,16,128]{2,1,0:T(8,128)S(1)}, f32[8,16,128]{2,1,0:T(8,128)S(1)}) custom-call(s32[1]{0:T(128)} %bitcast.1.at_ref.z_ref, bf16[8,144,256]{2,1,0:T(8,128)(2,1)S(1)} %all-to-all-done.x_ref), custom_call_target="tpu_custom_call" | custom-call | tf_op jit(solution)/shard_map/pick_x/pallas_call | solution.py:142
  32.1 7.9 %all-to-all-start.1 = ((bf16[32,128,256]{2,1,0:T(8,128)(2,1)}), bf16[32,128,256]{2,1,0:T(8,128)(2,1)S(1)}, u32[]{:S(2)}, u32[]{:S(2)}) async-start(bf16[32,128,256]{2,1,0:T(8,128)(2,1)} %get-tuple-element.83), calls=%async_computation.1 | async-start | bytes 4194304 | tf_op jit(solution)/shard_map/all_to_all | solution.py:486
  40.1 3.5 %turn_g.1 = (bf16[64,2048]{1,0:T(8,128)(2,1)}, bf16[64,2048]{1,0:T(8,128)(2,1)}, bf16[64,2048]{1,0:T(8,128)(2,1)}, bf16[64,2048]{1,0:T(8,128)(2,1)}, bf16[64,204...) custom-call(s32[3]{0:T(128)S(1)} %pad_add_fusion.at_ref, ...), custom_call_target="tpu_custom_call" | custom-call | tf_op jit(solution)/shard_map/turn_g/pallas_call | solution.py:210
  43.6 2.0 %collective-permute-start.5 = (bf16[64,2048]{1,0:T(8,128)(2,1)}, bf16[64,2048]{1,0:T(8,128)(2,1)S(1)}, u32[]{:S(2)}, u32[]{:S(2)}) collective-permute-start(bf16[64,2048]{1,0:T(8,128)(2,1)} %get-tuple-element.74), channel_id=1, source_target_pairs={{0,32},{32,64},{64,96},{96,128},{128,160},{160,192},{192,224},{224... | collective-permute-start | bytes 786440 | tf_op jit(solution)/shard_map/ppermute | solution.py:491
  45.6 2.4 %collective-permute-start.6 = (bf16[64,2048]{1,0:T(8,128)(2,1)}, bf16[64,2048]{1,0:T(8,128)(2,1)S(1)}, u32[]{:S(2)}, u32[]{:S(2)}) collective-permute-start(bf16[64,2048]{1,0:T(8,128)(2,1)} %get-tuple-element.75), channel_id=1, source_target_pairs={{0,64},{32,96},{64,128},{96,160},{128,192},{160,224},{192,0},{224,... | collective-permute-start | bytes 786440 | tf_op jit(solution)/shard_map/ppermute | solution.py:491
  48.0 2.7 %collective-permute-start.8 = (bf16[64,2048]{1,0:T(8,128)(2,1)}, bf16[64,2048]{1,0:T(8,128)(2,1)S(1)}, u32[]{:S(2)}, u32[]{:S(2)}) collective-permute-start(bf16[64,2048]{1,0:T(8,128)(2,1)} %get-tuple-element.77), channel_id=1, source_target_pairs={{0,128},{32,160},{64,192},{96,224},{128,0},{160,32},{192,64},{224,... | collective-permute-start | bytes 786440 | tf_op jit(solution)/shard_map/ppermute | solution.py:491
  50.7 3.6 %collective-permute-start.10 = (bf16[64,2048]{1,0:T(8,128)(2,1)}, bf16[64,2048]{1,0:T(8,128)(2,1)S(1)}, u32[]{:S(2)}, u32[]{:S(2)}) collective-permute-start(bf16[64,2048]{1,0:T(8,128)(2,1)} %get-tuple-element.79), channel_id=1, source_target_pairs={{0,192},{32,224},{64,0},{96,32},{128,64},{160,96},{192,128},{224,1... | collective-permute-start | bytes 786440 | tf_op jit(solution)/shard_map/ppermute | solution.py:491
  55.7 10.5 %all-to-all-done.1.x_ref = bf16[32,128,256]{2,1,0:T(8,128)(2,1)S(1)} async-done(((bf16[32,128,256]{2,1,0:T(8,128)(2,1)}), bf16[32,128,256]{2,1,0:T(8,128)(2,1)S(1)}, u32[]{:S(2)}, u32[]{:S(2)}) %all-to-all-start.1) | async-done | bytes 2097184 | tf_op jit(solution)/shard_map/all_to_all | solution.py:486
  66.2 7.9 %forward.1 = (bf16[32,128,256]{2,1,0:T(8,128)(2,1)}, f32[512,384]{1,0:T(8,128)}, f32[512,384]{1,0:T(8,128)}, bf16[512,384]{1,0:T(8,128)(2,1)}) custom-call(bf16[32,128,256]{2,1,0:T(8,128)(2,1)S(1)} %all-to-all-done.1.x_ref, bf16[1,2048,384]{2,1,0:T(8,128)(2,1)} %refs_10_.1, bf16[1,2048,384]{2,1,0:T(8,128)(2,1)} %refs_11_.1, bf16[1,384,2048]{2,1,0:T(8,128)(2,1)} %refs_12_.1), custom_call_target="tpu_custom_call" | custom-call | flops 2415919104 | bytes 11534336 | tf_op jit(solution)/shard_map/forward/pallas_call | solution.py:263
  74.1 1.9 %collective-permute-done.10.refs_6_ = bf16[64,2048]{1,0:T(8,128)(2,1)S(1)} collective-permute-done((bf16[64,2048]{1,0:T(8,128)(2,1)}, bf16[64,2048]{1,0:T(8,128)(2,1)S(1)}, u32[]{:S(2)}, u32[]{:S(2)}) %collective-permute-start.10) | collective-permute-done | bytes 262176 | tf_op jit(solution)/shard_map/ppermute | solution.py:491
  76.0 3.4 %collective-permute-done.11.refs_7_ = bf16[64,2048]{1,0:T(8,128)(2,1)S(1)} collective-permute-done((bf16[64,2048]{1,0:T(8,128)(2,1)}, bf16[64,2048]{1,0:T(8,128)(2,1)S(1)}, u32[]{:S(2)}, u32[]{:S(2)}) %collective-permute-start.11) | collective-permute-done | bytes 262176 | tf_op jit(solution)/shard_map/ppermute | solution.py:491
  80.2 7.6 %all-to-all-start.3 = ((bf16[32,128,256]{2,1,0:T(8,128)(2,1)}), bf16[32,128,256]{2,1,0:T(8,128)(2,1)}, u32[]{:S(2)}, u32[]{:S(2)}) async-start(bf16[32,128,256]{2,1,0:T(8,128)(2,1)} %get-tuple-element.91), calls=%async_computation.3 | async-start | bytes 4194304 | tf_op jit(solution)/shard_map/all_to_all | solution.py:486
  87.8 5.2 %collective-permute-start.7 = (bf16[64,2048]{1,0:T(8,128)(2,1)S(1)}, bf16[64,2048]{1,0:T(8,128)(2,1)S(1)}, u32[]{:S(2)}, u32[]{:S(2)}) collective-permute-start(bf16[64,2048]{1,0:T(8,128)(2,1)S(1)} %copy-done.19), channel_id=1, source_target_pairs={{0,96},{32,128},{64,160},{96,192},{128,224},{160,0},{192,32},{224,... | collective-permute-start | bytes 786440 | tf_op jit(solution)/shard_map/ppermute | solution.py:491
  93.1 17.2 %collective-permute-done.7.refs_3_ = bf16[64,2048]{1,0:T(8,128)(2,1)S(1)} collective-permute-done((bf16[64,2048]{1,0:T(8,128)(2,1)S(1)}, bf16[64,2048]{1,0:T(8,128)(2,1)S(1)}, u32[]{:S(2)}, u32[]{:S(2)}) %collective-permute-start.7) | collective-permute-done | bytes 262176 | tf_op jit(solution)/shard_map/ppermute | solution.py:491
  112.3 8.7 %backward.1 = (bf16[4,128,2048]{2,1,0:T(8,128)(2,1)}, bf16[32,128,256]{2,1,0:T(8,128)(2,1)}, bf16[512,384]{1,0:T(8,128)(2,1)}, bf16[512,384]{1,0:T(8,128)(2,1)}) custom-call(s32[3]{0:T(128)S(1)} %pad_add_fusion.at_ref, bf16[64,2048]{1,0:T(8,128)(2,1)} %get-tuple-element.73.refs_0_, bf16[64,2048]{1,0:T(8,128)(2,1)} %copy-done.18, ...), custom_call_target="tpu_custom_call" | custom-call | flops 2415919104 | bytes 13631488 | tf_op jit(solution)/shard_map/backward/pallas_call | solution.py:312
  121.0 7.5 %all-to-all-start.2 = ((bf16[32,128,256]{2,1,0:T(8,128)(2,1)}), bf16[32,128,256]{2,1,0:T(8,128)(2,1)S(1)}, u32[]{:S(2)}, u32[]{:S(2)}) async-start(bf16[32,128,256]{2,1,0:T(8,128)(2,1)} %get-tuple-element.87), calls=%async_computation.2 | async-start | bytes 4194304 | tf_op jit(solution)/shard_map/all_to_all | solution.py:486
  128.5 2.8 %join_out.1 = (f32[128,256]{1,0:T(8,128)S(1)}, bf16[128,256]{1,0:T(8,128)(2,1)S(1)}, bf16[128,256]{1,0:T(8,128)(2,1)S(1)}, bf16[128,256]{1,0:T(8,128)(2,1)S(1)},...) custom-call(s32[1]{0:T(128)} %bitcast.1.at_ref.z_ref, ...), custom_call_target="tpu_custom_call" | custom-call | tf_op jit(solution)/shard_map/join_out/pallas_call | solution.py:395
  131.3 5.0 %collective-permute-start.12 = (bf16[128,256]{1,0:T(8,128)(2,1)S(1)}, bf16[128,256]{1,0:T(8,128)(2,1)S(1)}, u32[]{:S(2)}, u32[]{:S(2)}) collective-permute-start(bf16[128,256]{1,0:T(8,128)(2,1)S(1)} %get-tuple-element.101), channel_id=1, source_target_pairs={{0,32},{32,64},{64,96},{96,128},{128,160},{160,192},{192,224},{224... | collective-permute-start | bytes 196616 | tf_op jit(solution)/shard_map/ppermute | solution.py:491
  136.3 3.1 %collective-permute-start.14 = (bf16[128,256]{1,0:T(8,128)(2,1)S(1)}, bf16[128,256]{1,0:T(8,128)(2,1)S(1)}, u32[]{:S(2)}, u32[]{:S(2)}) collective-permute-start(bf16[128,256]{1,0:T(8,128)(2,1)S(1)} %get-tuple-element.103), channel_id=1, source_target_pairs={{0,96},{32,128},{64,160},{96,192},{128,224},{160,0},{192,32},{224,... | collective-permute-start | bytes 196616 | tf_op jit(solution)/shard_map/ppermute | solution.py:491
  139.4 3.0 %collective-permute-start.15 = (bf16[128,256]{1,0:T(8,128)(2,1)S(1)}, bf16[128,256]{1,0:T(8,128)(2,1)S(1)}, u32[]{:S(2)}, u32[]{:S(2)}) collective-permute-start(bf16[128,256]{1,0:T(8,128)(2,1)S(1)} %get-tuple-element.104), channel_id=1, source_target_pairs={{0,128},{32,160},{64,192},{96,224},{128,0},{160,32},{192,64},{224,... | collective-permute-start | bytes 196616 | tf_op jit(solution)/shard_map/ppermute | solution.py:491
  148.6 5.2 %grads.1 = (bf16[1,2048,384]{2,1,0:T(8,128)(2,1)}, bf16[1,2048,384]{2,1,0:T(8,128)(2,1)}, bf16[1,384,2048]{2,1,0:T(8,128)(2,1)}) custom-call(bf16[32,128,256]{2,1,0:T(8,128)(2,1)S(1)} %copy-done.1, bf16[4,128,2048]{2,1,0:T(8,128)(2,1)S(1)} %copy-done.6, bf16[512,384]{1,0:T(8,128)(2,1)S(1)} %copy-done.11, bf16[512,384]{1,0:T(8,128)(2,1)S(1)} %copy-done.9, ...), custom_call_target="tpu_custom_call" | custom-call | flops 2415919104 | bytes 10485760 | tf_op jit(solution)/shard_map/grads/pallas_call | solution.py:357
  156.3 12.0 %all-to-all-start.4 = ((bf16[64,16,256]{2,1,0:T(8,128)(2,1)}), bf16[64,16,256]{2,1,0:T(8,128)(2,1)S(1)}, u32[]{:S(2)}, u32[]{:S(2)}) async-start(bf16[64,16,256]{2,1,0:T(8,128)(2,1)} %join_in.1), calls=%async_computation.4 | async-start | bytes 1048576 | tf_op jit(solution)/shard_map/all_to_all | solution.py:486
  168.8 2.5 %collective-permute-start.20 = (bf16[16,256]{1,0:T(8,128)(2,1)S(1)}, bf16[16,256]{1,0:T(8,128)(2,1)S(1)}, u32[]{:S(2)}, u32[]{:S(2)}) collective-permute-start(bf16[16,256]{1,0:T(8,128)(2,1)S(1)} %get-tuple-element.118), channel_id=1, source_target_pairs={{0,2},{1,3},{2,4},{3,5},{4,6},{5,7},{6,0},{7,1},{8,10},{9,11},{10,... | collective-permute-start | bytes 24584 | tf_op jit(solution)/shard_map/ppermute | solution.py:491
  171.3 2.4 %collective-permute-start.21 = (bf16[16,256]{1,0:T(8,128)(2,1)S(1)}, bf16[16,256]{1,0:T(8,128)(2,1)S(1)}, u32[]{:S(2)}, u32[]{:S(2)}) collective-permute-start(bf16[16,256]{1,0:T(8,128)(2,1)S(1)} %get-tuple-element.119), channel_id=1, source_target_pairs={{0,3},{1,4},{2,5},{3,6},{4,7},{5,0},{6,1},{7,2},{8,11},{9,12},{10,... | collective-permute-start | bytes 24584 | tf_op jit(solution)/shard_map/ppermute | solution.py:491
  174.2 3.2 %collective-permute-start.23 = (bf16[16,256]{1,0:T(8,128)(2,1)S(1)}, bf16[16,256]{1,0:T(8,128)(2,1)S(1)}, u32[]{:S(2)}, u32[]{:S(2)}) collective-permute-start(bf16[16,256]{1,0:T(8,128)(2,1)S(1)} %get-tuple-element.121), channel_id=1, source_target_pairs={{0,5},{1,6},{2,7},{3,0},{4,1},{5,2},{6,3},{7,4},{8,13},{9,14},{10,... | collective-permute-start | bytes 24584 | tf_op jit(solution)/shard_map/ppermute | solution.py:491
  177.5 2.4 %collective-permute-start.24 = (bf16[16,256]{1,0:T(8,128)(2,1)S(1)}, bf16[16,256]{1,0:T(8,128)(2,1)S(1)}, u32[]{:S(2)}, u32[]{:S(2)}) collective-permute-start(bf16[16,256]{1,0:T(8,128)(2,1)S(1)} %get-tuple-element.122), channel_id=1, source_target_pairs={{0,6},{1,7},{2,0},{3,1},{4,2},{5,3},{6,4},{7,5},{8,14},{9,15},{10,... | collective-permute-start | bytes 24584 | tf_op jit(solution)/shard_map/ppermute | solution.py:491
  180.4 4.7 %collective-permute-done.24.refs_6_ = bf16[16,256]{1,0:T(8,128)(2,1)S(1)} collective-permute-done((bf16[16,256]{1,0:T(8,128)(2,1)S(1)}, bf16[16,256]{1,0:T(8,128)(2,1)S(1)}, u32[]{:S(2)}, u32[]{:S(2)}) %collective-permute-start.24) | collective-permute-done | bytes 8224 | tf_op jit(solution)/shard_map/ppermute | solution.py:491
  185.0 2.1 %collective-permute-done.25.refs_7_ = bf16[16,256]{1,0:T(8,128)(2,1)S(1)} collective-permute-done((bf16[16,256]{1,0:T(8,128)(2,1)S(1)}, bf16[16,256]{1,0:T(8,128)(2,1)S(1)}, u32[]{:S(2)}, u32[]{:S(2)}) %collective-permute-start.25) | collective-permute-done | bytes 8224 | tf_op jit(solution)/shard_map/ppermute | solution.py:491
  (94 shorter events, 25.5 us)
Async XLA Ops:
  2.5 27.4 %all-to-all-start = ((bf16[8,144,256]{2,1,0:T(8,128)(2,1)}), bf16[8,144,256]{2,1,0:T(8,128)(2,1)S(1)}, u32[]{:S(2)}, u32[]{:S(2)}) async-start(bf16[8,144,256]{2,1,0:T(8,128)(2,1)} %get-tuple-element.81), calls=%async_computation | async-start | bytes 1179648 | tf_op jit(solution)/shard_map/all_to_all | solution.py:486
  15.2 14.6 %collective-permute-start = (bf16[128,2048]{1,0:T(8,128)(2,1)S(1)}, bf16[128,2048]{1,0:T(8,128)(2,1)S(1)}, u32[]{:S(2)}, u32[]{:S(2)}) collective-permute-start(bf16[128,2048]{1,0:T(8,128)(2,1)S(1)} %get-tuple-element.68), channel_id=1, source_target_pairs={{0,8},{4,12},{8,0},{12,4},{16,24},{20,28},{24,16},{28,20},{1,9},{5... | collective-permute-start | bytes 1572872 | tf_op jit(solution)/shard_map/ppermute | solution.py:506
  15.2 9.1 %collective-permute-start.1 = (bf16[128,1024]{1,0:T(8,128)(2,1)S(1)}, bf16[128,1024]{1,0:T(8,128)(2,1)S(1)}, u32[]{:S(2)}, u32[]{:S(2)}) collective-permute-start(bf16[128,1024]{1,0:T(8,128)(2,1)S(1)} %get-tuple-element.69), channel_id=1, source_target_pairs={{0,16},{4,20},{8,24},{12,28},{16,0},{20,4},{24,8},{28,12},{1,17},{... | collective-permute-start | bytes 786440 | tf_op jit(solution)/shard_map/ppermute | solution.py:506
  16.4 9.1 %collective-permute-start.2 = (bf16[128,1024]{1,0:T(8,128)(2,1)S(1)}, bf16[128,1024]{1,0:T(8,128)(2,1)S(1)}, u32[]{:S(2)}, u32[]{:S(2)}) collective-permute-start(bf16[128,1024]{1,0:T(8,128)(2,1)S(1)} %get-tuple-element.70), channel_id=1, source_target_pairs={{0,20},{4,16},{8,28},{12,24},{16,4},{20,0},{24,12},{28,8},{1,21},{... | collective-permute-start | bytes 786440 | tf_op jit(solution)/shard_map/ppermute | solution.py:506
  16.4 12.7 %collective-permute-start.3 = (bf16[128,1024]{1,0:T(8,128)(2,1)S(1)}, bf16[128,1024]{1,0:T(8,128)(2,1)S(1)}, u32[]{:S(2)}, u32[]{:S(2)}) collective-permute-start(bf16[128,1024]{1,0:T(8,128)(2,1)S(1)} %get-tuple-element.71), channel_id=1, source_target_pairs={{0,24},{4,28},{8,16},{12,20},{16,8},{20,12},{24,0},{28,4},{1,25},{... | collective-permute-start | bytes 786440 | tf_op jit(solution)/shard_map/ppermute | solution.py:506
  17.9 11.8 %collective-permute-start.4 = (bf16[128,1024]{1,0:T(8,128)(2,1)S(1)}, bf16[128,1024]{1,0:T(8,128)(2,1)S(1)}, u32[]{:S(2)}, u32[]{:S(2)}) collective-permute-start(bf16[128,1024]{1,0:T(8,128)(2,1)S(1)} %get-tuple-element.72), channel_id=1, source_target_pairs={{0,28},{4,24},{8,20},{12,16},{16,12},{20,8},{24,4},{28,0},{1,29},{... | collective-permute-start | bytes 786440 | tf_op jit(solution)/shard_map/ppermute | solution.py:506
  32.1 34.0 %all-to-all-start.1 = ((bf16[32,128,256]{2,1,0:T(8,128)(2,1)}), bf16[32,128,256]{2,1,0:T(8,128)(2,1)S(1)}, u32[]{:S(2)}, u32[]{:S(2)}) async-start(bf16[32,128,256]{2,1,0:T(8,128)(2,1)} %get-tuple-element.83), calls=%async_computation.1 | async-start | bytes 4194304 | tf_op jit(solution)/shard_map/all_to_all | solution.py:486
  43.6 30.4 %collective-permute-start.5 = (bf16[64,2048]{1,0:T(8,128)(2,1)}, bf16[64,2048]{1,0:T(8,128)(2,1)S(1)}, u32[]{:S(2)}, u32[]{:S(2)}) collective-permute-start(bf16[64,2048]{1,0:T(8,128)(2,1)} %get-tuple-element.74), channel_id=1, source_target_pairs={{0,32},{32,64},{64,96},{96,128},{128,160},{160,192},{192,224},{224... | collective-permute-start | bytes 786440 | tf_op jit(solution)/shard_map/ppermute | solution.py:491
  45.6 28.4 %collective-permute-start.6 = (bf16[64,2048]{1,0:T(8,128)(2,1)}, bf16[64,2048]{1,0:T(8,128)(2,1)S(1)}, u32[]{:S(2)}, u32[]{:S(2)}) collective-permute-start(bf16[64,2048]{1,0:T(8,128)(2,1)} %get-tuple-element.75), channel_id=1, source_target_pairs={{0,64},{32,96},{64,128},{96,160},{128,192},{160,224},{192,0},{224,... | collective-permute-start | bytes 786440 | tf_op jit(solution)/shard_map/ppermute | solution.py:491
  48.0 26.1 %collective-permute-start.8 = (bf16[64,2048]{1,0:T(8,128)(2,1)}, bf16[64,2048]{1,0:T(8,128)(2,1)S(1)}, u32[]{:S(2)}, u32[]{:S(2)}) collective-permute-start(bf16[64,2048]{1,0:T(8,128)(2,1)} %get-tuple-element.77), channel_id=1, source_target_pairs={{0,128},{32,160},{64,192},{96,224},{128,0},{160,32},{192,64},{224,... | collective-permute-start | bytes 786440 | tf_op jit(solution)/shard_map/ppermute | solution.py:491
  50.7 25.3 %collective-permute-start.10 = (bf16[64,2048]{1,0:T(8,128)(2,1)}, bf16[64,2048]{1,0:T(8,128)(2,1)S(1)}, u32[]{:S(2)}, u32[]{:S(2)}) collective-permute-start(bf16[64,2048]{1,0:T(8,128)(2,1)} %get-tuple-element.79), channel_id=1, source_target_pairs={{0,192},{32,224},{64,0},{96,32},{128,64},{160,96},{192,128},{224,1... | collective-permute-start | bytes 786440 | tf_op jit(solution)/shard_map/ppermute | solution.py:491
  54.3 25.2 %collective-permute-start.11 = (bf16[64,2048]{1,0:T(8,128)(2,1)}, bf16[64,2048]{1,0:T(8,128)(2,1)S(1)}, u32[]{:S(2)}, u32[]{:S(2)}) collective-permute-start(bf16[64,2048]{1,0:T(8,128)(2,1)} %get-tuple-element.80), channel_id=1, source_target_pairs={{0,224},{32,0},{64,32},{96,64},{128,96},{160,128},{192,160},{224,1... | collective-permute-start | bytes 786440 | tf_op jit(solution)/shard_map/ppermute | solution.py:491
  79.5 32.8 %copy-start.7 = (f32[512,384]{1,0:T(8,128)S(1)}, f32[512,384]{1,0:T(8,128)}, u32[]{:S(2)}) copy-start(f32[512,384]{1,0:T(8,128)} %get-tuple-element.85.refs_8_) | copy-start | bytes 2359300
  80.2 40.8 %all-to-all-start.3 = ((bf16[32,128,256]{2,1,0:T(8,128)(2,1)}), bf16[32,128,256]{2,1,0:T(8,128)(2,1)}, u32[]{:S(2)}, u32[]{:S(2)}) async-start(bf16[32,128,256]{2,1,0:T(8,128)(2,1)} %get-tuple-element.91), calls=%async_computation.3 | async-start | bytes 4194304 | tf_op jit(solution)/shard_map/all_to_all | solution.py:486
  87.8 22.5 %collective-permute-start.7 = (bf16[64,2048]{1,0:T(8,128)(2,1)S(1)}, bf16[64,2048]{1,0:T(8,128)(2,1)S(1)}, u32[]{:S(2)}, u32[]{:S(2)}) collective-permute-start(bf16[64,2048]{1,0:T(8,128)(2,1)S(1)} %copy-done.19), channel_id=1, source_target_pairs={{0,96},{32,128},{64,160},{96,192},{128,224},{160,0},{192,32},{224,... | collective-permute-start | bytes 786440 | tf_op jit(solution)/shard_map/ppermute | solution.py:491
  93.0 18.6 %collective-permute-start.9 = (bf16[64,2048]{1,0:T(8,128)(2,1)S(1)}, bf16[64,2048]{1,0:T(8,128)(2,1)S(1)}, u32[]{:S(2)}, u32[]{:S(2)}) collective-permute-start(bf16[64,2048]{1,0:T(8,128)(2,1)S(1)} %copy-done.17), channel_id=1, source_target_pairs={{0,160},{32,192},{64,224},{96,0},{128,32},{160,64},{192,96},{224,1... | collective-permute-start | bytes 786440 | tf_op jit(solution)/shard_map/ppermute | solution.py:491
  121.0 33.6 %all-to-all-start.2 = ((bf16[32,128,256]{2,1,0:T(8,128)(2,1)}), bf16[32,128,256]{2,1,0:T(8,128)(2,1)S(1)}, u32[]{:S(2)}, u32[]{:S(2)}) async-start(bf16[32,128,256]{2,1,0:T(8,128)(2,1)} %get-tuple-element.87), calls=%async_computation.2 | async-start | bytes 4194304 | tf_op jit(solution)/shard_map/all_to_all | solution.py:486
  131.3 12.7 %collective-permute-start.12 = (bf16[128,256]{1,0:T(8,128)(2,1)S(1)}, bf16[128,256]{1,0:T(8,128)(2,1)S(1)}, u32[]{:S(2)}, u32[]{:S(2)}) collective-permute-start(bf16[128,256]{1,0:T(8,128)(2,1)S(1)} %get-tuple-element.101), channel_id=1, source_target_pairs={{0,32},{32,64},{64,96},{96,128},{128,160},{160,192},{192,224},{224... | collective-permute-start | bytes 196616 | tf_op jit(solution)/shard_map/ppermute | solution.py:491
  136.3 10.0 %collective-permute-start.13 = (bf16[128,256]{1,0:T(8,128)(2,1)S(1)}, bf16[128,256]{1,0:T(8,128)(2,1)S(1)}, u32[]{:S(2)}, u32[]{:S(2)}) collective-permute-start(bf16[128,256]{1,0:T(8,128)(2,1)S(1)} %get-tuple-element.102), channel_id=1, source_target_pairs={{0,64},{32,96},{64,128},{96,160},{128,192},{160,224},{192,0},{224,... | collective-permute-start | bytes 196616 | tf_op jit(solution)/shard_map/ppermute | solution.py:491
  136.3 17.5 %collective-permute-start.14 = (bf16[128,256]{1,0:T(8,128)(2,1)S(1)}, bf16[128,256]{1,0:T(8,128)(2,1)S(1)}, u32[]{:S(2)}, u32[]{:S(2)}) collective-permute-start(bf16[128,256]{1,0:T(8,128)(2,1)S(1)} %get-tuple-element.103), channel_id=1, source_target_pairs={{0,96},{32,128},{64,160},{96,192},{128,224},{160,0},{192,32},{224,... | collective-permute-start | bytes 196616 | tf_op jit(solution)/shard_map/ppermute | solution.py:491
  139.4 14.4 %collective-permute-start.15 = (bf16[128,256]{1,0:T(8,128)(2,1)S(1)}, bf16[128,256]{1,0:T(8,128)(2,1)S(1)}, u32[]{:S(2)}, u32[]{:S(2)}) collective-permute-start(bf16[128,256]{1,0:T(8,128)(2,1)S(1)} %get-tuple-element.104), channel_id=1, source_target_pairs={{0,128},{32,160},{64,192},{96,224},{128,0},{160,32},{192,64},{224,... | collective-permute-start | bytes 196616 | tf_op jit(solution)/shard_map/ppermute | solution.py:491
  142.4 11.5 %collective-permute-start.16 = (bf16[128,256]{1,0:T(8,128)(2,1)S(1)}, bf16[128,256]{1,0:T(8,128)(2,1)S(1)}, u32[]{:S(2)}, u32[]{:S(2)}) collective-permute-start(bf16[128,256]{1,0:T(8,128)(2,1)S(1)} %get-tuple-element.105), channel_id=1, source_target_pairs={{0,160},{32,192},{64,224},{96,0},{128,32},{160,64},{192,96},{224,1... | collective-permute-start | bytes 196616 | tf_op jit(solution)/shard_map/ppermute | solution.py:491
  144.0 10.5 %collective-permute-start.17 = (bf16[128,256]{1,0:T(8,128)(2,1)S(1)}, bf16[128,256]{1,0:T(8,128)(2,1)S(1)}, u32[]{:S(2)}, u32[]{:S(2)}) collective-permute-start(bf16[128,256]{1,0:T(8,128)(2,1)S(1)} %get-tuple-element.106), channel_id=1, source_target_pairs={{0,192},{32,224},{64,0},{96,32},{128,64},{160,96},{192,128},{224,1... | collective-permute-start | bytes 196616 | tf_op jit(solution)/shard_map/ppermute | solution.py:491
  146.3 8.2 %collective-permute-start.18 = (bf16[128,256]{1,0:T(8,128)(2,1)S(1)}, bf16[128,256]{1,0:T(8,128)(2,1)S(1)}, u32[]{:S(2)}, u32[]{:S(2)}) collective-permute-start(bf16[128,256]{1,0:T(8,128)(2,1)S(1)} %get-tuple-element.107), channel_id=1, source_target_pairs={{0,224},{32,0},{64,32},{96,64},{128,96},{160,128},{192,160},{224,1... | collective-permute-start | bytes 196616 | tf_op jit(solution)/shard_map/ppermute | solution.py:491
  156.3 30.8 %all-to-all-start.4 = ((bf16[64,16,256]{2,1,0:T(8,128)(2,1)}), bf16[64,16,256]{2,1,0:T(8,128)(2,1)S(1)}, u32[]{:S(2)}, u32[]{:S(2)}) async-start(bf16[64,16,256]{2,1,0:T(8,128)(2,1)} %join_in.1), calls=%async_computation.4 | async-start | bytes 1048576 | tf_op jit(solution)/shard_map/all_to_all | solution.py:486
  168.3 9.2 %collective-permute-start.19 = (bf16[16,256]{1,0:T(8,128)(2,1)S(1)}, bf16[16,256]{1,0:T(8,128)(2,1)S(1)}, u32[]{:S(2)}, u32[]{:S(2)}) collective-permute-start(bf16[16,256]{1,0:T(8,128)(2,1)S(1)} %get-tuple-element.117), channel_id=1, source_target_pairs={{0,1},{1,2},{2,3},{3,4},{4,5},{5,6},{6,7},{7,0},{8,9},{9,10},{10,1... | collective-permute-start | bytes 24584 | tf_op jit(solution)/shard_map/ppermute | solution.py:491
  168.8 11.0 %collective-permute-start.20 = (bf16[16,256]{1,0:T(8,128)(2,1)S(1)}, bf16[16,256]{1,0:T(8,128)(2,1)S(1)}, u32[]{:S(2)}, u32[]{:S(2)}) collective-permute-start(bf16[16,256]{1,0:T(8,128)(2,1)S(1)} %get-tuple-element.118), channel_id=1, source_target_pairs={{0,2},{1,3},{2,4},{3,5},{4,6},{5,7},{6,0},{7,1},{8,10},{9,11},{10,... | collective-permute-start | bytes 24584 | tf_op jit(solution)/shard_map/ppermute | solution.py:491
  171.3 8.6 %collective-permute-start.21 = (bf16[16,256]{1,0:T(8,128)(2,1)S(1)}, bf16[16,256]{1,0:T(8,128)(2,1)S(1)}, u32[]{:S(2)}, u32[]{:S(2)}) collective-permute-start(bf16[16,256]{1,0:T(8,128)(2,1)S(1)} %get-tuple-element.119), channel_id=1, source_target_pairs={{0,3},{1,4},{2,5},{3,6},{4,7},{5,0},{6,1},{7,2},{8,11},{9,12},{10,... | collective-permute-start | bytes 24584 | tf_op jit(solution)/shard_map/ppermute | solution.py:491
  173.6 6.2 %collective-permute-start.22 = (bf16[16,256]{1,0:T(8,128)(2,1)S(1)}, bf16[16,256]{1,0:T(8,128)(2,1)S(1)}, u32[]{:S(2)}, u32[]{:S(2)}) collective-permute-start(bf16[16,256]{1,0:T(8,128)(2,1)S(1)} %get-tuple-element.120), channel_id=1, source_target_pairs={{0,4},{1,5},{2,6},{3,7},{4,0},{5,1},{6,2},{7,3},{8,12},{9,13},{10,... | collective-permute-start | bytes 24584 | tf_op jit(solution)/shard_map/ppermute | solution.py:491
  174.2 6.1 %collective-permute-start.23 = (bf16[16,256]{1,0:T(8,128)(2,1)S(1)}, bf16[16,256]{1,0:T(8,128)(2,1)S(1)}, u32[]{:S(2)}, u32[]{:S(2)}) collective-permute-start(bf16[16,256]{1,0:T(8,128)(2,1)S(1)} %get-tuple-element.121), channel_id=1, source_target_pairs={{0,5},{1,6},{2,7},{3,0},{4,1},{5,2},{6,3},{7,4},{8,13},{9,14},{10,... | collective-permute-start | bytes 24584 | tf_op jit(solution)/shard_map/ppermute | solution.py:491
  177.5 7.6 %collective-permute-start.24 = (bf16[16,256]{1,0:T(8,128)(2,1)S(1)}, bf16[16,256]{1,0:T(8,128)(2,1)S(1)}, u32[]{:S(2)}, u32[]{:S(2)}) collective-permute-start(bf16[16,256]{1,0:T(8,128)(2,1)S(1)} %get-tuple-element.122), channel_id=1, source_target_pairs={{0,6},{1,7},{2,0},{3,1},{4,2},{5,3},{6,4},{7,5},{8,14},{9,15},{10,... | collective-permute-start | bytes 24584 | tf_op jit(solution)/shard_map/ppermute | solution.py:491
  179.8 7.3 %collective-permute-start.25 = (bf16[16,256]{1,0:T(8,128)(2,1)S(1)}, bf16[16,256]{1,0:T(8,128)(2,1)S(1)}, u32[]{:S(2)}, u32[]{:S(2)}) collective-permute-start(bf16[16,256]{1,0:T(8,128)(2,1)S(1)} %get-tuple-element.123), channel_id=1, source_target_pairs={{0,7},{1,0},{2,1},{3,2},{4,3},{5,4},{6,5},{7,6},{8,15},{9,8},{10,9... | collective-permute-start | bytes 24584 | tf_op jit(solution)/shard_map/ppermute | solution.py:491
  (25 other events, 217.6 us)
